TPU v7x, 32 devices: a whole 2x2x4 slice. The times are simulated.
32 devices in a mesh: rows: 8 (over y, x, core), probe: 4 (over z).
Axes of the slice: x: 2, y: 2, z: 4, core: 2. Of those that a mesh axis runs over, the one named last changes fastest.
Arguments:
- responses: bfloat16 [256, 65536], P('probe', 'rows'), may hold values from -6 to 6
- probes: bfloat16 [256, 65536], P('probe', 'rows'), may hold values from -6 to 6
- left_factors: bfloat16 [5, 128, 65536], P(None, None, 'rows'), may hold values from -0.5 to 0.5
- right_factors: bfloat16 [5, 128, 65536], P(None, None, 'rows'), may hold values from -0.13258252 to 0.13258252
- level_ranks: int32 [5], replicated, may hold values from 32 to 128, as said below
Outputs:
- basis: float32 [256, 65536], P(None, ('rows', 'probe'))
Inputs may be any that keep to these rules, and one draw needn't show every extreme that they name: `level_ranks`: some level has rank 128 and some level rank 128 // 4.
All inputs are finite; a program needn't handle non-finite values.
Results may differ from a plain program's by a relative error of at most 0.0047.
Values may be sent and summed in bfloat16 or wider, within the bound.
No kernel may reach another device: no remote copies, remote signals or barrier semaphores. Data moves between devices by JAX's collectives and lax.ppermute only.
A program may use at most 128 MiB of HBM per device.

v0:
```python
import jax
import jax.numpy as jnp
from jax import lax
from jax.sharding import PartitionSpec as P

BLOCKS = 64


ridge_share = 0.05


def from_partner(value, axis, apart):
    mask = 2**apart
    pairs = [(source, source ^ mask) for source in range(lax.axis_size(axis))]
    return lax.ppermute(value, axis, pairs)


def shards(responses, probes, left_factors, right_factors, level_ranks):
    rows_count = lax.axis_size("rows")
    local_probes, rows_dev = responses.shape
    levels_count, rank_width, _ = left_factors.shape
    rank_iota = jnp.arange(rank_width)
    partials = []
    layouts = []
    for level_index in range(levels_count):
        clusters = 2 ** (level_index + 1)
        per_device = max(1, clusters // rows_count)
        cluster_span = max(1, rows_count // clusters)
        layouts.append((clusters, per_device, cluster_span))
        right_part = right_factors[level_index].reshape(
            rank_width, per_device, rows_dev // per_device
        )
        probe_part = probes.reshape(local_probes, per_device, rows_dev // per_device)
        partials.append(
            jnp.einsum("kcn,rcn->ckr", right_part, probe_part, preferred_element_type=jnp.float32)
        )
    siblings = []
    running = list(partials)
    finished = [None] * levels_count
    span_list = []
    for level_index in range(levels_count):
        clusters, per_device, cluster_span = layouts[level_index]
        span_list.append(cluster_span.bit_length() - 1)
        if clusters > rows_count:
            swapped = partials[level_index].reshape(per_device // 2, 2, rank_width, local_probes)[
                :, ::-1
            ]
            finished[level_index] = swapped.reshape(per_device, rank_width, local_probes)
    for bit_number in range(rows_count.bit_length() - 1):
        crossing = [
            level_index
            for level_index in range(levels_count)
            if finished[level_index] is None and span_list[level_index] >= bit_number
        ]
        payload = jnp.concatenate([running[level_index] for level_index in crossing], 0)
        received = from_partner(payload, "rows", bit_number)
        for slot_number, level_index in enumerate(crossing):
            incoming = received[slot_number : slot_number + 1]
            if span_list[level_index] > bit_number:
                running[level_index] = running[level_index] + incoming
            else:
                finished[level_index] = incoming
    siblings = finished
    residual = responses.astype(jnp.float32)
    for level_index in range(levels_count):
        clusters, per_device, cluster_span = layouts[level_index]
        keep_rows = rank_iota[None, :, None] < level_ranks[level_index]
        sibling = jnp.where(keep_rows, siblings[level_index], 0.0).astype(jnp.bfloat16)
        left_part = left_factors[level_index].reshape(
            rank_width, per_device, rows_dev // per_device
        )
        update = jnp.einsum("ckr,kcn->rcn", sibling, left_part, preferred_element_type=jnp.float32)
        residual = residual - update.reshape(local_probes, rows_dev)
    sample = residual.astype(jnp.bfloat16)
    slab = lax.all_to_all(sample, "probe", split_axis=1, concat_axis=0, tiled=True)
    all_probes, slab_rows = slab.shape
    block_rows = rows_dev * rows_count // BLOCKS
    piece_rows = min(block_rows, slab_rows)
    piece_count = slab_rows // piece_rows
    piece_view = slab.reshape(all_probes, piece_count, piece_rows)
    piece_gram = jnp.einsum(
        "rpg,spg->prs", piece_view, piece_view, preferred_element_type=jnp.float32
    )
    group_size = max(1, block_rows // slab_rows)
    full_gram = piece_gram
    for bit_number in range(group_size.bit_length() - 1):
        full_gram = full_gram + from_partner(full_gram, "probe", bit_number)
    shifted = full_gram + ridge_share * block_rows * jnp.eye(all_probes, dtype=jnp.float32)
    lower_factor = jnp.linalg.cholesky(shifted)
    right_sides = jnp.transpose(piece_view, (1, 0, 2)).astype(jnp.float32)
    solved = lax.linalg.triangular_solve(lower_factor, right_sides, left_side=True, lower=True)
    return jnp.transpose(solved, (1, 0, 2)).reshape(all_probes, slab_rows)


def solution(mesh):
    return jax.shard_map(
        shards,
        mesh=mesh,
        in_specs=(
            P("probe", "rows"),
            P("probe", "rows"),
            P(None, None, "rows"),
            P(None, None, "rows"),
            P(),
        ),
        out_specs=P(None, ("rows", "probe")),
        check_vma=False,
    )
```

profile of v0, /device:TPU:0, one launch (start us, length us, event | category | flops | bytes accessed | tf_op | source)
XLA Modules:
  0.0 209.1 jit_solution(5203763401729224298)
XLA Ops:
  0.0 2.8 %fusion.20 = f32[1,128,64]{1,2,0:T(8,128)S(1)} fusion(bf16[64,8192]{1,0:T(8,128)(2,1)} %param.6, bf16[5,128,8192]{2,1,0:T(8,128)(2,1)} %param.8), kind=kOutput, calls=%fused_computation.29 | convolution fusion | flops 134217728 | bytes 3178496 | tf_op jit(solution)/shard_map/kcn,rcn->ckr/dot_general | solution.py:35
  2.8 2.4 %fusion.26 = f32[1,128,64]{1,2,0:T(8,128)S(1)} fusion(bf16[64,8192]{1,0:T(8,128)(2,1)S(1)} %copy-done.1, bf16[5,128,8192]{2,1,0:T(8,128)(2,1)} %param.8), kind=kOutput, calls=%fused_computation.31 | convolution fusion | flops 134217728 | bytes 3178496 | tf_op jit(solution)/shard_map/kcn,rcn->ckr/dot_general | solution.py:35
  5.2 2.4 %fusion.23 = f32[1,128,64]{1,2,0:T(8,128)S(1)} fusion(bf16[64,8192]{1,0:T(8,128)(2,1)S(1)} %copy-done.1, bf16[5,128,8192]{2,1,0:T(8,128)(2,1)} %param.8), kind=kOutput, calls=%fused_computation.30 | convolution fusion | flops 134217728 | bytes 3178496 | tf_op jit(solution)/shard_map/kcn,rcn->ckr/dot_general | solution.py:35
  8.2 4.7 %fusion.68 = (bf16[1,128,8192]{2,1,0:T(8,128)(2,1)}, bf16[1,128,8192]{2,1,0:T(8,128)(2,1)}) fusion(bf16[5,128,8192]{2,1,0:T(8,128)(2,1)} %param.8), kind=kLoop, calls=%fused_computation.102 | loop fusion | bytes 8388608 | tf_op jit(solution)/shard_map/slice | solution.py:30
  12.9 3.2 %copy.93 = bf16[1,128,8192]{1,2,0:T(8,128)(2,1)S(1)} copy(bf16[1,128,8192]{2,1,0:T(8,128)(2,1)} %get-tuple-element.28) | data formatting | bytes 4194304
  18.2 4.6 %fusion.67 = (bf16[1,128,8192]{2,1,0:T(8,128)(2,1)}, bf16[1,128,8192]{2,1,0:T(8,128)(2,1)}) fusion(bf16[5,128,8192]{2,1,0:T(8,128)(2,1)} %param.7), kind=kLoop, calls=%fused_computation.101 | loop fusion | bytes 8388608 | tf_op jit(solution)/shard_map/slice | solution.py:69
  22.8 3.2 %copy.94 = bf16[1,128,8192]{1,2,0:T(8,128)(2,1)S(1)} copy(bf16[1,128,8192]{2,1,0:T(8,128)(2,1)} %get-tuple-element.26) | data formatting | bytes 4194304
  27.1 4.1 %copy.91 = bf16[1,128,8192]{1,2,0:T(8,128)(2,1)} copy(bf16[1,128,8192]{2,1,0:T(8,128)(2,1)} %get-tuple-element.27) | data formatting | bytes 4194304
  31.8 4.1 %copy.92 = bf16[1,128,8192]{1,2,0:T(8,128)(2,1)} copy(bf16[1,128,8192]{2,1,0:T(8,128)(2,1)} %get-tuple-element.25) | data formatting | bytes 4194304
  35.8 2.2 %fusion.32 = bf16[2,128,64]{1,2,0:T(8,128)(2,1)S(1)} fusion(bf16[128,2,4096]{0,2,1:T(8,128)(2,1)} %bitcast.129, bf16[8,2,8,4096]{3,2,1,0:T(8,128)(2,1)S(1)} %bitcast.135), kind=kOutput, calls=%fused_computation.36 | convolution fusion | flops 134217728 | bytes 3178496 | tf_op jit(solution)/shard_map/kcn,rcn->ckr/dot_general | solution.py:35
  40.4 2.6 %collective-permute-start.1 = (f32[2,128,64]{1,2,0:T(8,128)S(1)}, f32[2,128,64]{1,2,0:T(8,128)S(1)}, u32[]{:S(2)}, u32[]{:S(2)}) collective-permute-start(f32[2,128,64]{1,2,0:T(8,128)S(1)} %pad_maximum_fusion.1), channel_id=1, source_target_pairs={{0,8},{4,12},{8,0},{12,4},{16,24},{20,28},{24,16},{28,20},{1,9},{5... | collective-permute-start | bytes 196616 | tf_op jit(solution)/shard_map/ppermute | solution.py:15
  43.6 2.1 %collective-permute-done.1 = f32[2,128,64]{1,2,0:T(8,128)S(1)} collective-permute-done((f32[2,128,64]{1,2,0:T(8,128)S(1)}, f32[2,128,64]{1,2,0:T(8,128)S(1)}, u32[]{:S(2)}, u32[]{:S(2)}) %collective-permute-start.1) | collective-permute-done | bytes 65568 | tf_op jit(solution)/shard_map/ppermute | solution.py:15
  49.6 2.1 %fusion.2 = f32[64,8192]{1,0:T(8,128)S(1)} fusion(f32[64,8192]{1,0:T(8,128)S(1)} %fusion.5, bf16[5,128,8192]{2,1,0:T(8,128)(2,1)} %param.7, bf16[64,8192]{1,0:T(8,128)(2,1)S(1)} %copy-done.2, bf16[1,128,64]{1,2,0:T(8,128)(2,1)S(1)} %collective-permute-done.2, pred[128]{0:T(512)(128)(4,1)S(1)} %iota_compare_fusion.9), kind=kOutput, calls=%fused_computation.6 | convolution fusion | flops 135798784 | bytes 7356544 | tf_op jit(solution)/shard_map/ckr,kcn->rcn/dot_general | solution.py:72
  51.7 2.4 %fusion.3 = bf16[64,8192]{1,0:T(8,128)(2,1)S(1)} fusion(f32[64,8192]{1,0:T(8,128)S(1)} %bitcast.127, f32[64,8192]{1,0:T(8,128)S(1)} %bitcast.128, f32[64,8192]{1,0:T(8,128)S(1)} %fusion.2, bf16[5,128,8192]{2,1,0:T(8,128)(2,1)} %param.7, f32[3,128,64]{1,2,0:T(8,128)S(1)} %collective-permute-done, pred[128]{0:T(512)(128)(4,1)S(1)} %iota_compare_fusion.7), kind=kOutput, calls=%fused_computation.7 | convolution fusion | flops 136323072 | bytes 9454080 | tf_op jit(solution)/shard_map/ckr,kcn->rcn/dot_general | solution.py:72
  55.2 5.0 %all-to-all-start = ((bf16[64,4,2048]{2,0,1:T(8,128)(2,1)}), bf16[64,4,2048]{2,0,1:T(8,128)(2,1)S(1)}, u32[]{:S(2)}, u32[]{:S(2)}) async-start(bf16[64,4,2048]{2,0,1:T(8,128)(2,1)} %bitcast.119), calls=%async_computation | async-start | bytes 2097152 | tf_op jit(solution)/shard_map/all_to_all | solution.py:75
  61.0 24.3 %all-to-all-done = bf16[64,4,2048]{2,0,1:T(8,128)(2,1)S(1)} async-done(((bf16[64,4,2048]{2,0,1:T(8,128)(2,1)}), bf16[64,4,2048]{2,0,1:T(8,128)(2,1)S(1)}, u32[]{:S(2)}, u32[]{:S(2)}) %all-to-all-start) | async-done | bytes 1048608 | tf_op jit(solution)/shard_map/all_to_all | solution.py:75
  88.2 23.5 %custom-call.16 = f32[2,128,128]{2,1,0:T(8,128)S(1)} custom-call(f32[2,128,128]{2,1,0:T(8,128)S(1)} %cholesky.122), custom_call_target="Cholesky" | custom-call | tf_op jit(solution)/shard_map/jit(cholesky)/cholesky | solution.py:89
  111.7 19.7 %custom-call.17 = f32[2,1,128,128]{2,3,1,0:T(8,128)S(1)} custom-call(f32[2,1,128,128]{3,2,1,0:T(8,128)S(1)} %select_bitcast_fusion), custom_call_target="InvertDiagBlocksLowerTriangular" | custom-call | tf_op jit(solution)/shard_map/jit(cholesky)/cholesky | solution.py:89
  132.1 23.5 %custom-call.18 = f32[2,128,128]{2,1,0:T(8,128)S(1)} custom-call(f32[2,128,128]{2,1,0:T(8,128)S(1)} %convolution_subtract_fusion.3), custom_call_target="Cholesky" | custom-call | tf_op jit(solution)/shard_map/jit(cholesky)/cholesky | solution.py:89
  156.0 5.3 %while.1 = (s32[]{:T(128)}, f32[2,256,256]{2,1,0:T(8,128)S(1)}, s32[2,2]{1,0:T(2,128)S(1)}, f32[2,2,128,128]{3,2,0,1:T(8,128)}, s32[]{:T(128)}) while((s32[]{:T(128)}, f32[2,256,256]{2,1,0:T(8,128)S(1)}, s32[2,2]{1,0:T(2,128)S(1)}, f32[2,2,128,128]{3,2,0,1:T(8,128)}, s32[]{:T(128)}) %tuple.30), condition=%wide.while_cond, body=%wide.while_body.sunk | while | flops 2 | bytes 263277 | solution.py:91
  156.6 2.0 bitcast_dynamic-update-slice_fusion.2
  159.3 2.1 bitcast_dynamic-update-slice_fusion.2
  161.3 40.1 %custom-call.19 = f32[2,2,128,128]{2,3,1,0:T(8,128)S(1)} custom-call(f32[2,2,128,128]{3,2,1,0:T(8,128)} %bitcast.141), custom_call_target="InvertDiagBlocksLowerTriangular" | custom-call | tf_op jit(solution)/shard_map/triangular_solve | solution.py:91
  206.2 2.9 %copy.81 = f32[256,2048]{1,0:T(8,128)} copy(f32[256,2048]{0,1:T(8,128)} %bitcast.133) | data formatting | bytes 4194304 | tf_op jit(solution)/shard_map/reshape | solution.py:92
  (63 shorter events, 22.6 us)
Async XLA Ops:
  0.0 2.8 %copy-start.1 = (bf16[64,8192]{1,0:T(8,128)(2,1)S(1)}, bf16[64,8192]{1,0:T(8,128)(2,1)}, u32[]{:S(2)}) copy-start(bf16[64,8192]{1,0:T(8,128)(2,1)} %param.6) | copy-start | bytes 3145732
  7.7 32.6 %collective-permute-start = (f32[3,128,64]{1,2,0:T(8,128)S(1)}, f32[3,128,64]{1,2,0:T(8,128)S(1)}, u32[]{:S(2)}, u32[]{:S(2)}) collective-permute-start(f32[3,128,64]{1,2,0:T(8,128)S(1)} %pad_maximum_fusion), channel_id=1, source_target_pairs={{0,4},{4,0},{8,12},{12,8},{16,20},{20,16},{24,28},{28,24},{1,5},{5... | collective-permute-start | bytes 294920 | tf_op jit(solution)/shard_map/ppermute | solution.py:15
  16.1 0.7 copy-start.3
  35.8 2.3 %copy-start = (bf16[1,128,8192]{1,2,0:T(8,128)(2,1)S(1)}, bf16[1,128,8192]{1,2,0:T(8,128)(2,1)}, u32[]{:S(2)}) copy-start(bf16[1,128,8192]{1,2,0:T(8,128)(2,1)} %copy.92) | copy-start | bytes 6291460
  40.4 5.3 %collective-permute-start.1 = (f32[2,128,64]{1,2,0:T(8,128)S(1)}, f32[2,128,64]{1,2,0:T(8,128)S(1)}, u32[]{:S(2)}, u32[]{:S(2)}) collective-permute-start(f32[2,128,64]{1,2,0:T(8,128)S(1)} %pad_maximum_fusion.1), channel_id=1, source_target_pairs={{0,8},{4,12},{8,0},{12,4},{16,24},{20,28},{24,16},{28,20},{1,9},{5... | collective-permute-start | bytes 196616 | tf_op jit(solution)/shard_map/ppermute | solution.py:15
  45.7 3.9 %copy-start.2 = (bf16[64,8192]{1,0:T(8,128)(2,1)S(1)}, bf16[64,8192]{1,0:T(8,128)(2,1)}, u32[]{:S(2)}) copy-start(bf16[64,8192]{1,0:T(8,128)(2,1)} %param.5) | copy-start | bytes 3145732
  45.7 3.9 %collective-permute-start.2 = (bf16[1,128,64]{1,2,0:T(8,128)(2,1)S(1)}, bf16[1,128,64]{1,2,0:T(8,128)(2,1)S(1)}, u32[]{:S(2)}, u32[]{:S(2)}) collective-permute-start(bf16[1,128,64]{1,2,0:T(8,128)(2,1)S(1)} %slice_add_fusion), channel_id=1, source_target_pairs={{0,16},{4,20},{8,24},{12,28},{16,0},{20,4},{24,8},{28,12},{1,17},{... | collective-permute-start | bytes 49160 | tf_op jit(solution)/shard_map/ppermute | solution.py:15
  55.2 30.2 %all-to-all-start = ((bf16[64,4,2048]{2,0,1:T(8,128)(2,1)}), bf16[64,4,2048]{2,0,1:T(8,128)(2,1)S(1)}, u32[]{:S(2)}, u32[]{:S(2)}) async-start(bf16[64,4,2048]{2,0,1:T(8,128)(2,1)} %bitcast.119), calls=%async_computation | async-start | bytes 2097152 | tf_op jit(solution)/shard_map/all_to_all | solution.py:75
where the time goes:
time: 210 us; the launch traced here: 209 us
  other arithmetic  112 us (53%)
  local copies, waits for them, and re-layouts  37.5 us (18%)
  waiting for transfers between devices  26.5 us (13%)
  matrix products  22.4 us (11%)
  starting transfers between devices  9.96 us (5%)
    another operation x10, other arithmetic, shards(): lower_factor = jnp.linalg.cholesky(shifted)  66.9 us
    another operation x4, other arithmetic, shards(): lax.linalg.triangular_solve(lower_factor, right_sides, left_side=True, lo...  40.3 us
    all_to_all x1, waiting for transfers between devices, shards(): lax.all_to_all(sample, 'probe', split_axis=1, concat_axis=0, tiled=True)  24.3 us
    unnamed x12, local copies, waits for them, and re-layouts  14.7 us
    dot_general x5, matrix products, shards(): jnp.einsum('kcn,rcn->ckr', right_part, probe_part, preferred_element_type...  10.4 us
    dot_general x5, matrix products, shards(): jnp.einsum('ckr,kcn->rcn', sibling, left_part, preferred_element_type=jnp...  8.22 us
    another operation x6, local copies, waits for them, and re-layouts  5.28 us
    all_to_all x1, starting transfers between devices, shards(): lax.all_to_all(sample, 'probe', split_axis=1, concat_axis=0, tiled=True)  5.05 us
  transfers between devices with their start and end apart: 4, of which 2 were waited for; matrix products, arithmetic and copies ran while one was open for 17% of the time, Pallas kernels for 0%

commit v1 on v0

v1 whole, which is shorter than its diff:
```python
import functools

import jax
import jax.numpy as jnp
from jax import lax
from jax.experimental import pallas as pl
from jax.experimental.pallas import tpu as pltpu
from jax.sharding import PartitionSpec as P

BLOCKS = 64

ridge_share = 0.05

LANES = 128
SUBLANES = 8
EXACT = lax.Precision.HIGHEST
VMEM_LIMIT = 40 * 2**20


def xor_permute(value, axis, mask):
    pairs = [(source, source ^ mask) for source in range(lax.axis_size(axis))]
    return lax.ppermute(value, axis, pairs)


def coupling_kernel(parts, steps, probes_ref, right_ref, out_ref):
    step = pl.program_id(0)
    per_part = steps // parts
    part = step // per_part

    @pl.when(step % per_part == 0)
    def _():
        out_ref[:, part] = jnp.zeros_like(out_ref[:, part])

    for slot in range(out_ref.shape[0]):
        out_ref[slot, part] += lax.dot_general(
            probes_ref[...],
            right_ref[slot],
            (((1,), (1,)), ((), ())),
            preferred_element_type=jnp.float32,
        )


def couplings(probes, right_factors, levels, parts):
    local_probes, rows_dev = probes.shape
    count = len(levels)
    first = levels[0]
    rank_width = right_factors.shape[1]
    chunk = min(1024, rows_dev // parts)
    steps = rows_dev // chunk
    return pl.pallas_call(
        functools.partial(coupling_kernel, parts, steps),
        grid=(steps,),
        in_specs=[
            pl.BlockSpec((local_probes, chunk), lambda s: (0, s)),
            pl.BlockSpec((count, rank_width, chunk), lambda s: (first // count, 0, s)),
        ],
        out_specs=pl.BlockSpec((count, parts, local_probes, rank_width), lambda s: (0, 0, 0, 0)),
        out_shape=jax.ShapeDtypeStruct((count, parts, local_probes, rank_width), jnp.float32),
        compiler_params=pltpu.CompilerParams(vmem_limit_bytes=VMEM_LIMIT),
        cost_estimate=pl.CostEstimate(
            flops=2 * count * rank_width * local_probes * rows_dev,
            bytes_accessed=2 * rows_dev * (count * rank_width + local_probes),
            transcendentals=0,
        ),
        name="couplings",
    )(probes, right_factors)


def update_kernel(masks, where_ref, *refs):
    payload_refs = refs[: len(masks)]
    left_ref, out_ref, sibling_ref = refs[len(masks) :]
    levels, local_probes, rank_width = payload_refs[0].shape

    @pl.when(pl.program_id(0) == 0)
    def _():
        for mask, payload_ref in zip(masks, payload_refs):
            start = pl.multiple_of((where_ref[0] ^ mask) * local_probes, local_probes)
            for level in range(levels):
                sibling_ref[pl.ds(start, local_probes), level * rank_width : (level + 1) * rank_width] = (
                    payload_ref[level]
                )

    chunk = left_ref.shape[2]
    out_ref[...] = jnp.dot(
        sibling_ref[...],
        left_ref[...].reshape(levels * rank_width, chunk),
        preferred_element_type=jnp.float32,
    )


def update_of_slab(payloads, masks, left_factors, where, slab_rows):
    levels, local_probes, rank_width = payloads[0].shape
    all_probes = local_probes * len(masks)
    chunk = min(512, slab_rows)
    steps = slab_rows // chunk
    whole = pl.BlockSpec((levels, local_probes, rank_width), lambda s, w: (0, 0, 0))
    return pl.pallas_call(
        functools.partial(update_kernel, masks),
        grid_spec=pltpu.PrefetchScalarGridSpec(
            num_scalar_prefetch=1,
            grid=(steps,),
            in_specs=[whole] * len(masks)
            + [pl.BlockSpec((levels, rank_width, chunk), lambda s, w: (0, 0, w[0] * steps + s))],
            out_specs=pl.BlockSpec((all_probes, chunk), lambda s, w: (0, s)),
            scratch_shapes=[pltpu.VMEM((all_probes, levels * rank_width), jnp.bfloat16)],
        ),
        out_shape=jax.ShapeDtypeStruct((all_probes, slab_rows), jnp.float32),
        compiler_params=pltpu.CompilerParams(vmem_limit_bytes=VMEM_LIMIT),
        cost_estimate=pl.CostEstimate(
            flops=2 * levels * rank_width * all_probes * slab_rows,
            bytes_accessed=slab_rows * (2 * levels * rank_width + 4 * all_probes),
            transcendentals=0,
        ),
        name="update",
    )(where, *payloads, left_factors)


def row_of(value, index):
    return jnp.broadcast_to(value[index : index + 1, :], value.shape)


def column_of(value, index):
    return jnp.broadcast_to(value[:, index : index + 1], value.shape)


def sum_tree(terms):
    while len(terms) > 1:
        terms = [
            terms[i] + terms[i + 1] if i + 1 < len(terms) else terms[i]
            for i in range(0, len(terms), 2)
        ]
    return terms[0]


def eliminate(tiles, offset):
    row_iota = lax.broadcasted_iota(jnp.int32, (SUBLANES, LANES), 0)
    equal = [row_iota == a for a in range(SUBLANES)]
    after = [row_iota >= a for a in range(SUBLANES)]
    tiles = list(tiles)
    finished = []
    for group in range(len(tiles)):
        base = offset + SUBLANES * group
        pivot = tiles[group]
        columns = [column_of(pivot, base + b) for b in range(SUBLANES)]
        rest = range(group + 1, len(tiles))
        rest_columns = {h: [column_of(tiles[h], base + c) for c in range(SUBLANES)] for h in rest}
        scaled = None
        for a in range(SUBLANES):
            diagonal = row_of(columns[a], a)
            inverse = 1.0 / diagonal
            current = row_of(pivot, a)
            root_row = current * lax.rsqrt(diagonal)
            scaled = root_row if a == 0 else jnp.where(after[a], root_row, scaled)
            unit_row = current * inverse
            pivot = jnp.where(equal[a], unit_row, pivot - columns[a] * unit_row)
            for b in range(a + 1, SUBLANES):
                entry = row_of(columns[b], a) * inverse
                columns[b] = jnp.where(equal[a], entry, columns[b] - columns[a] * entry)
        finished.append(scaled)
        solved = [row_of(pivot, c) for c in range(SUBLANES)]
        for h in rest:
            tiles[h] = tiles[h] - sum_tree([rest_columns[h][c] * solved[c] for c in range(SUBLANES)])
    return jnp.concatenate(finished, 0)


def lane_groups(value):
    return [value[:, i : i + LANES] for i in range(0, value.shape[1], LANES)]


def inverse_factors(grams):
    size = grams[0].shape[0]
    block = LANES // 2
    count = size // block
    lane = lax.broadcasted_iota(jnp.int32, (block, LANES), 1)
    sub = lax.broadcasted_iota(jnp.int32, (block, LANES), 0)
    work = [[gram[block * k : block * (k + 1)] for k in range(count)] for gram in grams]
    result = [[] for _ in grams]
    for k in range(count):
        offset = (block * k) % LANES
        other = block - offset
        group = (block * k) // LANES
        mine = (lane >= offset) & (lane < offset + block)
        eye_mine = jnp.where(lane == sub + offset, 1.0, 0.0)
        eye_other = jnp.where(lane == sub + other, 1.0, 0.0)
        for m in range(len(grams)):
            start = jnp.where(mine, lane_groups(work[m][k])[group], eye_other)
            rows = eliminate([start[i : i + SUBLANES] for i in range(0, block, SUBLANES)], offset)
            inverse = jnp.where(mine, 0.0, rows)
            parts = lane_groups(work[m][k])
            parts[group] = jnp.where(mine, eye_mine, parts[group])
            right_side = jnp.concatenate(parts, 1)
            done = jnp.dot(
                inverse,
                jnp.concatenate([right_side, right_side], 0),
                preferred_element_type=jnp.float32,
                precision=EXACT,
            )
            result[m].append(done)
            moved = pltpu.roll(inverse, block, 1)
            for i in range(k + 1, count):
                parts = lane_groups(work[m][i])
                panel = lax.dot_general(
                    jnp.where(mine, parts[group], 0.0),
                    moved,
                    (((1,), (1,)), ((), ())),
                    preferred_element_type=jnp.float32,
                    precision=EXACT,
                )
                parts[group] = jnp.where(mine, 0.0, parts[group])
                work[m][i] = jnp.concatenate(parts, 1) - jnp.dot(
                    panel, done, preferred_element_type=jnp.float32, precision=EXACT
                )
    out = []
    for m in range(len(grams)):
        wide = lax.broadcasted_iota(jnp.int32, (block, size), 1)
        out.append(
            jnp.concatenate(
                [jnp.where(wide < block * (k + 1), result[m][k], 0.0) for k in range(count)], 0
            )
        )
    return out


def fill_sample(masks, where_ref, piece_refs, update_ref, sample_ref):
    local_probes = piece_refs[0].shape[0]
    for mask, piece_ref in zip(masks, piece_refs):
        start = pl.multiple_of((where_ref[0] ^ mask) * local_probes, local_probes)
        rows = pl.ds(start, local_probes)
        sample_ref[rows, :] = (piece_ref[...].astype(jnp.float32) - update_ref[rows, :]).astype(
            jnp.bfloat16
        )


def gram_of(sample):
    return lax.dot_general(
        sample, sample, (((1,), (1,)), ((), ())), preferred_element_type=jnp.float32
    )


def shifted(gram, shift):
    size = gram.shape[0]
    on_diagonal = lax.broadcasted_iota(jnp.int32, (size, size), 0) == lax.broadcasted_iota(
        jnp.int32, (size, size), 1
    )
    return jnp.where(on_diagonal, gram + shift, gram)


def write_basis(factors, sample_ref, out_ref, buffer_ref, sems):
    all_probes, slab_rows = sample_ref.shape
    piece_rows = slab_rows // len(factors)
    chunk = slab_rows // sems.shape[0]
    copies = []
    terms = []
    for factor in factors:
        high = factor.astype(jnp.bfloat16)
        rest = factor - high.astype(jnp.float32)
        middle = rest.astype(jnp.bfloat16)
        terms.append((high, middle))
    for index in range(sems.shape[0]):
        columns = pl.ds(index * chunk, chunk)
        high, middle = terms[index * chunk // piece_rows]
        part = sample_ref[:, columns]
        buffer_ref[:, columns] = jnp.dot(
            high, part, preferred_element_type=jnp.float32
        ) + jnp.dot(middle, part, preferred_element_type=jnp.float32)
        copy = pltpu.make_async_copy(
            buffer_ref.at[:, columns], out_ref.at[:, columns], sems.at[index]
        )
        copy.start()
        copies.append(copy)
    for copy in copies:
        copy.wait()


def slab_kernel(masks, pieces, shift, where_ref, *refs):
    piece_refs = refs[: len(masks)]
    update_ref, out_ref, sample_ref, buffer_ref, sems = refs[len(masks) :]
    fill_sample(masks, where_ref, piece_refs, update_ref, sample_ref)
    piece_rows = sample_ref.shape[1] // pieces
    grams = [
        shifted(gram_of(sample_ref[:, i * piece_rows : (i + 1) * piece_rows]), shift)
        for i in range(pieces)
    ]
    write_basis(inverse_factors(grams), sample_ref, out_ref, buffer_ref, sems)


def sample_kernel(masks, where_ref, *refs):
    piece_refs = refs[: len(masks)]
    update_ref, sample_ref, gram_ref = refs[len(masks) :]
    fill_sample(masks, where_ref, piece_refs, update_ref, sample_ref)
    gram_ref[...] = gram_of(sample_ref[...])


def basis_kernel(shift, gram_ref, sample_ref, out_ref, buffer_ref, sems):
    factors = inverse_factors([shifted(gram_ref[...], shift)])
    write_basis(factors, sample_ref, out_ref, buffer_ref, sems)


def smem():
    return pl.BlockSpec(memory_space=pltpu.SMEM)


def vmem():
    return pl.BlockSpec(memory_space=pltpu.VMEM)


def chunks_of(slab_rows):
    return max(1, slab_rows // 512)


def slab_basis(pieces, masks, update, where, block_rows):
    all_probes, slab_rows = update.shape
    count = slab_rows // block_rows
    chunks = chunks_of(slab_rows)
    return pl.pallas_call(
        functools.partial(slab_kernel, masks, count, ridge_share * block_rows),
        in_specs=[smem()] + [vmem()] * (len(masks) + 1),
        out_specs=pl.BlockSpec(memory_space=pl.ANY),
        out_shape=jax.ShapeDtypeStruct((all_probes, slab_rows), jnp.float32),
        scratch_shapes=[
            pltpu.VMEM((all_probes, slab_rows), jnp.bfloat16),
            pltpu.VMEM((all_probes, slab_rows), jnp.float32),
            pltpu.SemaphoreType.DMA((chunks,)),
        ],
        compiler_params=pltpu.CompilerParams(vmem_limit_bytes=VMEM_LIMIT),
        name="slab_basis",
    )(where, *pieces, update)


def shared_basis(pieces, masks, update, where, block_rows):
    all_probes, slab_rows = update.shape
    sample, gram = pl.pallas_call(
        functools.partial(sample_kernel, masks),
        in_specs=[smem()] + [vmem()] * (len(masks) + 1),
        out_specs=[vmem(), vmem()],
        out_shape=[
            jax.ShapeDtypeStruct((all_probes, slab_rows), jnp.bfloat16),
            jax.ShapeDtypeStruct((all_probes, all_probes), jnp.float32),
        ],
        compiler_params=pltpu.CompilerParams(vmem_limit_bytes=VMEM_LIMIT),
        name="sample_gram",
    )(where, *pieces, update)
    apart = 1
    while apart * slab_rows < block_rows:
        gram = gram + xor_permute(gram, "probe", apart)
        apart *= 2
    chunks = chunks_of(slab_rows)
    return pl.pallas_call(
        functools.partial(basis_kernel, ridge_share * block_rows),
        in_specs=[vmem(), vmem()],
        out_specs=pl.BlockSpec(memory_space=pl.ANY),
        out_shape=jax.ShapeDtypeStruct((all_probes, slab_rows), jnp.float32),
        scratch_shapes=[
            pltpu.VMEM((all_probes, slab_rows), jnp.float32),
            pltpu.SemaphoreType.DMA((chunks,)),
        ],
        compiler_params=pltpu.CompilerParams(vmem_limit_bytes=VMEM_LIMIT),
        name="basis",
    )(gram, sample)


def shards(responses, probes, left_factors, right_factors, level_ranks):
    rows_count = lax.axis_size("rows")
    probe_count = lax.axis_size("probe")
    local_probes, rows_dev = responses.shape
    levels_count, rank_width, _ = left_factors.shape
    slab_rows = rows_dev // probe_count
    block_rows = rows_dev * rows_count // BLOCKS
    place = lax.axis_index("probe")
    where = place.astype(jnp.int32).reshape(1)
    masks = tuple(range(probe_count))

    order = sorted(range(1, probe_count), key=lambda mask: -mask.bit_length())
    pieces = {0: lax.dynamic_slice_in_dim(responses, place * slab_rows, slab_rows, 1)}
    for mask in order:
        piece = lax.dynamic_slice_in_dim(responses, (place ^ mask) * slab_rows, slab_rows, 1)
        pieces[mask] = xor_permute(piece, "probe", mask)

    wide = [l for l in range(levels_count) if 2 ** (l + 1) <= rows_count]
    narrow = [l for l in range(levels_count) if 2 ** (l + 1) > rows_count]
    rank_iota = jnp.arange(rank_width)

    def masked(value, level):
        return jnp.where(rank_iota < level_ranks[level], value, 0.0).astype(jnp.bfloat16)

    running = couplings(probes, right_factors, wide, 1)[:, 0]
    siblings = {}
    spans = {l: (rows_count // 2 ** (l + 1)).bit_length() - 1 for l in wide}
    near = xor_permute(running, "rows", 1)
    sums = {}
    for slot, level in enumerate(wide):
        if spans[level] == 0:
            siblings[level] = near[slot]
        else:
            sums[level] = running[slot] + near[slot]
    for level in sums:
        flip = 2 ** spans[level]
        siblings[level] = sum_tree(
            [xor_permute(sums[level], "rows", flip ^ low) for low in range(0, flip, 2)]
        )
    fixed = [masked(siblings[level], level) for level in wide]
    local = {}
    for level in narrow:
        parts = 2 ** (level + 1) // rows_count
        values = couplings(probes, right_factors, [level], parts)[0]
        local[level] = (parts, masked(values, level))

    def payload_for(target):
        picked = list(fixed)
        for level in narrow:
            parts, values = local[level]
            cluster = (target * parts // probe_count) ^ 1
            picked.append(lax.dynamic_index_in_dim(values, cluster, 0, keepdims=False))
        return jnp.stack(picked)

    payloads = [payload_for(place)]
    for mask in range(1, probe_count):
        payloads.append(xor_permute(payload_for(place ^ mask), "probe", mask))

    update = update_of_slab(payloads, masks, left_factors, where, slab_rows)
    ordered = [pieces[mask] for mask in masks]
    if block_rows > slab_rows:
        return shared_basis(ordered, masks, update, where, block_rows)
    return slab_basis(ordered, masks, update, where, block_rows)


def solution(mesh):
    return jax.shard_map(
        shards,
        mesh=mesh,
        in_specs=(
            P("probe", "rows"),
            P("probe", "rows"),
            P(None, None, "rows"),
            P(None, None, "rows"),
            P(),
        ),
        out_specs=P(None, ("rows", "probe")),
        check_vma=False,
    )
```

time: 210 us -> 71 us (0.34)
  other arithmetic: 112 us -> 3.17 us
  Pallas kernels: 0 us -> 27.6 us
  local copies, waits for them, and re-layouts: 37.5 us -> 14 us
  matrix products: 22.4 us -> 0 us
  waiting for transfers between devices: 26.5 us -> 10 us
  starting transfers between devices: 9.96 us -> 15.4 us
    another operation x14 -> x0, other arithmetic: 107 us -> none  [the longest x10 66.9 us: shards(): lower_factor = jnp.linalg.cholesky(shifted)]
    pallas_call x0 -> x5, Pallas kernels: none -> 27.6 us  [the longest x1 17.6 us: slab_basis(): pl.pallas_call(functools.partial(slab_kernel, masks, count, ridge_share *...]
    all_to_all x1 -> x0, waiting for transfers between devices: 24.3 us -> none  [shards(): lax.all_to_all(sample, 'probe', split_axis=1, concat_axis=0, tiled=True)]
    dot_general x11 -> x0, matrix products: 19.1 us -> none  [the longest x5 10.4 us: shards(): jnp.einsum('kcn,rcn->ckr', right_part, probe_part, preferred_element_type...]
    ppermute x3 -> x10, starting transfers between devices: 4.91 us -> 15.4 us  [xor_permute(): return lax.ppermute(value, axis, pairs)]
    slice x3 -> x1, local copies, waits for them, and re-layouts: 9.98 us -> 0.66 us  [masked(): level_ranks[level]]
    ppermute x3 -> x10, waiting for transfers between devices: 2.13 us -> 10 us  [xor_permute(): return lax.ppermute(value, axis, pairs)]
    another operation x9 -> x1, local copies, waits for them, and re-layouts: 5.4 us -> 0.03 us  [payload_for(): return jnp.stack(picked)]
  transfers between devices with their start and end apart: 4 -> 10, of which waited for: 2 -> 6; matrix products, arithmetic and copies ran while one was open for 17% -> 6% of each run, Pallas kernels for 0% -> 9%
where the time goes in v1:
time: 71 us; the launch traced here: 70.7 us
  Pallas kernels  27.6 us (39%)
  starting transfers between devices  15.4 us (22%)
  local copies, waits for them, and re-layouts  14 us (20%)
  waiting for transfers between devices  10 us (14%)
  other arithmetic  3.17 us (4%)
    pallas_call x1, Pallas kernels, slab_basis(): pl.pallas_call(functools.partial(slab_kernel, masks, count, ridge_share *...  17.6 us
    ppermute x10, starting transfers between devices, xor_permute(): return lax.ppermute(value, axis, pairs)  15.4 us
    unnamed x21, local copies, waits for them, and re-layouts  13.3 us
    ppermute x10, waiting for transfers between devices, xor_permute(): return lax.ppermute(value, axis, pairs)  10 us
    pallas_call x3, Pallas kernels, couplings(): pl.pallas_call(functools.partial(coupling_kernel, parts, steps), grid=(st...  7.87 us
    lt x5, other arithmetic, masked(): rank_iota < level_ranks[level]  3.1 us
    pallas_call x1, Pallas kernels, update_of_slab(): pl.pallas_call(functools.partial(update_kernel, masks), grid_spec=pltpu.P...  2.13 us
  transfers between devices with their start and end apart: 10, of which 6 were waited for; matrix products, arithmetic and copies ran while one was open for 6% of the time, Pallas kernels for 9%

profile of v1, /device:TPU:0, one launch (start us, length us, event | category | flops | bytes accessed | tf_op | source)
XLA Modules:
  0.0 70.7 jit_solution(18123996155870376593)
XLA Ops:
  0.0 4.0 %copy-done = bf16[5,128,8192]{2,1,0:T(8,128)(2,1)S(1)} copy-done((bf16[5,128,8192]{2,1,0:T(8,128)(2,1)S(1)}, bf16[5,128,8192]{2,1,0:T(8,128)(2,1)}, u32[]{:S(2)}) %copy-start) | copy-done | bytes 10485784
  4.0 1.2 %copy-done.3 = bf16[64,8192]{1,0:T(8,128)(2,1)S(1)} copy-done((bf16[64,8192]{1,0:T(8,128)(2,1)S(1)}, bf16[64,8192]{1,0:T(8,128)(2,1)}, u32[]{:S(2)}) %copy-start.3) | copy-done | bytes 1048600
  5.2 3.8 %couplings.3 = f32[3,1,64,128]{3,2,1,0:T(8,128)S(1)} custom-call(bf16[64,8192]{1,0:T(8,128)(2,1)S(1)} %copy-done.3, bf16[5,128,8192]{2,1,0:T(8,128)(2,1)S(1)} %copy-done), custom_call_target="tpu_custom_call" | custom-call | flops 402653184 | bytes 7340032 | tf_op jit(solution)/shard_map/couplings/pallas_call | solution.py:50
  9.6 4.7 %collective-permute-start.2 = (bf16[64,2048]{1,0:T(8,128)(2,1)S(1)}, bf16[64,2048]{1,0:T(8,128)(2,1)S(1)}, u32[]{:S(2)}, u32[]{:S(2)}) collective-permute-start(bf16[64,2048]{1,0:T(8,128)(2,1)S(1)} %get-tuple-element.5), channel_id=1, source_target_pairs={{0,3},{1,2},{2,1},{3,0},{4,7},{5,6},{6,5},{7,4},{8,11},{9,10},{10,... | collective-permute-start | bytes 786440 | tf_op jit(solution)/shard_map/ppermute | solution.py:22
  14.3 0.6 collective-permute-start.1
  15.0 4.0 %copy-done.1 = bf16[5,128,8192]{2,1,0:T(8,128)(2,1)S(1)} copy-done((bf16[5,128,8192]{2,1,0:T(8,128)(2,1)S(1)}, bf16[5,128,8192]{2,1,0:T(8,128)(2,1)}, u32[]{:S(2)}) %copy-start.1) | copy-done | bytes 10485784
  19.0 2.1 %couplings.4 = f32[1,2,64,128]{3,2,1,0:T(8,128)S(1)} custom-call(bf16[64,8192]{1,0:T(8,128)(2,1)S(1)} %copy-done.4, bf16[5,128,8192]{2,1,0:T(8,128)(2,1)S(1)} %copy-done.1), custom_call_target="tpu_custom_call" | custom-call | flops 134217728 | bytes 3145728 | tf_op jit(solution)/shard_map/couplings/pallas_call | solution.py:50
  21.0 2.1 %couplings.5 = f32[1,4,64,128]{3,2,1,0:T(8,128)S(1)} custom-call(bf16[64,8192]{1,0:T(8,128)(2,1)S(1)} %copy-done.4, bf16[5,128,8192]{2,1,0:T(8,128)(2,1)S(1)} %copy-done.1), custom_call_target="tpu_custom_call" | custom-call | flops 134217728 | bytes 3145728 | tf_op jit(solution)/shard_map/couplings/pallas_call | solution.py:50
  23.1 0.7 fusion.7
  23.8 0.6 iota_compare_fusion
  25.0 0.6 iota_compare_fusion.3
  26.3 0.6 iota_compare_fusion.4
  27.0 2.7 %collective-permute-start.5 = (f32[64,128]{1,0:T(8,128)S(1)}, f32[64,128]{1,0:T(8,128)S(1)}, u32[]{:S(2)}, u32[]{:S(2)}) collective-permute-start(f32[64,128]{1,0:T(8,128)S(1)} %fusion.4), channel_id=1, source_target_pairs={{0,24},{4,28},{8,16},{12,20},{16,8},{20,12},{24,0},{28,4},{1,25},{... | collective-permute-start | bytes 98312 | tf_op jit(solution)/shard_map/ppermute | solution.py:22
  30.2 1.7 %collective-permute-done.5 = f32[64,128]{1,0:T(8,128)S(1)} collective-permute-done((f32[64,128]{1,0:T(8,128)S(1)}, f32[64,128]{1,0:T(8,128)S(1)}, u32[]{:S(2)}, u32[]{:S(2)}) %collective-permute-start.5) | collective-permute-done | bytes 32800 | tf_op jit(solution)/shard_map/ppermute | solution.py:22
  31.9 1.6 %collective-permute-start.6 = (bf16[64,128]{1,0:T(8,128)(2,1)S(1)}, bf16[64,128]{1,0:T(8,128)(2,1)S(1)}, u32[]{:S(2)}, u32[]{:S(2)}) collective-permute-start(bf16[64,128]{1,0:T(8,128)(2,1)S(1)} %fusion.3), channel_id=1, source_target_pairs={{0,8},{4,12},{8,0},{12,4},{16,24},{20,28},{24,16},{28,20},{1,9},{5... | collective-permute-start | bytes 49160 | tf_op jit(solution)/shard_map/ppermute | solution.py:22
  33.6 2.0 %collective-permute-done.6 = bf16[64,128]{1,0:T(8,128)(2,1)S(1)} collective-permute-done((bf16[64,128]{1,0:T(8,128)(2,1)S(1)}, bf16[64,128]{1,0:T(8,128)(2,1)S(1)}, u32[]{:S(2)}, u32[]{:S(2)}) %collective-permute-start.6) | collective-permute-done | bytes 16416 | tf_op jit(solution)/shard_map/ppermute | solution.py:22
  35.8 3.9 %collective-permute-start.9 = (bf16[5,64,128]{2,1,0:T(8,128)(2,1)S(1)}, bf16[5,64,128]{2,1,0:T(8,128)(2,1)S(1)}, u32[]{:S(2)}, u32[]{:S(2)}) collective-permute-start(bf16[5,64,128]{2,1,0:T(8,128)(2,1)S(1)} %get-tuple-element.9), channel_id=1, source_target_pairs={{0,3},{1,2},{2,1},{3,0},{4,7},{5,6},{6,5},{7,4},{8,11},{9,10},{10,... | collective-permute-start | bytes 245768 | tf_op jit(solution)/shard_map/ppermute | solution.py:22
  39.7 2.6 %collective-permute-done.9.refs_3_ = bf16[5,64,128]{2,1,0:T(8,128)(2,1)S(1)} collective-permute-done((bf16[5,64,128]{2,1,0:T(8,128)(2,1)S(1)}, bf16[5,64,128]{2,1,0:T(8,128)(2,1)S(1)}, u32[]{:S(2)}, u32[]{:S(2)}) %collective-permute-start.9) | collective-permute-done | bytes 81952 | tf_op jit(solution)/shard_map/ppermute | solution.py:22
  42.3 0.8 %collective-permute-start.7 = (bf16[5,64,128]{2,1,0:T(8,128)(2,1)S(1)}, bf16[5,64,128]{2,1,0:T(8,128)(2,1)S(1)}, u32[]{:S(2)}, u32[]{:S(2)}) collective-permute-start(bf16[5,64,128]{2,1,0:T(8,128)(2,1)S(1)} %get-tuple-element.11), channel_id=1, source_target_pairs={{0,1},{1,0},{2,3},{3,2},{4,5},{5,4},{6,7},{7,6},{8,9},{9,8},{10,11... | collective-permute-start | bytes 245768 | tf_op jit(solution)/shard_map/ppermute | solution.py:22
  43.1 2.0 %collective-permute-done.8.refs_2_ = bf16[5,64,128]{2,1,0:T(8,128)(2,1)S(1)} collective-permute-done((bf16[5,64,128]{2,1,0:T(8,128)(2,1)S(1)}, bf16[5,64,128]{2,1,0:T(8,128)(2,1)S(1)}, u32[]{:S(2)}, u32[]{:S(2)}) %collective-permute-start.8) | collective-permute-done | bytes 81952 | tf_op jit(solution)/shard_map/ppermute | solution.py:22
  45.1 1.7 %collective-permute-done.7.refs_1_ = bf16[5,64,128]{2,1,0:T(8,128)(2,1)S(1)} collective-permute-done((bf16[5,64,128]{2,1,0:T(8,128)(2,1)S(1)}, bf16[5,64,128]{2,1,0:T(8,128)(2,1)S(1)}, u32[]{:S(2)}, u32[]{:S(2)}) %collective-permute-start.7) | collective-permute-done | bytes 81952 | tf_op jit(solution)/shard_map/ppermute | solution.py:22
  46.7 4.0 %copy-done.2 = bf16[5,128,8192]{2,1,0:T(8,128)(2,1)S(1)} copy-done((bf16[5,128,8192]{2,1,0:T(8,128)(2,1)S(1)}, bf16[5,128,8192]{2,1,0:T(8,128)(2,1)}, u32[]{:S(2)}) %copy-start.2) | copy-done | bytes 10485784
  50.7 2.1 %update.1.refs_4_ = f32[256,2048]{1,0:T(8,128)S(1)} custom-call(s32[1]{0:T(128)} %bitcast.where_ref, bf16[5,64,128]{2,1,0:T(8,128)(2,1)S(1)} %get-tuple-element.12.refs_0_, bf16[5,64,128]{2,1,0:T(8,128)(2,1)S(1)} %collective-permute-done.7.refs_1_, bf16[5,64,128]{2,1,0:T(8,128)(2,1)S(1)} %collective-permute-done.8.refs_2_, ...), custom_call_target="tpu_custom_call" | custom-call | flops 671088640 | bytes 4718592 | tf_op jit(solution)/shard_map/update/pallas_call | solution.py:97
  52.9 17.6 %slab_basis.1 = f32[256,2048]{1,0:T(8,128)} custom-call(s32[1]{0:T(128)} %bitcast.where_ref, bf16[64,2048]{1,0:T(8,128)(2,1)S(1)} %get-tuple-element.7.refs_0_, bf16[64,2048]{1,0:T(8,128)(2,1)S(1)} %collective-permute-done.refs_1_, bf16[64,2048]{1,0:T(8,128)(2,1)S(1)} %collective-permute-done.1.refs_2_, bf16[64,2048]{1,0:T(8,128)(2,1)S(1)} %collective-permute-done.2.refs_3_, ...), custom_call_target="tpu_custom_call" | custom-call | tf_op jit(solution)/shard_map/slab_basis/pallas_call | solution.py:315
  (37 shorter events, 2.6 us)
Async XLA Ops:
  0.0 4.0 %copy-start = (bf16[5,128,8192]{2,1,0:T(8,128)(2,1)S(1)}, bf16[5,128,8192]{2,1,0:T(8,128)(2,1)}, u32[]{:S(2)}) copy-start(bf16[5,128,8192]{2,1,0:T(8,128)(2,1)} %right_ref.5) | copy-start | bytes 31457284
  4.0 1.2 %copy-start.3 = (bf16[64,8192]{1,0:T(8,128)(2,1)S(1)}, bf16[64,8192]{1,0:T(8,128)(2,1)}, u32[]{:S(2)}) copy-start(bf16[64,8192]{1,0:T(8,128)(2,1)} %probes_ref.5) | copy-start | bytes 3145732
  5.2 4.3 %copy-start.5 = (bf16[64,8192]{1,0:T(8,128)(2,1)S(1)}, bf16[64,8192]{1,0:T(8,128)(2,1)}, u32[]{:S(2)}) copy-start(bf16[64,8192]{1,0:T(8,128)(2,1)} %param.5) | copy-start | bytes 3145732
  5.2 9.8 %copy-start.4 = (bf16[64,8192]{1,0:T(8,128)(2,1)S(1)}, bf16[64,8192]{1,0:T(8,128)(2,1)}, u32[]{:S(2)}) copy-start(bf16[64,8192]{1,0:T(8,128)(2,1)} %probes_ref.5) | copy-start | bytes 3145732
  9.0 18.0 %collective-permute-start.3 = (f32[3,64,128]{2,1,0:T(8,128)S(1)}, f32[3,64,128]{2,1,0:T(8,128)S(1)}, u32[]{:S(2)}, u32[]{:S(2)}) collective-permute-start(f32[3,64,128]{2,1,0:T(8,128)S(1)} %bitcast.35), channel_id=1, source_target_pairs={{0,4},{4,0},{8,12},{12,8},{16,20},{20,16},{24,28},{28,24},{1,5},{5... | collective-permute-start | bytes 294920 | tf_op jit(solution)/shard_map/ppermute | solution.py:22
  9.6 43.3 %collective-permute-start.2 = (bf16[64,2048]{1,0:T(8,128)(2,1)S(1)}, bf16[64,2048]{1,0:T(8,128)(2,1)S(1)}, u32[]{:S(2)}, u32[]{:S(2)}) collective-permute-start(bf16[64,2048]{1,0:T(8,128)(2,1)S(1)} %get-tuple-element.5), channel_id=1, source_target_pairs={{0,3},{1,2},{2,1},{3,0},{4,7},{5,6},{6,5},{7,4},{8,11},{9,10},{10,... | collective-permute-start | bytes 786440 | tf_op jit(solution)/shard_map/ppermute | solution.py:22
  14.3 38.5 %collective-permute-start = (bf16[64,2048]{1,0:T(8,128)(2,1)S(1)}, bf16[64,2048]{1,0:T(8,128)(2,1)S(1)}, u32[]{:S(2)}, u32[]{:S(2)}) collective-permute-start(bf16[64,2048]{1,0:T(8,128)(2,1)S(1)} %get-tuple-element.6), channel_id=1, source_target_pairs={{0,1},{1,0},{2,3},{3,2},{4,5},{5,4},{6,7},{7,6},{8,9},{9,8},{10,11... | collective-permute-start | bytes 786440 | tf_op jit(solution)/shard_map/ppermute | solution.py:22
  14.3 38.6 %collective-permute-start.1 = (bf16[64,2048]{1,0:T(8,128)(2,1)S(1)}, bf16[64,2048]{1,0:T(8,128)(2,1)S(1)}, u32[]{:S(2)}, u32[]{:S(2)}) collective-permute-start(bf16[64,2048]{1,0:T(8,128)(2,1)S(1)} %get-tuple-element.8), channel_id=1, source_target_pairs={{0,2},{1,3},{2,0},{3,1},{4,6},{5,7},{6,4},{7,5},{8,10},{9,11},{10,... | collective-permute-start | bytes 786440 | tf_op jit(solution)/shard_map/ppermute | solution.py:22
  15.0 4.0 %copy-start.1 = (bf16[5,128,8192]{2,1,0:T(8,128)(2,1)S(1)}, bf16[5,128,8192]{2,1,0:T(8,128)(2,1)}, u32[]{:S(2)}) copy-start(bf16[5,128,8192]{2,1,0:T(8,128)(2,1)} %right_ref.5) | copy-start | bytes 31457284
  18.9 4.1 %copy-start.6 = (s32[5]{0:T(128)S(1)}, s32[5]{0:T(128)}, u32[]{:S(2)}) copy-start(s32[5]{0:T(128)} %param.9) | copy-start | bytes 64
  27.0 4.9 %collective-permute-start.5 = (f32[64,128]{1,0:T(8,128)S(1)}, f32[64,128]{1,0:T(8,128)S(1)}, u32[]{:S(2)}, u32[]{:S(2)}) collective-permute-start(f32[64,128]{1,0:T(8,128)S(1)} %fusion.4), channel_id=1, source_target_pairs={{0,24},{4,28},{8,16},{12,20},{16,8},{20,12},{24,0},{28,4},{1,25},{... | collective-permute-start | bytes 98312 | tf_op jit(solution)/shard_map/ppermute | solution.py:22
  29.7 3.9 %collective-permute-start.4 = (f32[64,128]{1,0:T(8,128)S(1)}, f32[64,128]{1,0:T(8,128)S(1)}, u32[]{:S(2)}, u32[]{:S(2)}) collective-permute-start(f32[64,128]{1,0:T(8,128)S(1)} %fusion.4), channel_id=1, source_target_pairs={{0,16},{4,20},{8,24},{12,28},{16,0},{20,4},{24,8},{28,12},{1,17},{... | collective-permute-start | bytes 98312 | tf_op jit(solution)/shard_map/ppermute | solution.py:22
  31.9 3.7 %collective-permute-start.6 = (bf16[64,128]{1,0:T(8,128)(2,1)S(1)}, bf16[64,128]{1,0:T(8,128)(2,1)S(1)}, u32[]{:S(2)}, u32[]{:S(2)}) collective-permute-start(bf16[64,128]{1,0:T(8,128)(2,1)S(1)} %fusion.3), channel_id=1, source_target_pairs={{0,8},{4,12},{8,0},{12,4},{16,24},{20,28},{24,16},{28,20},{1,9},{5... | collective-permute-start | bytes 49160 | tf_op jit(solution)/shard_map/ppermute | solution.py:22
  35.8 6.5 %collective-permute-start.9 = (bf16[5,64,128]{2,1,0:T(8,128)(2,1)S(1)}, bf16[5,64,128]{2,1,0:T(8,128)(2,1)S(1)}, u32[]{:S(2)}, u32[]{:S(2)}) collective-permute-start(bf16[5,64,128]{2,1,0:T(8,128)(2,1)S(1)} %get-tuple-element.9), channel_id=1, source_target_pairs={{0,3},{1,2},{2,1},{3,0},{4,7},{5,6},{6,5},{7,4},{8,11},{9,10},{10,... | collective-permute-start | bytes 245768 | tf_op jit(solution)/shard_map/ppermute | solution.py:22
  39.7 5.3 %collective-permute-start.8 = (bf16[5,64,128]{2,1,0:T(8,128)(2,1)S(1)}, bf16[5,64,128]{2,1,0:T(8,128)(2,1)S(1)}, u32[]{:S(2)}, u32[]{:S(2)}) collective-permute-start(bf16[5,64,128]{2,1,0:T(8,128)(2,1)S(1)} %get-tuple-element.10), channel_id=1, source_target_pairs={{0,2},{1,3},{2,0},{3,1},{4,6},{5,7},{6,4},{7,5},{8,10},{9,11},{10,... | collective-permute-start | bytes 245768 | tf_op jit(solution)/shard_map/ppermute | solution.py:22
  42.3 4.4 %collective-permute-start.7 = (bf16[5,64,128]{2,1,0:T(8,128)(2,1)S(1)}, bf16[5,64,128]{2,1,0:T(8,128)(2,1)S(1)}, u32[]{:S(2)}, u32[]{:S(2)}) collective-permute-start(bf16[5,64,128]{2,1,0:T(8,128)(2,1)S(1)} %get-tuple-element.11), channel_id=1, source_target_pairs={{0,1},{1,0},{2,3},{3,2},{4,5},{5,4},{6,7},{7,6},{8,9},{9,8},{10,11... | collective-permute-start | bytes 245768 | tf_op jit(solution)/shard_map/ppermute | solution.py:22
  46.7 4.0 %copy-start.2 = (bf16[5,128,8192]{2,1,0:T(8,128)(2,1)S(1)}, bf16[5,128,8192]{2,1,0:T(8,128)(2,1)}, u32[]{:S(2)}) copy-start(bf16[5,128,8192]{2,1,0:T(8,128)(2,1)} %refs_4_.1) | copy-start | bytes 31457284

commit v2 on v0

v2 whole, which is shorter than its diff:
```python
import functools

import jax
import jax.numpy as jnp
from jax import lax
from jax.experimental import pallas as pl
from jax.experimental.pallas import tpu as pltpu
from jax.sharding import PartitionSpec as P

BLOCKS = 64

ridge_share = 0.05

LANES = 128
SUBLANES = 8
EXACT = lax.Precision.HIGHEST
VMEM_LIMIT = 24 * 2**20
STREAM_VMEM = 48 * 2**20
CHEAP = pl.CostEstimate(flops=1, bytes_accessed=1, transcendentals=0)


def xor_permute(value, axis, mask):
    pairs = [(source, source ^ mask) for source in range(lax.axis_size(axis))]
    return lax.ppermute(value, axis, pairs)


def smem():
    return pl.BlockSpec(memory_space=pltpu.SMEM)


def vmem():
    return pl.BlockSpec(memory_space=pltpu.VMEM)


def hbm():
    return pl.BlockSpec(memory_space=pltpu.HBM)


def chunks_of(slab_rows):
    return max(1, slab_rows // 512)


def coupling_kernel(parts, joined, ahead, ranks_ref, probes_ref, right_ref, *refs):
    out_refs = refs[:-5]
    probe_buffer, right_buffer, total_ref, probe_sems, right_sems = refs[-5:]
    levels, rank_width, rows_dev = right_buffer.shape
    local_probes = probe_buffer.shape[0]
    chunks = probe_sems.shape[0]
    chunk = rows_dev // chunks
    starts = [sum(parts[:slot]) for slot in range(levels)]

    def columns_of(index):
        return pl.ds(pl.multiple_of(index * chunk, chunk), chunk)

    def copies(index):
        columns = columns_of(index)
        return (
            pltpu.make_async_copy(
                probes_ref.at[:, columns], probe_buffer.at[:, columns], probe_sems.at[index]
            ),
            pltpu.make_async_copy(
                right_ref.at[:, :, columns],
                right_buffer.at[:, :, columns],
                right_sems.at[index],
            ),
        )

    for index in range(min(ahead, chunks)):
        for copy in copies(index):
            copy.start()
    total_ref[...] = jnp.zeros_like(total_ref)

    def add_chunk(index, carry):
        for copy in copies(index):
            copy.wait()

        @pl.when(index + ahead < chunks)
        def _():
            for copy in copies(index + ahead):
                copy.start()

        columns = columns_of(index)
        term = lax.dot_general(
            right_buffer[:, :, columns].reshape(levels * rank_width, chunk),
            probe_buffer[:, columns],
            (((1,), (1,)), ((), ())),
            preferred_element_type=jnp.float32,
        )
        for slot in range(levels):
            part = starts[slot] + index // (chunks // parts[slot])
            total_ref[part] += term[slot * rank_width : (slot + 1) * rank_width]
        return carry

    lax.fori_loop(0, chunks, add_chunk, 0)
    rank = lax.broadcasted_iota(jnp.int32, (rank_width, local_probes), 0)
    for slot in range(levels):
        for part in range(parts[slot]):
            kept = jnp.where(rank < ranks_ref[slot], total_ref[starts[slot] + part], 0.0).T
            if slot < joined:
                out_refs[0][slot] = kept
            else:
                out_refs[slot - joined + 1][part] = kept.astype(jnp.bfloat16)


def couplings(probes, right_factors, level_ranks, parts, joined):
    local_probes, rows_dev = probes.shape
    levels, rank_width, _ = right_factors.shape
    chunks = max(4, *parts)
    shapes = [jax.ShapeDtypeStruct((joined, local_probes, rank_width), jnp.float32)] + [
        jax.ShapeDtypeStruct((count, local_probes, rank_width), jnp.bfloat16)
        for count in parts[joined:]
    ]
    return pl.pallas_call(
        functools.partial(coupling_kernel, tuple(parts), joined, 2),
        in_specs=[smem(), hbm(), hbm()],
        out_specs=[vmem()] * len(shapes),
        out_shape=shapes,
        scratch_shapes=[
            pltpu.VMEM((local_probes, rows_dev), probes.dtype),
            pltpu.VMEM((levels, rank_width, rows_dev), right_factors.dtype),
            pltpu.VMEM((sum(parts), rank_width, local_probes), jnp.float32),
            pltpu.SemaphoreType.DMA((chunks,)),
            pltpu.SemaphoreType.DMA((chunks,)),
        ],
        compiler_params=pltpu.CompilerParams(vmem_limit_bytes=STREAM_VMEM),
        cost_estimate=CHEAP,
        name="couplings",
    )(level_ranks, probes, right_factors)


def pack_kernel(masks, sources, narrow_parts, where_ref, early_ref, near_ref, *refs):
    out_refs = refs[-len(masks) :]
    term_refs = list(refs[: -len(masks)])
    level = 0
    for kind, value in sources:
        if kind == "slot":
            sibling = near_ref[value]
        else:
            terms, term_refs = term_refs[:value], term_refs[value:]
            sibling = sum_tree([term[...] for term in terms])
        sibling = sibling.astype(jnp.bfloat16)
        for out_ref in out_refs:
            out_ref[level] = sibling
        level += 1
    for parts, values_ref in zip(narrow_parts, term_refs):
        for mask, out_ref in zip(masks, out_refs):
            out_ref[level] = values_ref[((where_ref[0] ^ mask) * parts // len(masks)) ^ 1]
        level += 1


def payloads_of(masks, sources, early, near, terms, narrow_parts, local, where):
    _, local_probes, rank_width = near.shape
    shape = (len(sources) + len(local), local_probes, rank_width)
    return pl.pallas_call(
        functools.partial(pack_kernel, masks, tuple(sources), tuple(narrow_parts)),
        in_specs=[smem(), hbm()] + [vmem()] * (1 + len(terms) + len(local)),
        out_specs=[vmem()] * len(masks),
        out_shape=[jax.ShapeDtypeStruct(shape, jnp.bfloat16)] * len(masks),
        compiler_params=pltpu.CompilerParams(vmem_limit_bytes=VMEM_LIMIT),
        cost_estimate=CHEAP,
        name="payloads",
    )(where, early, near, *terms, *local)


HALF = LANES // 2


def row_of(value, index):
    return jnp.broadcast_to(value[index : index + 1, :], value.shape)


def column_of(value, index, half_start):
    return jnp.take_along_axis(value, half_start + index, axis=1)


def sum_tree(terms):
    while len(terms) > 1:
        terms = [
            terms[i] + terms[i + 1] if i + 1 < len(terms) else terms[i]
            for i in range(0, len(terms), 2)
        ]
    return terms[0]


def eliminate(left, right):
    row_iota = lax.broadcasted_iota(jnp.int32, (SUBLANES, LANES), 0)
    half_start = lax.broadcasted_iota(jnp.int32, (SUBLANES, LANES), 1) // HALF * HALF
    equal = [row_iota == a for a in range(SUBLANES)]
    after = [row_iota >= a for a in range(SUBLANES)]
    left, right = list(left), list(right)
    finished = []
    for group in range(len(left)):
        base = SUBLANES * group
        pivot_left, pivot_right = left[group], right[group]
        columns = [column_of(pivot_left, base + b, half_start) for b in range(SUBLANES)]
        rest = range(group + 1, len(left))
        rest_columns = {
            h: [column_of(left[h], base + c, half_start) for c in range(SUBLANES)] for h in rest
        }
        inverses = []
        collected = pivots = None
        for a in range(0, SUBLANES, 2):
            first = row_of(columns[a], a)
            cross = row_of(columns[a + 1], a)
            determinant = first * row_of(columns[a + 1], a + 1) - cross * cross
            inverse_first = 1.0 / first
            inverse_second = first * (1.0 / determinant)
            second = determinant * inverse_first
            for at, diagonal, inverse in (
                (a, first, inverse_first),
                (a + 1, second, inverse_second),
            ):
                factor = jnp.where(equal[at], 0.0, columns[at]) * inverse
                for b in range(at + 1, SUBLANES):
                    columns[b] = columns[b] - factor * row_of(columns[b], at)
                current_left, current_right = row_of(pivot_left, at), row_of(pivot_right, at)
                pivot_left = pivot_left - factor * current_left
                pivot_right = pivot_right - factor * current_right
                collected = current_right if at == 0 else jnp.where(after[at], current_right, collected)
                pivots = diagonal if at == 0 else jnp.where(after[at], diagonal, pivots)
                inverses.append(inverse)
        finished.append(collected * lax.rsqrt(pivots))
        if group + 1 < len(left):
            solved_left = [row_of(pivot_left, c) * inverses[c] for c in range(SUBLANES)]
            solved_right = [row_of(pivot_right, c) * inverses[c] for c in range(SUBLANES)]
            for h in rest:
                left[h] = left[h] - sum_tree(
                    [rest_columns[h][c] * solved_left[c] for c in range(SUBLANES)]
                )
                right[h] = right[h] - sum_tree(
                    [rest_columns[h][c] * solved_right[c] for c in range(SUBLANES)]
                )
    return jnp.concatenate(finished, 0)


def lane_groups(value):
    return [value[:, i : i + LANES] for i in range(0, value.shape[1], LANES)]


def inverse_factors(grams):
    size = grams[0].shape[0]
    count = size // HALF
    lane = lax.broadcasted_iota(jnp.int32, (HALF, LANES), 1)
    sub = lax.broadcasted_iota(jnp.int32, (HALF, LANES), 0)
    eye = jnp.where(lane % HALF == sub, 1.0, 0.0)
    halves = [lane < HALF, lane >= HALF]
    work = [[gram[HALF * k : HALF * (k + 1)] for k in range(count)] for gram in grams]
    result = [[], []]
    for k in range(count):
        group = k // 2
        mine = [halves[(k ^ m) % 2] for m in range(2)]
        start = jnp.where(mine[0], lane_groups(work[0][k])[group], lane_groups(work[1][k])[group])
        tiles = [slice(i, i + SUBLANES) for i in range(0, HALF, SUBLANES)]
        inverses = eliminate([start[t] for t in tiles], [eye[t] for t in tiles])
        for m in range(2):
            inverse = jnp.where(mine[m], inverses, 0.0)
            parts = lane_groups(work[m][k])
            parts[group] = jnp.where(mine[m], eye, parts[group])
            right_side = jnp.concatenate(parts, 1)
            done = jnp.dot(
                inverse,
                jnp.concatenate([right_side, right_side], 0),
                preferred_element_type=jnp.float32,
                precision=EXACT,
            )
            result[m].append(done)
            for i in range(k + 1, count):
                parts = lane_groups(work[m][i])
                panel = lax.dot_general(
                    parts[group],
                    inverse,
                    (((1,), (1,)), ((), ())),
                    preferred_element_type=jnp.float32,
                    precision=EXACT,
                )
                parts[group] = jnp.where(mine[m], 0.0, parts[group])
                work[m][i] = jnp.concatenate(parts, 1) - jnp.dot(
                    panel, done, preferred_element_type=jnp.float32, precision=EXACT
                )
    place = lax.broadcasted_iota(jnp.int32, (HALF, size), 1) // HALF
    out = []
    for m in range(2):
        rows = [jnp.where((place ^ m) <= k, result[m][k], 0.0) for k in range(count)]
        out.append(jnp.concatenate(rows, 0))
    return out


def fill_sample(masks, where_ref, piece_refs, payload_refs, left_ref, sample_ref, scratch):
    sibling_ref, left_buffer, left_sems = scratch
    levels, local_probes, rank_width = payload_refs[0].shape
    slab_rows = sample_ref.shape[1]
    chunk = slab_rows // left_sems.shape[0]
    copies = []
    for index in range(left_sems.shape[0]):
        begin = pl.multiple_of(where_ref[0] * slab_rows + index * chunk, chunk)
        copies.append(
            pltpu.make_async_copy(
                left_ref.at[:, :, pl.ds(begin, chunk)],
                left_buffer.at[:, :, pl.ds(index * chunk, chunk)],
                left_sems.at[index],
            )
        )
        copies[-1].start()
    spans = []
    for mask, payload_ref in zip(masks, payload_refs):
        start = pl.multiple_of((where_ref[0] ^ mask) * local_probes, local_probes)
        spans.append(pl.ds(start, local_probes))
        for level in range(levels):
            sibling_ref[spans[-1], level * rank_width : (level + 1) * rank_width] = payload_ref[level]
    for mask, piece_ref in zip(masks, piece_refs):
        sample_ref[spans[mask], :] = piece_ref[...]
    for index in range(left_sems.shape[0]):
        copies[index].wait()
        columns = slice(index * chunk, (index + 1) * chunk)
        update = jnp.dot(
            sibling_ref[...],
            left_buffer[:, :, columns].reshape(levels * rank_width, chunk),
            preferred_element_type=jnp.float32,
        )
        sample_ref[:, columns] = (sample_ref[:, columns].astype(jnp.float32) - update).astype(
            jnp.bfloat16
        )


def fill_scratch(all_probes, levels, rank_width, slab_rows):
    return [
        pltpu.VMEM((all_probes, levels * rank_width), jnp.bfloat16),
        pltpu.VMEM((levels, rank_width, slab_rows), jnp.bfloat16),
        pltpu.SemaphoreType.DMA((2,)),
    ]


def exchanged(sample):
    blocks = [sample[i : i + HALF] for i in range(0, sample.shape[0], HALF)]
    return jnp.concatenate([blocks[i ^ 1] for i in range(len(blocks))], 0)


def gram_of(sample, other):
    return lax.dot_general(
        sample, other, (((1,), (1,)), ((), ())), preferred_element_type=jnp.float32
    )


def shifted(gram, shift, flip):
    size = gram.shape[0]
    rows = lax.broadcasted_iota(jnp.int32, (size, size), 0)
    columns = lax.broadcasted_iota(jnp.int32, (size, size), 1)
    return jnp.where(rows == columns ^ flip, gram + shift, gram)


def write_basis(factors, samples, out_ref, buffer_ref, sems):
    slab_rows = out_ref.shape[1]
    piece_rows = slab_rows // len(samples)
    chunk = slab_rows // sems.shape[0]
    copies = []
    terms = []
    for factor in factors:
        high = factor.astype(jnp.bfloat16)
        terms.append((high, (factor - high.astype(jnp.float32)).astype(jnp.bfloat16)))
    for index in range(sems.shape[0]):
        columns = pl.ds(index * chunk, chunk)
        which, within = divmod(index * chunk, piece_rows)
        high, low = terms[which]
        part = samples[which][:, within : within + chunk]
        buffer_ref[:, columns] = jnp.dot(
            high, part, preferred_element_type=jnp.float32
        ) + jnp.dot(low, part, preferred_element_type=jnp.float32)
        copy = pltpu.make_async_copy(
            buffer_ref.at[:, columns], out_ref.at[:, columns], sems.at[index]
        )
        copy.start()
        copies.append(copy)
    for copy in copies:
        copy.wait()


def slab_kernel(masks, pieces, shift, where_ref, *refs):
    count = len(masks)
    piece_refs, payload_refs = refs[:count], refs[count : 2 * count]
    left_ref, out_ref, sample_ref, buffer_ref, sems = refs[2 * count : 2 * count + 5]
    scratch = refs[2 * count + 5 :]
    fill_sample(masks, where_ref, piece_refs, payload_refs, left_ref, sample_ref, scratch)
    piece_rows = sample_ref.shape[1] // pieces
    samples = [sample_ref[:, i * piece_rows : (i + 1) * piece_rows] for i in range(pieces)]
    factors, others = [], []
    for i in range(0, pieces, 2):
        pair = [samples[i], samples[min(i + 1, pieces - 1)]]
        swapped = exchanged(pair[1])
        grams = [shifted(gram_of(pair[0], pair[0]), shift, 0)]
        grams.append(shifted(gram_of(pair[1], swapped), shift, HALF))
        factors += inverse_factors(grams)
        others += [pair[0], swapped]
    write_basis(factors[:pieces], others[:pieces], out_ref, buffer_ref, sems)


def sample_kernel(masks, where_ref, *refs):
    count = len(masks)
    piece_refs, payload_refs = refs[:count], refs[count : 2 * count]
    left_ref, sample_ref, gram_ref = refs[2 * count : 2 * count + 3]
    scratch = refs[2 * count + 3 :]
    fill_sample(masks, where_ref, piece_refs, payload_refs, left_ref, sample_ref, scratch)
    gram_ref[...] = gram_of(sample_ref[...], sample_ref[...])


def basis_kernel(shift, gram_ref, sample_ref, out_ref, buffer_ref, sems):
    gram = shifted(gram_ref[...], shift, 0)
    columns = [gram[:, i : i + HALF] for i in range(0, gram.shape[1], HALF)]
    swapped = jnp.concatenate([columns[i ^ 1] for i in range(len(columns))], 1)
    factors = inverse_factors([gram, swapped])
    write_basis(factors[:1], [sample_ref[...]], out_ref, buffer_ref, sems)


def slab_basis(pieces, payloads, left_factors, slab_rows, masks, where, block_rows):
    levels, rank_width, _ = left_factors.shape
    all_probes = len(masks) * pieces[0].shape[0]
    count = slab_rows // block_rows
    return pl.pallas_call(
        functools.partial(slab_kernel, masks, count, ridge_share * block_rows),
        in_specs=[smem()] + [vmem()] * (2 * len(masks)) + [hbm()],
        out_specs=hbm(),
        out_shape=jax.ShapeDtypeStruct((all_probes, slab_rows), jnp.float32),
        scratch_shapes=[
            pltpu.VMEM((all_probes, slab_rows), jnp.bfloat16),
            pltpu.VMEM((all_probes, slab_rows), jnp.float32),
            pltpu.SemaphoreType.DMA((chunks_of(slab_rows),)),
        ]
        + fill_scratch(all_probes, levels, rank_width, slab_rows),
        compiler_params=pltpu.CompilerParams(vmem_limit_bytes=VMEM_LIMIT),
        name="slab_basis",
    )(where, *pieces, *payloads, left_factors)


def shared_basis(pieces, payloads, left_factors, slab_rows, masks, where, block_rows):
    levels, rank_width, _ = left_factors.shape
    all_probes = len(masks) * pieces[0].shape[0]
    sample, gram = pl.pallas_call(
        functools.partial(sample_kernel, masks),
        in_specs=[smem()] + [vmem()] * (2 * len(masks)) + [hbm()],
        out_specs=[vmem(), vmem()],
        out_shape=[
            jax.ShapeDtypeStruct((all_probes, slab_rows), jnp.bfloat16),
            jax.ShapeDtypeStruct((all_probes, all_probes), jnp.float32),
        ],
        scratch_shapes=fill_scratch(all_probes, levels, rank_width, slab_rows),
        compiler_params=pltpu.CompilerParams(vmem_limit_bytes=VMEM_LIMIT),
        name="sample_gram",
    )(where, *pieces, *payloads, left_factors)
    apart = 1
    while apart * slab_rows < block_rows:
        gram = gram + xor_permute(gram, "probe", apart)
        apart *= 2
    return pl.pallas_call(
        functools.partial(basis_kernel, ridge_share * block_rows),
        in_specs=[vmem(), vmem()],
        out_specs=pl.BlockSpec(memory_space=pl.ANY),
        out_shape=jax.ShapeDtypeStruct((all_probes, slab_rows), jnp.float32),
        scratch_shapes=[
            pltpu.VMEM((all_probes, slab_rows), jnp.float32),
            pltpu.SemaphoreType.DMA((chunks_of(slab_rows),)),
        ],
        compiler_params=pltpu.CompilerParams(vmem_limit_bytes=VMEM_LIMIT),
        name="basis",
    )(gram, sample)


def shards(responses, probes, left_factors, right_factors, level_ranks):
    rows_count = lax.axis_size("rows")
    probe_count = lax.axis_size("probe")
    local_probes, rows_dev = responses.shape
    levels_count, rank_width, _ = left_factors.shape
    slab_rows = rows_dev // probe_count
    block_rows = rows_dev * rows_count // BLOCKS
    place = lax.axis_index("probe")
    where = place.astype(jnp.int32).reshape(1)
    masks = tuple(range(probe_count))

    def piece_for(values, mask):
        return lax.dynamic_slice_in_dim(values, (place ^ mask) * slab_rows, slab_rows, 1)

    far = probe_count // 2
    pieces = {far: xor_permute(piece_for(responses, far), "probe", far)}
    level_ranks = xor_permute(level_ranks, "rows", 1)

    parts = [max(1, 2 ** (l + 1) // rows_count) for l in range(levels_count)]
    wide = [l for l in range(levels_count) if 2 ** (l + 1) <= rows_count]
    running, *local = couplings(probes, right_factors, level_ranks, parts, len(wide))
    later_responses, running = lax.optimization_barrier((responses, running))
    near = xor_permute(running, "rows", 1)
    for mask in sorted(range(1, probe_count), key=lambda mask: -mask.bit_length()):
        if mask != far:
            pieces[mask] = xor_permute(piece_for(later_responses, mask), "probe", mask)
    pieces[0] = piece_for(later_responses, 0)
    sources, terms = [], []
    for slot, level in enumerate(wide):
        flip = rows_count // 2 ** (level + 1)
        if flip == 1:
            sources.append(("slot", slot))
        else:
            total = running[slot] + near[slot]
            sources.append(("terms", len(range(0, flip, 2))))
            terms += [xor_permute(total, "rows", flip ^ low) for low in range(0, flip, 2)]
    narrow_parts = parts[len(wide) :]

    payloads = payloads_of(masks, sources, pieces[far], near, terms, narrow_parts, local, where)
    payloads = [payloads[0]] + [
        xor_permute(payloads[mask], "probe", mask) for mask in range(1, probe_count)
    ]
    ordered = [pieces[mask] for mask in masks]
    work = shared_basis if block_rows > slab_rows else slab_basis
    return work(ordered, payloads, left_factors, slab_rows, masks, where, block_rows)


def solution(mesh):
    return jax.shard_map(
        shards,
        mesh=mesh,
        in_specs=(
            P("probe", "rows"),
            P("probe", "rows"),
            P(None, None, "rows"),
            P(None, None, "rows"),
            P(),
        ),
        out_specs=P(None, ("rows", "probe")),
        check_vma=False,
    )
```

time: 210 us -> 47.3 us (0.23)
  other arithmetic: 112 us -> 0.01 us
  local copies, waits for them, and re-layouts: 37.5 us -> 2.42 us
  matrix products: 22.4 us -> 0 us
  Pallas kernels: 0 us -> 18.6 us
  waiting for transfers between devices: 26.5 us -> 10.1 us
  starting transfers between devices: 9.96 us -> 15.7 us
    another operation x14 -> x0, other arithmetic: 107 us -> none  [the longest x10 66.9 us: shards(): lower_factor = jnp.linalg.cholesky(shifted)]
    all_to_all x1 -> x0, waiting for transfers between devices: 24.3 us -> none  [shards(): lax.all_to_all(sample, 'probe', split_axis=1, concat_axis=0, tiled=True)]
    dot_general x11 -> x0, matrix products: 19.1 us -> none  [the longest x5 10.4 us: shards(): jnp.einsum('kcn,rcn->ckr', right_part, probe_part, preferred_element_type...]
    pallas_call x0 -> x3, Pallas kernels: none -> 18.6 us  [the longest x1 12.4 us: slab_basis(): pl.pallas_call(functools.partial(slab_kernel, masks, count, ridge_share *...]
    unnamed x12 -> x6, local copies, waits for them, and re-layouts: 14.7 us -> 1.38 us
    ppermute x3 -> x11, starting transfers between devices: 4.91 us -> 15.7 us  [xor_permute(): return lax.ppermute(value, axis, pairs)]
    slice x3 -> x0, local copies, waits for them, and re-layouts: 9.98 us -> none  [the longest x1 4.7 us: shards(): right_factors[level_index]]
    ppermute x3 -> x11, waiting for transfers between devices: 2.13 us -> 10.1 us  [xor_permute(): return lax.ppermute(value, axis, pairs)]
  transfers between devices with their start and end apart: 4 -> 11, of which waited for: 2 -> 6; matrix products, arithmetic and copies ran while one was open for 17% -> 2% of each run, Pallas kernels for 0% -> 13%
where the time goes in v2:
time: 47.3 us; the launch traced here: 46.9 us
  Pallas kernels  18.6 us (39%)
  starting transfers between devices  15.7 us (33%)
  waiting for transfers between devices  10.1 us (21%)
  local copies, waits for them, and re-layouts  2.42 us (5%)
    ppermute x11, starting transfers between devices, xor_permute(): return lax.ppermute(value, axis, pairs)  15.7 us
    pallas_call x1, Pallas kernels, slab_basis(): pl.pallas_call(functools.partial(slab_kernel, masks, count, ridge_share *...  12.4 us
    ppermute x11, waiting for transfers between devices, xor_permute(): return lax.ppermute(value, axis, pairs)  10.1 us
    pallas_call x1, Pallas kernels, couplings(): pl.pallas_call(functools.partial(coupling_kernel, tuple(parts), joined, 2...  6.22 us
    unnamed x6, local copies, waits for them, and re-layouts  1.38 us
    dynamic_slice x2, local copies, waits for them, and re-layouts, piece_for(): lax.dynamic_slice_in_dim(values, (place ^ mask) * slab_rows, slab_rows, 1)  1.03 us
  transfers between devices with their start and end apart: 11, of which 6 were waited for; matrix products, arithmetic and copies ran while one was open for 2% of the time, Pallas kernels for 13%

profile of v2, /device:TPU:0, one launch (start us, length us, event | category | flops | bytes accessed | tf_op | source)
XLA Modules:
  0.0 46.9 jit_solution(10118469897869022490)
XLA Ops:
  0.0 0.5 collective-permute-start
  0.5 1.0 %constant_dynamic-slice_fusion.1 = bf16[64,2048]{1,0:T(8,128)(2,1)S(1)} fusion(bf16[64,8192]{1,0:T(8,128)(2,1)} %param.5, s32[]{:T(128)S(6)} %select_n.14), kind=kLoop, calls=%fused_computation.5 | loop fusion | bytes 524292 | tf_op jit(solution)/shard_map/dynamic_slice | solution.py:478
  1.4 3.7 %collective-permute-start.2 = (bf16[64,2048]{1,0:T(8,128)(2,1)S(1)}, bf16[64,2048]{1,0:T(8,128)(2,1)S(1)}, u32[]{:S(2)}, u32[]{:S(2)}) collective-permute-start(bf16[64,2048]{1,0:T(8,128)(2,1)S(1)} %constant_dynamic-slice_fusion.1), channel_id=1, source_target_pairs={{0,2},{1,3},{2,0},{3,1},{4,6},{5,7},{6,4},{7,5},{8,10},{9,11},{10,... | collective-permute-start | bytes 786440 | tf_op jit(solution)/shard_map/ppermute | solution.py:24
  5.1 0.0 collective-permute-done.ranks_ref
  5.1 1.4 %copy-done.1 = bf16[64,8192]{1,0:T(8,128)(2,1)S(1)} copy-done((bf16[64,8192]{1,0:T(8,128)(2,1)S(1)}, bf16[64,8192]{1,0:T(8,128)(2,1)}, u32[]{:S(2)}) %copy-start.1) | copy-done | bytes 1048600
  6.5 6.2 %couplings.1 = (f32[3,64,128]{2,1,0:T(8,128)S(1)}, bf16[2,64,128]{2,1,0:T(8,128)(2,1)S(1)}, bf16[4,64,128]{2,1,0:T(8,128)(2,1)S(1)}) custom-call(s32[5]{0:T(128)S(1)} %collective-permute-done.ranks_ref, bf16[64,8192]{1,0:T(8,128)(2,1)S(1)} %copy-done.1, bf16[5,128,8192]{2,1,0:T(8,128)(2,1)} %right_ref.1), custom_call_target="tpu_custom_call" | custom-call | flops 1 | bytes 1 | tf_op jit(solution)/shard_map/couplings/pallas_call | solution.py:113
  12.7 0.3 collective-permute-start.4
  13.0 0.1 constant_dynamic-slice_fusion
  13.1 1.4 %collective-permute-start.3 = (bf16[64,2048]{1,0:T(8,128)(2,1)S(1)}, bf16[64,2048]{1,0:T(8,128)(2,1)S(1)}, u32[]{:S(2)}, u32[]{:S(2)}) collective-permute-start(bf16[64,2048]{1,0:T(8,128)(2,1)S(1)} %get-tuple-element.23), channel_id=1, source_target_pairs={{0,3},{1,2},{2,1},{3,0},{4,7},{5,6},{6,5},{7,4},{8,11},{9,10},{10,... | collective-permute-start | bytes 786440 | tf_op jit(solution)/shard_map/ppermute | solution.py:24
  14.5 0.3 collective-permute-start.1
  14.8 0.0 collective-permute-done.4.near_ref
  14.8 1.6 %collective-permute-start.7 = (f32[64,128]{1,0:T(8,128)S(1)}, f32[64,128]{1,0:T(8,128)S(1)}, u32[]{:S(2)}, u32[]{:S(2)}) collective-permute-start(f32[64,128]{1,0:T(8,128)S(1)} %get-tuple-element.26), channel_id=1, source_target_pairs={{0,8},{4,12},{8,0},{12,4},{16,24},{20,28},{24,16},{28,20},{1,9},{5... | collective-permute-start | bytes 98312 | tf_op jit(solution)/shard_map/ppermute | solution.py:24
  16.3 1.5 %collective-permute-start.6 = (f32[64,128]{1,0:T(8,128)S(1)}, f32[64,128]{1,0:T(8,128)S(1)}, u32[]{:S(2)}, u32[]{:S(2)}) collective-permute-start(f32[64,128]{1,0:T(8,128)S(1)} %get-tuple-element.27), channel_id=1, source_target_pairs={{0,24},{4,28},{8,16},{12,20},{16,8},{20,12},{24,0},{28,4},{1,25},{... | collective-permute-start | bytes 98312 | tf_op jit(solution)/shard_map/ppermute | solution.py:24
  17.8 0.9 %collective-permute-done.7.refs_2_ = f32[64,128]{1,0:T(8,128)S(1)} collective-permute-done((f32[64,128]{1,0:T(8,128)S(1)}, f32[64,128]{1,0:T(8,128)S(1)}, u32[]{:S(2)}, u32[]{:S(2)}) %collective-permute-start.7) | collective-permute-done | bytes 32800 | tf_op jit(solution)/shard_map/ppermute | solution.py:24
  18.8 1.7 %collective-permute-start.5 = (f32[64,128]{1,0:T(8,128)S(1)}, f32[64,128]{1,0:T(8,128)S(1)}, u32[]{:S(2)}, u32[]{:S(2)}) collective-permute-start(f32[64,128]{1,0:T(8,128)S(1)} %get-tuple-element.27), channel_id=1, source_target_pairs={{0,16},{4,20},{8,24},{12,28},{16,0},{20,4},{24,8},{28,12},{1,17},{... | collective-permute-start | bytes 98312 | tf_op jit(solution)/shard_map/ppermute | solution.py:24
  20.4 0.8 %collective-permute-done.6.refs_1_ = f32[64,128]{1,0:T(8,128)S(1)} collective-permute-done((f32[64,128]{1,0:T(8,128)S(1)}, f32[64,128]{1,0:T(8,128)S(1)}, u32[]{:S(2)}, u32[]{:S(2)}) %collective-permute-start.6) | collective-permute-done | bytes 32800 | tf_op jit(solution)/shard_map/ppermute | solution.py:24
  21.2 1.5 %collective-permute-done.5.refs_0_ = f32[64,128]{1,0:T(8,128)S(1)} collective-permute-done((f32[64,128]{1,0:T(8,128)S(1)}, f32[64,128]{1,0:T(8,128)S(1)}, u32[]{:S(2)}, u32[]{:S(2)}) %collective-permute-start.5) | collective-permute-done | bytes 32800 | tf_op jit(solution)/shard_map/ppermute | solution.py:24
  22.7 1.8 %collective-permute-start.8 = (bf16[5,64,128]{2,1,0:T(8,128)(2,1)S(1)}, bf16[5,64,128]{2,1,0:T(8,128)(2,1)S(1)}, u32[]{:S(2)}, u32[]{:S(2)}) collective-permute-start(bf16[5,64,128]{2,1,0:T(8,128)(2,1)S(1)} %get-tuple-element.20), channel_id=1, source_target_pairs={{0,1},{1,0},{2,3},{3,2},{4,5},{5,4},{6,7},{7,6},{8,9},{9,8},{10,11... | collective-permute-start | bytes 245768 | tf_op jit(solution)/shard_map/ppermute | solution.py:24
  24.5 3.1 %collective-permute-start.9 = (bf16[5,64,128]{2,1,0:T(8,128)(2,1)S(1)}, bf16[5,64,128]{2,1,0:T(8,128)(2,1)S(1)}, u32[]{:S(2)}, u32[]{:S(2)}) collective-permute-start(bf16[5,64,128]{2,1,0:T(8,128)(2,1)S(1)} %get-tuple-element.21), channel_id=1, source_target_pairs={{0,2},{1,3},{2,0},{3,1},{4,6},{5,7},{6,4},{7,5},{8,10},{9,11},{10,... | collective-permute-start | bytes 245768 | tf_op jit(solution)/shard_map/ppermute | solution.py:24
  27.6 3.0 %collective-permute-done.1.refs_1_ = bf16[64,2048]{1,0:T(8,128)(2,1)S(1)} collective-permute-done((bf16[64,2048]{1,0:T(8,128)(2,1)S(1)}, bf16[64,2048]{1,0:T(8,128)(2,1)S(1)}, u32[]{:S(2)}, u32[]{:S(2)}) %collective-permute-start.1) | collective-permute-done | bytes 262176 | tf_op jit(solution)/shard_map/ppermute | solution.py:24
  30.6 2.1 %collective-permute-done.8.refs_5_ = bf16[5,64,128]{2,1,0:T(8,128)(2,1)S(1)} collective-permute-done((bf16[5,64,128]{2,1,0:T(8,128)(2,1)S(1)}, bf16[5,64,128]{2,1,0:T(8,128)(2,1)S(1)}, u32[]{:S(2)}, u32[]{:S(2)}) %collective-permute-start.8) | collective-permute-done | bytes 81952 | tf_op jit(solution)/shard_map/ppermute | solution.py:24
  32.7 1.8 %collective-permute-done.9.refs_6_ = bf16[5,64,128]{2,1,0:T(8,128)(2,1)S(1)} collective-permute-done((bf16[5,64,128]{2,1,0:T(8,128)(2,1)S(1)}, bf16[5,64,128]{2,1,0:T(8,128)(2,1)S(1)}, u32[]{:S(2)}, u32[]{:S(2)}) %collective-permute-start.9) | collective-permute-done | bytes 81952 | tf_op jit(solution)/shard_map/ppermute | solution.py:24
  34.5 0.0 collective-permute-done.10.refs_7_
  34.5 12.4 %slab_basis.1 = f32[256,2048]{1,0:T(8,128)} custom-call(s32[1]{0:T(128)} %bitcast.where_ref, bf16[64,2048]{1,0:T(8,128)(2,1)S(1)} %get-tuple-element.25.refs_0_, bf16[64,2048]{1,0:T(8,128)(2,1)S(1)} %collective-permute-done.1.refs_1_, bf16[64,2048]{1,0:T(8,128)(2,1)S(1)} %collective-permute-done.2.early_ref.refs_2_, ...), custom_call_target="tpu_custom_call" | custom-call | tf_op jit(solution)/shard_map/slab_basis/pallas_call | solution.py:417
  (10 shorter events, 0.1 us)
Async XLA Ops:
  0.0 5.1 %collective-permute-start = (s32[5]{0:T(128)}, s32[5]{0:T(128)S(1)}, u32[]{:S(2)}, u32[]{:S(2)}) collective-permute-start(s32[5]{0:T(128)} %param.9), channel_id=1, source_target_pairs={{0,4},{4,0},{8,12},{12,8},{16,20},{20,16},{24,28},{28,24},{1,5},{5... | collective-permute-start | bytes 68 | tf_op jit(solution)/shard_map/ppermute | solution.py:24
  1.4 21.3 %collective-permute-start.2 = (bf16[64,2048]{1,0:T(8,128)(2,1)S(1)}, bf16[64,2048]{1,0:T(8,128)(2,1)S(1)}, u32[]{:S(2)}, u32[]{:S(2)}) collective-permute-start(bf16[64,2048]{1,0:T(8,128)(2,1)S(1)} %constant_dynamic-slice_fusion.1), channel_id=1, source_target_pairs={{0,2},{1,3},{2,0},{3,1},{4,6},{5,7},{6,4},{7,5},{8,10},{9,11},{10,... | collective-permute-start | bytes 786440 | tf_op jit(solution)/shard_map/ppermute | solution.py:24
  5.1 29.5 %copy-start = (bf16[5,128,8192]{2,1,0:T(8,128)(2,1)S(1)}, bf16[5,128,8192]{2,1,0:T(8,128)(2,1)}, u32[]{:S(2)}) copy-start(bf16[5,128,8192]{2,1,0:T(8,128)(2,1)} %refs_8_.1) | copy-start | bytes 31457284
  5.1 1.4 %copy-start.1 = (bf16[64,8192]{1,0:T(8,128)(2,1)S(1)}, bf16[64,8192]{1,0:T(8,128)(2,1)}, u32[]{:S(2)}) copy-start(bf16[64,8192]{1,0:T(8,128)(2,1)} %probes_ref.1) | copy-start | bytes 3145732
  6.5 6.5 %copy-start.2 = (bf16[64,8192]{1,0:T(8,128)(2,1)S(1)}, bf16[64,8192]{1,0:T(8,128)(2,1)}, u32[]{:S(2)}) copy-start(bf16[64,8192]{1,0:T(8,128)(2,1)} %param.5) | copy-start | bytes 3145732
  12.7 2.1 %collective-permute-start.4 = (f32[3,64,128]{2,1,0:T(8,128)S(1)}, f32[3,64,128]{2,1,0:T(8,128)S(1)}, u32[]{:S(2)}, u32[]{:S(2)}) collective-permute-start(f32[3,64,128]{2,1,0:T(8,128)S(1)} %get-tuple-element.16), channel_id=1, source_target_pairs={{0,4},{4,0},{8,12},{12,8},{16,20},{20,16},{24,28},{28,24},{1,5},{5... | collective-permute-start | bytes 294920 | tf_op jit(solution)/shard_map/ppermute | solution.py:24
  13.1 14.6 %collective-permute-start.3 = (bf16[64,2048]{1,0:T(8,128)(2,1)S(1)}, bf16[64,2048]{1,0:T(8,128)(2,1)S(1)}, u32[]{:S(2)}, u32[]{:S(2)}) collective-permute-start(bf16[64,2048]{1,0:T(8,128)(2,1)S(1)} %get-tuple-element.23), channel_id=1, source_target_pairs={{0,3},{1,2},{2,1},{3,0},{4,7},{5,6},{6,5},{7,4},{8,11},{9,10},{10,... | collective-permute-start | bytes 786440 | tf_op jit(solution)/shard_map/ppermute | solution.py:24
  14.5 16.1 %collective-permute-start.1 = (bf16[64,2048]{1,0:T(8,128)(2,1)S(1)}, bf16[64,2048]{1,0:T(8,128)(2,1)S(1)}, u32[]{:S(2)}, u32[]{:S(2)}) collective-permute-start(bf16[64,2048]{1,0:T(8,128)(2,1)S(1)} %get-tuple-element.24), channel_id=1, source_target_pairs={{0,1},{1,0},{2,3},{3,2},{4,5},{5,4},{6,7},{7,6},{8,9},{9,8},{10,11... | collective-permute-start | bytes 786440 | tf_op jit(solution)/shard_map/ppermute | solution.py:24
  14.8 4.0 %collective-permute-start.7 = (f32[64,128]{1,0:T(8,128)S(1)}, f32[64,128]{1,0:T(8,128)S(1)}, u32[]{:S(2)}, u32[]{:S(2)}) collective-permute-start(f32[64,128]{1,0:T(8,128)S(1)} %get-tuple-element.26), channel_id=1, source_target_pairs={{0,8},{4,12},{8,0},{12,4},{16,24},{20,28},{24,16},{28,20},{1,9},{5... | collective-permute-start | bytes 98312 | tf_op jit(solution)/shard_map/ppermute | solution.py:24
  16.3 4.9 %collective-permute-start.6 = (f32[64,128]{1,0:T(8,128)S(1)}, f32[64,128]{1,0:T(8,128)S(1)}, u32[]{:S(2)}, u32[]{:S(2)}) collective-permute-start(f32[64,128]{1,0:T(8,128)S(1)} %get-tuple-element.27), channel_id=1, source_target_pairs={{0,24},{4,28},{8,16},{12,20},{16,8},{20,12},{24,0},{28,4},{1,25},{... | collective-permute-start | bytes 98312 | tf_op jit(solution)/shard_map/ppermute | solution.py:24
  18.8 3.9 %collective-permute-start.5 = (f32[64,128]{1,0:T(8,128)S(1)}, f32[64,128]{1,0:T(8,128)S(1)}, u32[]{:S(2)}, u32[]{:S(2)}) collective-permute-start(f32[64,128]{1,0:T(8,128)S(1)} %get-tuple-element.27), channel_id=1, source_target_pairs={{0,16},{4,20},{8,24},{12,28},{16,0},{20,4},{24,8},{28,12},{1,17},{... | collective-permute-start | bytes 98312 | tf_op jit(solution)/shard_map/ppermute | solution.py:24
  22.7 9.9 %collective-permute-start.8 = (bf16[5,64,128]{2,1,0:T(8,128)(2,1)S(1)}, bf16[5,64,128]{2,1,0:T(8,128)(2,1)S(1)}, u32[]{:S(2)}, u32[]{:S(2)}) collective-permute-start(bf16[5,64,128]{2,1,0:T(8,128)(2,1)S(1)} %get-tuple-element.20), channel_id=1, source_target_pairs={{0,1},{1,0},{2,3},{3,2},{4,5},{5,4},{6,7},{7,6},{8,9},{9,8},{10,11... | collective-permute-start | bytes 245768 | tf_op jit(solution)/shard_map/ppermute | solution.py:24
  24.5 10.0 %collective-permute-start.9 = (bf16[5,64,128]{2,1,0:T(8,128)(2,1)S(1)}, bf16[5,64,128]{2,1,0:T(8,128)(2,1)S(1)}, u32[]{:S(2)}, u32[]{:S(2)}) collective-permute-start(bf16[5,64,128]{2,1,0:T(8,128)(2,1)S(1)} %get-tuple-element.21), channel_id=1, source_target_pairs={{0,2},{1,3},{2,0},{3,1},{4,6},{5,7},{6,4},{7,5},{8,10},{9,11},{10,... | collective-permute-start | bytes 245768 | tf_op jit(solution)/shard_map/ppermute | solution.py:24
  27.6 6.9 %collective-permute-start.10 = (bf16[5,64,128]{2,1,0:T(8,128)(2,1)S(1)}, bf16[5,64,128]{2,1,0:T(8,128)(2,1)S(1)}, u32[]{:S(2)}, u32[]{:S(2)}) collective-permute-start(bf16[5,64,128]{2,1,0:T(8,128)(2,1)S(1)} %get-tuple-element.22), channel_id=1, source_target_pairs={{0,3},{1,2},{2,1},{3,0},{4,7},{5,6},{6,5},{7,4},{8,11},{9,10},{10,... | collective-permute-start | bytes 245768 | tf_op jit(solution)/shard_map/ppermute | solution.py:24

commit v3 on v2

v3 whole, which is shorter than its diff:
```python
import functools

import jax
import jax.numpy as jnp
from jax import lax
from jax.experimental import pallas as pl
from jax.experimental.pallas import tpu as pltpu
from jax.sharding import PartitionSpec as P

BLOCKS = 64

ridge_share = 0.05

LANES = 128
SUBLANES = 8
EXACT = lax.Precision.HIGHEST
VMEM_LIMIT = 24 * 2**20
STREAM_VMEM = 48 * 2**20
CHEAP = pl.CostEstimate(flops=1, bytes_accessed=1, transcendentals=0)


def xor_permute(value, axis, mask):
    pairs = [(source, source ^ mask) for source in range(lax.axis_size(axis))]
    return lax.ppermute(value, axis, pairs)


def smem():
    return pl.BlockSpec(memory_space=pltpu.SMEM)


def vmem():
    return pl.BlockSpec(memory_space=pltpu.VMEM)


def hbm():
    return pl.BlockSpec(memory_space=pltpu.HBM)


def chunks_of(slab_rows):
    return max(1, slab_rows // 512)


RANK_STEP = 32


def coupling_kernel(parts, joined, ahead, ranks_ref, probes_ref, right_ref, *refs):
    out_refs = refs[:-5]
    probe_buffer, right_buffer, total_ref, probe_sems, right_sems = refs[-5:]
    levels, rank_width, rows_dev = right_ref.shape
    local_probes = probe_buffer.shape[0]
    chunks = probe_sems.shape[0]
    chunk = rows_dev // chunks
    counts, starts = [], []
    start = 0
    for level in range(levels):
        steps = (jnp.clip(ranks_ref[level], 1, rank_width) + RANK_STEP - 1) // RANK_STEP
        counts.append(pl.multiple_of(steps * RANK_STEP, RANK_STEP))
        starts.append(pl.multiple_of(start, RANK_STEP))
        start = start + counts[-1]

    def columns_of(index):
        return pl.ds(pl.multiple_of(index * chunk, chunk), chunk)

    def copies(index):
        columns = columns_of(index)
        found = [
            pltpu.make_async_copy(
                probes_ref.at[:, columns], probe_buffer.at[:, columns], probe_sems.at[index]
            )
        ]
        for level in range(levels):
            found.append(
                pltpu.make_async_copy(
                    right_ref.at[level, pl.ds(0, counts[level]), columns],
                    right_buffer.at[pl.ds(starts[level], counts[level]), columns],
                    right_sems.at[index, level],
                )
            )
        return found

    for index in range(min(ahead, chunks)):
        for copy in copies(index):
            copy.start()

    def multiply(index, rows):
        columns = columns_of(index)
        total_ref[index, :rows] = lax.dot_general(
            right_buffer[:rows, columns],
            probe_buffer[:, columns],
            (((1,), (1,)), ((), ())),
            preferred_element_type=jnp.float32,
        )

    def add_chunk(index, carry):
        for copy in copies(index):
            copy.wait()

        @pl.when(index + ahead < chunks)
        def _():
            for copy in copies(index + ahead):
                copy.start()

        lower = 0
        for upper in [levels * rank_width * part // 10 for part in (6, 8, 10)]:
            @pl.when((start > lower) & (start <= upper))
            def _():
                multiply(index, upper)

            lower = upper
        return carry

    lax.fori_loop(0, chunks, add_chunk, 0)
    rank = lax.broadcasted_iota(jnp.int32, (rank_width, local_probes), 0)
    for level in range(levels):
        rows = pl.ds(starts[level], rank_width)
        kept = rank < ranks_ref[level]
        per_part = chunks // parts[level]
        for part in range(parts[level]):
            terms = [total_ref[part * per_part + i, rows] for i in range(per_part)]
            value = jnp.where(kept, sum_tree(terms), 0.0).T
            if level < joined:
                out_refs[0][level] = value
            else:
                out_refs[level - joined + 1][part] = value.astype(jnp.bfloat16)


def couplings(probes, right_factors, level_ranks, parts, joined):
    local_probes, rows_dev = probes.shape
    levels, rank_width, _ = right_factors.shape
    chunks = max(4, *parts)
    shapes = [jax.ShapeDtypeStruct((joined, local_probes, rank_width), jnp.float32)] + [
        jax.ShapeDtypeStruct((count, local_probes, rank_width), jnp.bfloat16)
        for count in parts[joined:]
    ]
    return pl.pallas_call(
        functools.partial(coupling_kernel, tuple(parts), joined, 3),
        in_specs=[smem(), hbm(), hbm()],
        out_specs=[vmem()] * len(shapes),
        out_shape=shapes,
        scratch_shapes=[
            pltpu.VMEM((local_probes, rows_dev), probes.dtype),
            pltpu.VMEM((levels * rank_width, rows_dev), right_factors.dtype),
            pltpu.VMEM((chunks, (levels + 1) * rank_width, local_probes), jnp.float32),
            pltpu.SemaphoreType.DMA((chunks,)),
            pltpu.SemaphoreType.DMA((chunks, levels)),
        ],
        compiler_params=pltpu.CompilerParams(vmem_limit_bytes=STREAM_VMEM),
        cost_estimate=CHEAP,
        name="couplings",
    )(level_ranks, probes, right_factors)


def left_kernel(where_ref, early_ref, left_ref, out_ref, sem):
    slab_rows = out_ref.shape[2]
    begin = pl.multiple_of(where_ref[0] * slab_rows, slab_rows)
    copy = pltpu.make_async_copy(left_ref.at[:, :, pl.ds(begin, slab_rows)], out_ref, sem)
    copy.start()
    copy.wait()


def left_of_slab(left_factors, early, where, slab_rows):
    levels, rank_width, _ = left_factors.shape
    return pl.pallas_call(
        left_kernel,
        in_specs=[smem(), hbm(), hbm()],
        out_specs=vmem(),
        out_shape=jax.ShapeDtypeStruct((levels, rank_width, slab_rows), left_factors.dtype),
        scratch_shapes=[pltpu.SemaphoreType.DMA],
        compiler_params=pltpu.CompilerParams(vmem_limit_bytes=STREAM_VMEM),
        cost_estimate=CHEAP,
        name="left_of_slab",
    )(where, early, left_factors)


def pack_kernel(masks, sources, narrow_parts, where_ref, near_ref, *refs):
    out_refs = refs[-len(masks) :]
    term_refs = list(refs[: -len(masks)])
    level = 0
    for kind, value in sources:
        if kind == "slot":
            sibling = near_ref[value]
        else:
            terms, term_refs = term_refs[:value], term_refs[value:]
            sibling = sum_tree([term[...] for term in terms])
        sibling = sibling.astype(jnp.bfloat16)
        for out_ref in out_refs:
            out_ref[level] = sibling
        level += 1
    for parts, values_ref in zip(narrow_parts, term_refs):
        for mask, out_ref in zip(masks, out_refs):
            out_ref[level] = values_ref[((where_ref[0] ^ mask) * parts // len(masks)) ^ 1]
        level += 1


def payloads_of(masks, sources, near, terms, narrow_parts, local, where):
    _, local_probes, rank_width = near.shape
    shape = (len(sources) + len(local), local_probes, rank_width)
    return pl.pallas_call(
        functools.partial(pack_kernel, masks, tuple(sources), tuple(narrow_parts)),
        in_specs=[smem()] + [vmem()] * (1 + len(terms) + len(local)),
        out_specs=[vmem()] * len(masks),
        out_shape=[jax.ShapeDtypeStruct(shape, jnp.bfloat16)] * len(masks),
        compiler_params=pltpu.CompilerParams(vmem_limit_bytes=VMEM_LIMIT),
        cost_estimate=CHEAP,
        name="payloads",
    )(where, near, *terms, *local)


HALF = LANES // 2


def row_of(value, index):
    return jnp.broadcast_to(value[index : index + 1, :], value.shape)


def column_of(value, index, half_start):
    return jnp.take_along_axis(value, half_start + index, axis=1)


def sum_tree(terms):
    while len(terms) > 1:
        terms = [
            terms[i] + terms[i + 1] if i + 1 < len(terms) else terms[i]
            for i in range(0, len(terms), 2)
        ]
    return terms[0]


def eliminate(left, right):
    row_iota = lax.broadcasted_iota(jnp.int32, (SUBLANES, LANES), 0)
    half_start = lax.broadcasted_iota(jnp.int32, (SUBLANES, LANES), 1) // HALF * HALF
    equal = [row_iota == a for a in range(SUBLANES)]
    after = [row_iota >= a for a in range(SUBLANES)]
    left, right = list(left), list(right)
    finished = []
    for group in range(len(left)):
        base = SUBLANES * group
        pivot_left, pivot_right = left[group], right[group]
        columns = [column_of(pivot_left, base + b, half_start) for b in range(SUBLANES)]
        rest = range(group + 1, len(left))
        rest_columns = {
            h: [column_of(left[h], base + c, half_start) for c in range(SUBLANES)] for h in rest
        }
        inverses = []
        collected = pivots = None
        for a in range(0, SUBLANES, 2):
            first = row_of(columns[a], a)
            cross = row_of(columns[a + 1], a)
            determinant = first * row_of(columns[a + 1], a + 1) - cross * cross
            inverse_first = 1.0 / first
            inverse_second = first * (1.0 / determinant)
            second = determinant * inverse_first
            for at, diagonal, inverse in (
                (a, first, inverse_first),
                (a + 1, second, inverse_second),
            ):
                factor = jnp.where(equal[at], 0.0, columns[at]) * inverse
                for b in range(at + 1, SUBLANES):
                    columns[b] = columns[b] - factor * row_of(columns[b], at)
                current_left, current_right = row_of(pivot_left, at), row_of(pivot_right, at)
                pivot_left = pivot_left - factor * current_left
                pivot_right = pivot_right - factor * current_right
                collected = current_right if at == 0 else jnp.where(after[at], current_right, collected)
                pivots = diagonal if at == 0 else jnp.where(after[at], diagonal, pivots)
                inverses.append(inverse)
        finished.append(collected * lax.rsqrt(pivots))
        if group + 1 < len(left):
            solved_left = [row_of(pivot_left, c) * inverses[c] for c in range(SUBLANES)]
            solved_right = [row_of(pivot_right, c) * inverses[c] for c in range(SUBLANES)]
            for h in rest:
                left[h] = left[h] - sum_tree(
                    [rest_columns[h][c] * solved_left[c] for c in range(SUBLANES)]
                )
                right[h] = right[h] - sum_tree(
                    [rest_columns[h][c] * solved_right[c] for c in range(SUBLANES)]
                )
    return jnp.concatenate(finished, 0)


def lane_groups(value):
    return [value[:, i : i + LANES] for i in range(0, value.shape[1], LANES)]


def inverse_factors(grams, take_rows):
    size = grams[0].shape[0]
    count = size // HALF
    lane = lax.broadcasted_iota(jnp.int32, (HALF, LANES), 1)
    sub = lax.broadcasted_iota(jnp.int32, (HALF, LANES), 0)
    place = lax.broadcasted_iota(jnp.int32, (HALF, size), 1) // HALF
    eye = jnp.where(lane % HALF == sub, 1.0, 0.0)
    halves = [lane < HALF, lane >= HALF]
    tiles = [slice(i, i + SUBLANES) for i in range(0, HALF, SUBLANES)]
    work = [
        [lane_groups(gram[HALF * k : HALF * (k + 1)]) for k in range(count)] for gram in grams
    ]
    waiting = []
    for k in range(count):
        group = k // 2
        mine = [halves[(k ^ m) % 2] for m in range(2)]
        start = jnp.where(mine[0], work[0][k][group], work[1][k][group])
        inverses = eliminate([start[t] for t in tiles], [eye[t] for t in tiles])
        for task in waiting:
            task()
        waiting = []
        rows = [None, None]

        def panel_of(m, first, last, inverse, group=group):
            return lax.dot_general(
                jnp.concatenate([work[m][i][group] for i in range(first, last)], 0),
                inverse,
                (((1,), (1,)), ((), ())),
                preferred_element_type=jnp.float32,
                precision=EXACT,
            )

        def subtract(m, i, g, term, group=group, mine=mine):
            old = jnp.where(mine[m], 0.0, work[m][i][g]) if g == group else work[m][i][g]
            work[m][i][g] = old - term

        def rest_of(m, panel, inverse, done, k=k, panel_of=panel_of, subtract=subtract):
            def task():
                full = panel
                if k + 2 < count:
                    full = jnp.concatenate([panel, panel_of(m, k + 2, count, inverse)], 0)
                terms = jnp.dot(full, done, preferred_element_type=jnp.float32, precision=EXACT)
                for i in range(k + 1, count):
                    block = lane_groups(terms[HALF * (i - k - 1) : HALF * (i - k)])
                    for g, term in enumerate(block):
                        if (i, g) != (k + 1, (k + 1) // 2):
                            subtract(m, i, g, term)

            return task

        for m in range(2):
            inverse = jnp.where(mine[m], inverses, 0.0)
            parts = list(work[m][k])
            parts[group] = jnp.where(mine[m], eye, parts[group])
            right_side = jnp.concatenate(parts, 1)
            done = jnp.dot(
                inverse,
                jnp.concatenate([right_side, right_side], 0),
                preferred_element_type=jnp.float32,
                precision=EXACT,
            )
            rows[m] = jnp.where((place ^ m) <= k, done, 0.0)
            if k + 1 < count:
                needed = (k + 1) // 2
                panel = panel_of(m, k + 1, k + 2, inverse)
                part = done[:, needed * LANES : (needed + 1) * LANES]
                subtract(
                    m,
                    k + 1,
                    needed,
                    jnp.dot(panel, part, preferred_element_type=jnp.float32, precision=EXACT),
                )
                waiting.append(rest_of(m, panel, inverse, done))
        waiting.append(lambda k=k, rows=rows: take_rows(k, rows))
    for task in waiting:
        task()


def fill_sample(masks, where_ref, piece_refs, payload_refs, left_ref, sample_ref, sibling_ref):
    levels, local_probes, rank_width = payload_refs[0].shape
    slab_rows = sample_ref.shape[1]
    spans = []
    for mask, payload_ref in zip(masks, payload_refs):
        start = pl.multiple_of((where_ref[0] ^ mask) * local_probes, local_probes)
        spans.append(pl.ds(start, local_probes))
        for level in range(levels):
            sibling_ref[spans[-1], level * rank_width : (level + 1) * rank_width] = payload_ref[level]
    for mask, piece_ref in zip(masks, piece_refs):
        sample_ref[spans[mask], :] = piece_ref[...]
    chunk = slab_rows // chunks_of(slab_rows)
    for begin in range(0, slab_rows, chunk):
        columns = slice(begin, begin + chunk)
        update = jnp.dot(
            sibling_ref[...],
            left_ref[:, :, columns].reshape(levels * rank_width, chunk),
            preferred_element_type=jnp.float32,
        )
        sample_ref[:, columns] = (sample_ref[:, columns].astype(jnp.float32) - update).astype(
            jnp.bfloat16
        )


def exchanged(sample):
    blocks = [sample[i : i + HALF] for i in range(0, sample.shape[0], HALF)]
    return jnp.concatenate([blocks[i ^ 1] for i in range(len(blocks))], 0)


def gram_of(sample, other):
    return lax.dot_general(
        sample, other, (((1,), (1,)), ((), ())), preferred_element_type=jnp.float32
    )


def shifted(gram, shift, flip):
    size = gram.shape[0]
    rows = lax.broadcasted_iota(jnp.int32, (size, size), 0)
    columns = lax.broadcasted_iota(jnp.int32, (size, size), 1)
    return jnp.where(rows == columns ^ flip, gram + shift, gram)


def write_basis(grams, samples, out_ref, buffer_ref, sems):
    piece_rows = samples[0].shape[1]
    count = grams[0].shape[0] // HALF
    copies, held = [], []

    def take_rows(k, factors):
        held.append(factors)
        if k < count - 2:
            return
        height = HALF * len(held)
        at = slice(HALF * (k + 1) - height, HALF * (k + 1))
        for which, sample in enumerate(samples):
            factor = jnp.concatenate([factors[which] for factors in held], 0)
            high = factor.astype(jnp.bfloat16)
            low = (factor - high.astype(jnp.float32)).astype(jnp.bfloat16)
            both = jnp.dot(
                jnp.concatenate([high, low], 0), sample, preferred_element_type=jnp.float32
            )
            columns = slice(which * piece_rows, (which + 1) * piece_rows)
            buffer_ref[at, columns] = both[:height] + both[height:]
        held.clear()
        copies.append(
            pltpu.make_async_copy(buffer_ref.at[at], out_ref.at[at], sems.at[len(copies)])
        )
        copies[-1].start()

    inverse_factors(grams, take_rows)
    for copy in copies:
        copy.wait()


def slab_kernel(masks, pieces, shift, where_ref, *refs):
    count = len(masks)
    piece_refs, payload_refs = refs[:count], refs[count : 2 * count]
    left_ref, out_ref, sample_ref, buffer_ref, sems = refs[2 * count : 2 * count + 5]
    sibling_ref = refs[2 * count + 5]
    fill_sample(masks, where_ref, piece_refs, payload_refs, left_ref, sample_ref, sibling_ref)
    piece_rows = sample_ref.shape[1] // pieces
    for i in range(0, pieces, 2):
        pair = [
            sample_ref[:, j * piece_rows : (j + 1) * piece_rows]
            for j in range(i, min(i + 2, pieces))
        ]
        swapped = exchanged(pair[-1])
        grams = [
            shifted(gram_of(pair[0], pair[0]), shift, 0),
            shifted(gram_of(pair[-1], swapped), shift, HALF),
        ]
        columns = pl.ds(i * piece_rows, len(pair) * piece_rows)
        write_basis(
            grams,
            [pair[0], swapped][: len(pair)],
            out_ref.at[:, columns],
            buffer_ref.at[:, columns],
            sems,
        )


def sample_kernel(masks, where_ref, *refs):
    count = len(masks)
    piece_refs, payload_refs = refs[:count], refs[count : 2 * count]
    left_ref, sample_ref, gram_ref = refs[2 * count : 2 * count + 3]
    sibling_ref = refs[2 * count + 3]
    fill_sample(masks, where_ref, piece_refs, payload_refs, left_ref, sample_ref, sibling_ref)
    gram_ref[...] = gram_of(sample_ref[...], sample_ref[...])


def basis_kernel(shift, gram_ref, sample_ref, out_ref, buffer_ref, sems):
    gram = shifted(gram_ref[...], shift, 0)
    columns = [gram[:, i : i + HALF] for i in range(0, gram.shape[1], HALF)]
    swapped = jnp.concatenate([columns[i ^ 1] for i in range(len(columns))], 1)
    write_basis([gram, swapped], [sample_ref[...]], out_ref, buffer_ref, sems)


def slab_basis(pieces, payloads, left_slab, masks, where, block_rows):
    levels, rank_width, slab_rows = left_slab.shape
    all_probes = len(masks) * pieces[0].shape[0]
    count = slab_rows // block_rows
    return pl.pallas_call(
        functools.partial(slab_kernel, masks, count, ridge_share * block_rows),
        in_specs=[smem()] + [vmem()] * (2 * len(masks) + 1),
        out_specs=hbm(),
        out_shape=jax.ShapeDtypeStruct((all_probes, slab_rows), jnp.float32),
        scratch_shapes=[
            pltpu.VMEM((all_probes, slab_rows), jnp.bfloat16),
            pltpu.VMEM((all_probes, slab_rows), jnp.float32),
            pltpu.SemaphoreType.DMA((all_probes // HALF,)),
        ]
        + [pltpu.VMEM((all_probes, levels * rank_width), jnp.bfloat16)],
        compiler_params=pltpu.CompilerParams(vmem_limit_bytes=VMEM_LIMIT),
        name="slab_basis",
    )(where, *pieces, *payloads, left_slab)


def shared_basis(pieces, payloads, left_slab, masks, where, block_rows):
    levels, rank_width, slab_rows = left_slab.shape
    all_probes = len(masks) * pieces[0].shape[0]
    sample, gram = pl.pallas_call(
        functools.partial(sample_kernel, masks),
        in_specs=[smem()] + [vmem()] * (2 * len(masks) + 1),
        out_specs=[vmem(), vmem()],
        out_shape=[
            jax.ShapeDtypeStruct((all_probes, slab_rows), jnp.bfloat16),
            jax.ShapeDtypeStruct((all_probes, all_probes), jnp.float32),
        ],
        scratch_shapes=[pltpu.VMEM((all_probes, levels * rank_width), jnp.bfloat16)],
        compiler_params=pltpu.CompilerParams(vmem_limit_bytes=VMEM_LIMIT),
        name="sample_gram",
    )(where, *pieces, *payloads, left_slab)
    apart = 1
    while apart * slab_rows < block_rows:
        gram = gram + xor_permute(gram, "probe", apart)
        apart *= 2
    return pl.pallas_call(
        functools.partial(basis_kernel, ridge_share * block_rows),
        in_specs=[vmem(), vmem()],
        out_specs=pl.BlockSpec(memory_space=pl.ANY),
        out_shape=jax.ShapeDtypeStruct((all_probes, slab_rows), jnp.float32),
        scratch_shapes=[
            pltpu.VMEM((all_probes, slab_rows), jnp.float32),
            pltpu.SemaphoreType.DMA((all_probes // HALF,)),
        ],
        compiler_params=pltpu.CompilerParams(vmem_limit_bytes=VMEM_LIMIT),
        name="basis",
    )(gram, sample)


def shards(responses, probes, left_factors, right_factors, level_ranks):
    rows_count = lax.axis_size("rows")
    probe_count = lax.axis_size("probe")
    local_probes, rows_dev = responses.shape
    levels_count, rank_width, _ = left_factors.shape
    slab_rows = rows_dev // probe_count
    block_rows = rows_dev * rows_count // BLOCKS
    place = lax.axis_index("probe")
    where = place.astype(jnp.int32).reshape(1)
    masks = tuple(range(probe_count))

    def piece_for(values, mask):
        return lax.dynamic_slice_in_dim(values, (place ^ mask) * slab_rows, slab_rows, 1)

    far = probe_count // 2
    far_piece = piece_for(responses, far)
    pieces = {far: xor_permute(far_piece, "probe", far)}
    level_ranks, far_piece = lax.optimization_barrier((level_ranks, far_piece))
    level_ranks = xor_permute(level_ranks, "rows", 1)

    parts = [max(1, 2 ** (l + 1) // rows_count) for l in range(levels_count)]
    wide = [l for l in range(levels_count) if 2 ** (l + 1) <= rows_count]
    running, *local = couplings(probes, right_factors, level_ranks, parts, len(wide))
    later_responses, running = lax.optimization_barrier((responses, running))
    near = xor_permute(running, "rows", 1)
    for mask in sorted(range(1, probe_count), key=lambda mask: -mask.bit_length()):
        if mask != far:
            pieces[mask] = xor_permute(piece_for(later_responses, mask), "probe", mask)
    pieces[0] = piece_for(later_responses, 0)
    sources, terms = [], []
    for slot, level in enumerate(wide):
        flip = rows_count // 2 ** (level + 1)
        if flip == 1:
            sources.append(("slot", slot))
        else:
            total = running[slot] + near[slot]
            sources.append(("terms", len(range(0, flip, 2))))
            terms += [xor_permute(total, "rows", flip ^ low) for low in range(0, flip, 2)]
    narrow_parts = parts[len(wide) :]

    payloads = payloads_of(masks, sources, near, terms, narrow_parts, local, where)
    payloads = [payloads[0]] + [
        xor_permute(payloads[mask], "probe", mask) for mask in range(1, probe_count)
    ]
    ordered = [pieces[mask] for mask in masks]
    work = shared_basis if block_rows > slab_rows else slab_basis
    left_slab = left_of_slab(left_factors, pieces[far], where, slab_rows)
    return work(ordered, payloads, left_slab, masks, where, block_rows)


def solution(mesh):
    return jax.shard_map(
        shards,
        mesh=mesh,
        in_specs=(
            P("probe", "rows"),
            P("probe", "rows"),
            P(None, None, "rows"),
            P(None, None, "rows"),
            P(),
        ),
        out_specs=P(None, ("rows", "probe")),
        check_vma=False,
    )
```

time: 47.3 us -> 46.2 us (0.977)
  starting transfers between devices: 15.7 us -> 15.2 us
    pallas_call x1 -> x2, Pallas kernels: 6.22 us -> 7.75 us  [the longest x1 6 us: couplings(): pl.pallas_call(functools.partial(coupling_kernel, tuple(parts), joined, 3...]
    pallas_call x1, Pallas kernels: 12.4 us -> 10.9 us  [slab_basis(): pl.pallas_call(functools.partial(slab_kernel, masks, count, ridge_share *...]
    unnamed x6 -> x4, local copies, waits for them, and re-layouts: 1.38 us -> 1.23 us
  transfers between devices with their start and end apart: 11 -> 11, of which waited for: 6 -> 6; matrix products, arithmetic and copies ran while one was open for 2% -> 0% of each run, Pallas kernels for 13% -> 17%
where the time goes in v3:
time: 46.2 us; the launch traced here: 46.3 us
  Pallas kernels  18.7 us (40%)
  starting transfers between devices  15.2 us (33%)
  waiting for transfers between devices  9.97 us (22%)
  local copies, waits for them, and re-layouts  2.26 us (5%)
    ppermute x11, starting transfers between devices, xor_permute(): return lax.ppermute(value, axis, pairs)  15.2 us
    pallas_call x1, Pallas kernels, slab_basis(): pl.pallas_call(functools.partial(slab_kernel, masks, count, ridge_share *...  10.9 us
    ppermute x11, waiting for transfers between devices, xor_permute(): return lax.ppermute(value, axis, pairs)  9.97 us
    pallas_call x1, Pallas kernels, couplings(): pl.pallas_call(functools.partial(coupling_kernel, tuple(parts), joined, 3...  6 us
    pallas_call x1, Pallas kernels, left_of_slab(): pl.pallas_call(left_kernel, in_specs=[smem(), hbm(), hbm()], out_specs=vm...  1.75 us
    unnamed x4, local copies, waits for them, and re-layouts  1.23 us
    dynamic_slice x2, local copies, waits for them, and re-layouts, piece_for(): lax.dynamic_slice_in_dim(values, (place ^ mask) * slab_rows, slab_rows, 1)  1.03 us
  transfers between devices with their start and end apart: 11, of which 6 were waited for; matrix products, arithmetic and copies ran while one was open for 0% of the time, Pallas kernels for 17%

profile of v3, /device:TPU:0, one launch (start us, length us, event | category | flops | bytes accessed | tf_op | source)
XLA Modules:
  0.0 46.3 jit_solution(18340182161935704797)
XLA Ops:
  0.0 1.0 %constant_dynamic-slice_fusion.3 = bf16[64,2048]{1,0:T(8,128)(2,1)S(1)} fusion(bf16[64,8192]{1,0:T(8,128)(2,1)} %param.5, s32[]{:T(128)S(6)} %select_n.12), kind=kLoop, calls=%fused_computation.7 | loop fusion | bytes 524292 | tf_op jit(solution)/shard_map/dynamic_slice | solution.py:543
  1.0 4.1 %collective-permute-start.2 = (bf16[64,2048]{1,0:T(8,128)(2,1)S(1)}, bf16[64,2048]{1,0:T(8,128)(2,1)S(1)}, u32[]{:S(2)}, u32[]{:S(2)}) collective-permute-start(bf16[64,2048]{1,0:T(8,128)(2,1)S(1)} %constant_dynamic-slice_fusion.3), channel_id=1, source_target_pairs={{0,2},{1,3},{2,0},{3,1},{4,6},{5,7},{6,4},{7,5},{8,10},{9,11},{10,... | collective-permute-start | bytes 786440 | tf_op jit(solution)/shard_map/ppermute | solution.py:24
  5.1 1.3 %collective-permute-done.ranks_ref = s32[5]{0:T(128)S(1)} collective-permute-done((s32[5]{0:T(128)}, s32[5]{0:T(128)S(1)}, u32[]{:S(2)}, u32[]{:S(2)}) %collective-permute-start) | collective-permute-done | bytes 52 | tf_op jit(solution)/shard_map/ppermute | solution.py:24
  6.3 1.2 %copy-done = bf16[64,8192]{1,0:T(8,128)(2,1)S(1)} copy-done((bf16[64,8192]{1,0:T(8,128)(2,1)S(1)}, bf16[64,8192]{1,0:T(8,128)(2,1)}, u32[]{:S(2)}) %copy-start) | copy-done | bytes 1048600
  7.6 6.0 %couplings.1 = (f32[3,64,128]{2,1,0:T(8,128)S(1)}, bf16[2,64,128]{2,1,0:T(8,128)(2,1)S(1)}, bf16[4,64,128]{2,1,0:T(8,128)(2,1)S(1)}) custom-call(s32[5]{0:T(128)S(1)} %collective-permute-done.ranks_ref, bf16[64,8192]{1,0:T(8,128)(2,1)S(1)} %copy-done, bf16[5,128,8192]{2,1,0:T(8,128)(2,1)} %right_ref.1), custom_call_target="tpu_custom_call" | custom-call | flops 1 | bytes 1 | tf_op jit(solution)/shard_map/couplings/pallas_call | solution.py:135
  13.6 0.3 collective-permute-start.4
  13.8 0.1 constant_dynamic-slice_fusion
  13.9 1.4 %collective-permute-start.3 = (bf16[64,2048]{1,0:T(8,128)(2,1)S(1)}, bf16[64,2048]{1,0:T(8,128)(2,1)S(1)}, u32[]{:S(2)}, u32[]{:S(2)}) collective-permute-start(bf16[64,2048]{1,0:T(8,128)(2,1)S(1)} %get-tuple-element.25), channel_id=1, source_target_pairs={{0,3},{1,2},{2,1},{3,0},{4,7},{5,6},{6,5},{7,4},{8,11},{9,10},{10,... | collective-permute-start | bytes 786440 | tf_op jit(solution)/shard_map/ppermute | solution.py:24
  15.3 0.3 collective-permute-start.1
  15.6 1.6 %collective-permute-start.7 = (f32[64,128]{1,0:T(8,128)S(1)}, f32[64,128]{1,0:T(8,128)S(1)}, u32[]{:S(2)}, u32[]{:S(2)}) collective-permute-start(f32[64,128]{1,0:T(8,128)S(1)} %get-tuple-element.28), channel_id=1, source_target_pairs={{0,8},{4,12},{8,0},{12,4},{16,24},{20,28},{24,16},{28,20},{1,9},{5... | collective-permute-start | bytes 98312 | tf_op jit(solution)/shard_map/ppermute | solution.py:24
  17.2 1.5 %collective-permute-start.6 = (f32[64,128]{1,0:T(8,128)S(1)}, f32[64,128]{1,0:T(8,128)S(1)}, u32[]{:S(2)}, u32[]{:S(2)}) collective-permute-start(f32[64,128]{1,0:T(8,128)S(1)} %get-tuple-element.29), channel_id=1, source_target_pairs={{0,24},{4,28},{8,16},{12,20},{16,8},{20,12},{24,0},{28,4},{1,25},{... | collective-permute-start | bytes 98312 | tf_op jit(solution)/shard_map/ppermute | solution.py:24
  18.7 0.9 %collective-permute-done.7.refs_2_ = f32[64,128]{1,0:T(8,128)S(1)} collective-permute-done((f32[64,128]{1,0:T(8,128)S(1)}, f32[64,128]{1,0:T(8,128)S(1)}, u32[]{:S(2)}, u32[]{:S(2)}) %collective-permute-start.7) | collective-permute-done | bytes 32800 | tf_op jit(solution)/shard_map/ppermute | solution.py:24
  19.6 1.7 %collective-permute-start.5 = (f32[64,128]{1,0:T(8,128)S(1)}, f32[64,128]{1,0:T(8,128)S(1)}, u32[]{:S(2)}, u32[]{:S(2)}) collective-permute-start(f32[64,128]{1,0:T(8,128)S(1)} %get-tuple-element.29), channel_id=1, source_target_pairs={{0,16},{4,20},{8,24},{12,28},{16,0},{20,4},{24,8},{28,12},{1,17},{... | collective-permute-start | bytes 98312 | tf_op jit(solution)/shard_map/ppermute | solution.py:24
  21.3 0.7 %collective-permute-done.6.refs_1_ = f32[64,128]{1,0:T(8,128)S(1)} collective-permute-done((f32[64,128]{1,0:T(8,128)S(1)}, f32[64,128]{1,0:T(8,128)S(1)}, u32[]{:S(2)}, u32[]{:S(2)}) %collective-permute-start.6) | collective-permute-done | bytes 32800 | tf_op jit(solution)/shard_map/ppermute | solution.py:24
  22.0 1.5 %collective-permute-done.5.refs_0_ = f32[64,128]{1,0:T(8,128)S(1)} collective-permute-done((f32[64,128]{1,0:T(8,128)S(1)}, f32[64,128]{1,0:T(8,128)S(1)}, u32[]{:S(2)}, u32[]{:S(2)}) %collective-permute-start.5) | collective-permute-done | bytes 32800 | tf_op jit(solution)/shard_map/ppermute | solution.py:24
  23.6 1.8 %collective-permute-start.8 = (bf16[5,64,128]{2,1,0:T(8,128)(2,1)S(1)}, bf16[5,64,128]{2,1,0:T(8,128)(2,1)S(1)}, u32[]{:S(2)}, u32[]{:S(2)}) collective-permute-start(bf16[5,64,128]{2,1,0:T(8,128)(2,1)S(1)} %get-tuple-element.22), channel_id=1, source_target_pairs={{0,1},{1,0},{2,3},{3,2},{4,5},{5,4},{6,7},{7,6},{8,9},{9,8},{10,11... | collective-permute-start | bytes 245768 | tf_op jit(solution)/shard_map/ppermute | solution.py:24
  25.4 1.7 %collective-permute-start.9 = (bf16[5,64,128]{2,1,0:T(8,128)(2,1)S(1)}, bf16[5,64,128]{2,1,0:T(8,128)(2,1)S(1)}, u32[]{:S(2)}, u32[]{:S(2)}) collective-permute-start(bf16[5,64,128]{2,1,0:T(8,128)(2,1)S(1)} %get-tuple-element.23), channel_id=1, source_target_pairs={{0,2},{1,3},{2,0},{3,1},{4,6},{5,7},{6,4},{7,5},{8,10},{9,11},{10,... | collective-permute-start | bytes 245768 | tf_op jit(solution)/shard_map/ppermute | solution.py:24
  27.1 0.0 collective-permute-done.2.early_ref.refs_2_
  27.1 1.0 %collective-permute-start.10 = (bf16[5,64,128]{2,1,0:T(8,128)(2,1)S(1)}, bf16[5,64,128]{2,1,0:T(8,128)(2,1)S(1)}, u32[]{:S(2)}, u32[]{:S(2)}) collective-permute-start(bf16[5,64,128]{2,1,0:T(8,128)(2,1)S(1)} %get-tuple-element.24), channel_id=1, source_target_pairs={{0,3},{1,2},{2,1},{3,0},{4,7},{5,6},{6,5},{7,4},{8,11},{9,10},{10,... | collective-permute-start | bytes 245768 | tf_op jit(solution)/shard_map/ppermute | solution.py:24
  28.0 1.7 %left_of_slab.1.refs_8_ = bf16[5,128,2048]{2,1,0:T(8,128)(2,1)S(1)} custom-call(s32[1]{0:T(128)} %bitcast.where_ref, bf16[64,2048]{1,0:T(8,128)(2,1)S(1)} %collective-permute-done.2.early_ref.refs_2_, bf16[5,128,8192]{2,1,0:T(8,128)(2,1)} %left_ref.1), custom_call_target="tpu_custom_call" | custom-call | flops 1 | bytes 1 | tf_op jit(solution)/shard_map/left_of_slab/pallas_call | solution.py:163
  29.8 2.9 %collective-permute-done.8.refs_5_ = bf16[5,64,128]{2,1,0:T(8,128)(2,1)S(1)} collective-permute-done((bf16[5,64,128]{2,1,0:T(8,128)(2,1)S(1)}, bf16[5,64,128]{2,1,0:T(8,128)(2,1)S(1)}, u32[]{:S(2)}, u32[]{:S(2)}) %collective-permute-start.8) | collective-permute-done | bytes 81952 | tf_op jit(solution)/shard_map/ppermute | solution.py:24
  32.7 0.0 collective-permute-done.9.refs_6_
  32.7 2.6 %collective-permute-done.10.refs_7_ = bf16[5,64,128]{2,1,0:T(8,128)(2,1)S(1)} collective-permute-done((bf16[5,64,128]{2,1,0:T(8,128)(2,1)S(1)}, bf16[5,64,128]{2,1,0:T(8,128)(2,1)S(1)}, u32[]{:S(2)}, u32[]{:S(2)}) %collective-permute-start.10) | collective-permute-done | bytes 81952 | tf_op jit(solution)/shard_map/ppermute | solution.py:24
  35.3 10.9 %slab_basis.1 = f32[256,2048]{1,0:T(8,128)} custom-call(s32[1]{0:T(128)} %bitcast.where_ref, bf16[64,2048]{1,0:T(8,128)(2,1)S(1)} %get-tuple-element.27.refs_0_, bf16[64,2048]{1,0:T(8,128)(2,1)S(1)} %collective-permute-done.1.refs_1_, bf16[64,2048]{1,0:T(8,128)(2,1)S(1)} %collective-permute-done.2.early_ref.refs_2_, ...), custom_call_target="tpu_custom_call" | custom-call | tf_op jit(solution)/shard_map/slab_basis/pallas_call | solution.py:482
  (9 shorter events, 0.1 us)
Async XLA Ops:
  1.0 26.1 %collective-permute-start.2 = (bf16[64,2048]{1,0:T(8,128)(2,1)S(1)}, bf16[64,2048]{1,0:T(8,128)(2,1)S(1)}, u32[]{:S(2)}, u32[]{:S(2)}) collective-permute-start(bf16[64,2048]{1,0:T(8,128)(2,1)S(1)} %constant_dynamic-slice_fusion.3), channel_id=1, source_target_pairs={{0,2},{1,3},{2,0},{3,1},{4,6},{5,7},{6,4},{7,5},{8,10},{9,11},{10,... | collective-permute-start | bytes 786440 | tf_op jit(solution)/shard_map/ppermute | solution.py:24
  5.1 1.3 %collective-permute-start = (s32[5]{0:T(128)}, s32[5]{0:T(128)S(1)}, u32[]{:S(2)}, u32[]{:S(2)}) collective-permute-start(s32[5]{0:T(128)} %param.9), channel_id=1, source_target_pairs={{0,4},{4,0},{8,12},{12,8},{16,20},{20,16},{24,28},{28,24},{1,5},{5... | collective-permute-start | bytes 68 | tf_op jit(solution)/shard_map/ppermute | solution.py:24
  6.3 1.2 %copy-start = (bf16[64,8192]{1,0:T(8,128)(2,1)S(1)}, bf16[64,8192]{1,0:T(8,128)(2,1)}, u32[]{:S(2)}) copy-start(bf16[64,8192]{1,0:T(8,128)(2,1)} %probes_ref.1) | copy-start | bytes 3145732
  7.6 6.3 %copy-start.1 = (bf16[64,8192]{1,0:T(8,128)(2,1)S(1)}, bf16[64,8192]{1,0:T(8,128)(2,1)}, u32[]{:S(2)}) copy-start(bf16[64,8192]{1,0:T(8,128)(2,1)} %param.5) | copy-start | bytes 3145732
  13.6 2.1 %collective-permute-start.4 = (f32[3,64,128]{2,1,0:T(8,128)S(1)}, f32[3,64,128]{2,1,0:T(8,128)S(1)}, u32[]{:S(2)}, u32[]{:S(2)}) collective-permute-start(f32[3,64,128]{2,1,0:T(8,128)S(1)} %get-tuple-element.18), channel_id=1, source_target_pairs={{0,4},{4,0},{8,12},{12,8},{16,20},{20,16},{24,28},{28,24},{1,5},{5... | collective-permute-start | bytes 294920 | tf_op jit(solution)/shard_map/ppermute | solution.py:24
  13.9 21.4 %collective-permute-start.3 = (bf16[64,2048]{1,0:T(8,128)(2,1)S(1)}, bf16[64,2048]{1,0:T(8,128)(2,1)S(1)}, u32[]{:S(2)}, u32[]{:S(2)}) collective-permute-start(bf16[64,2048]{1,0:T(8,128)(2,1)S(1)} %get-tuple-element.25), channel_id=1, source_target_pairs={{0,3},{1,2},{2,1},{3,0},{4,7},{5,6},{6,5},{7,4},{8,11},{9,10},{10,... | collective-permute-start | bytes 786440 | tf_op jit(solution)/shard_map/ppermute | solution.py:24
  15.3 20.0 %collective-permute-start.1 = (bf16[64,2048]{1,0:T(8,128)(2,1)S(1)}, bf16[64,2048]{1,0:T(8,128)(2,1)S(1)}, u32[]{:S(2)}, u32[]{:S(2)}) collective-permute-start(bf16[64,2048]{1,0:T(8,128)(2,1)S(1)} %get-tuple-element.26), channel_id=1, source_target_pairs={{0,1},{1,0},{2,3},{3,2},{4,5},{5,4},{6,7},{7,6},{8,9},{9,8},{10,11... | collective-permute-start | bytes 786440 | tf_op jit(solution)/shard_map/ppermute | solution.py:24
  15.6 4.0 %collective-permute-start.7 = (f32[64,128]{1,0:T(8,128)S(1)}, f32[64,128]{1,0:T(8,128)S(1)}, u32[]{:S(2)}, u32[]{:S(2)}) collective-permute-start(f32[64,128]{1,0:T(8,128)S(1)} %get-tuple-element.28), channel_id=1, source_target_pairs={{0,8},{4,12},{8,0},{12,4},{16,24},{20,28},{24,16},{28,20},{1,9},{5... | collective-permute-start | bytes 98312 | tf_op jit(solution)/shard_map/ppermute | solution.py:24
  17.2 4.8 %collective-permute-start.6 = (f32[64,128]{1,0:T(8,128)S(1)}, f32[64,128]{1,0:T(8,128)S(1)}, u32[]{:S(2)}, u32[]{:S(2)}) collective-permute-start(f32[64,128]{1,0:T(8,128)S(1)} %get-tuple-element.29), channel_id=1, source_target_pairs={{0,24},{4,28},{8,16},{12,20},{16,8},{20,12},{24,0},{28,4},{1,25},{... | collective-permute-start | bytes 98312 | tf_op jit(solution)/shard_map/ppermute | solution.py:24
  19.6 3.9 %collective-permute-start.5 = (f32[64,128]{1,0:T(8,128)S(1)}, f32[64,128]{1,0:T(8,128)S(1)}, u32[]{:S(2)}, u32[]{:S(2)}) collective-permute-start(f32[64,128]{1,0:T(8,128)S(1)} %get-tuple-element.29), channel_id=1, source_target_pairs={{0,16},{4,20},{8,24},{12,28},{16,0},{20,4},{24,8},{28,12},{1,17},{... | collective-permute-start | bytes 98312 | tf_op jit(solution)/shard_map/ppermute | solution.py:24
  23.6 9.1 %collective-permute-start.8 = (bf16[5,64,128]{2,1,0:T(8,128)(2,1)S(1)}, bf16[5,64,128]{2,1,0:T(8,128)(2,1)S(1)}, u32[]{:S(2)}, u32[]{:S(2)}) collective-permute-start(bf16[5,64,128]{2,1,0:T(8,128)(2,1)S(1)} %get-tuple-element.22), channel_id=1, source_target_pairs={{0,1},{1,0},{2,3},{3,2},{4,5},{5,4},{6,7},{7,6},{8,9},{9,8},{10,11... | collective-permute-start | bytes 245768 | tf_op jit(solution)/shard_map/ppermute | solution.py:24
  25.4 7.3 %collective-permute-start.9 = (bf16[5,64,128]{2,1,0:T(8,128)(2,1)S(1)}, bf16[5,64,128]{2,1,0:T(8,128)(2,1)S(1)}, u32[]{:S(2)}, u32[]{:S(2)}) collective-permute-start(bf16[5,64,128]{2,1,0:T(8,128)(2,1)S(1)} %get-tuple-element.23), channel_id=1, source_target_pairs={{0,2},{1,3},{2,0},{3,1},{4,6},{5,7},{6,4},{7,5},{8,10},{9,11},{10,... | collective-permute-start | bytes 245768 | tf_op jit(solution)/shard_map/ppermute | solution.py:24
  27.1 8.3 %collective-permute-start.10 = (bf16[5,64,128]{2,1,0:T(8,128)(2,1)S(1)}, bf16[5,64,128]{2,1,0:T(8,128)(2,1)S(1)}, u32[]{:S(2)}, u32[]{:S(2)}) collective-permute-start(bf16[5,64,128]{2,1,0:T(8,128)(2,1)S(1)} %get-tuple-element.24), channel_id=1, source_target_pairs={{0,3},{1,2},{2,1},{3,0},{4,7},{5,6},{6,5},{7,4},{8,11},{9,10},{10,... | collective-permute-start | bytes 245768 | tf_op jit(solution)/shard_map/ppermute | solution.py:24

commit v4 on v3

--- a/solution.py
+++ b/solution.py
@@ -226,53 +226,67 @@
     return terms[0]
 
 
+PANEL = 2
+
+
 def eliminate(left, right):
     row_iota = lax.broadcasted_iota(jnp.int32, (SUBLANES, LANES), 0)
     half_start = lax.broadcasted_iota(jnp.int32, (SUBLANES, LANES), 1) // HALF * HALF
-    equal = [row_iota == a for a in range(SUBLANES)]
-    after = [row_iota >= a for a in range(SUBLANES)]
+    equal = [row_iota == r for r in range(SUBLANES)]
+    after = [row_iota >= r for r in range(SUBLANES)]
     left, right = list(left), list(right)
     finished = []
-    for group in range(len(left)):
-        base = SUBLANES * group
-        pivot_left, pivot_right = left[group], right[group]
-        columns = [column_of(pivot_left, base + b, half_start) for b in range(SUBLANES)]
-        rest = range(group + 1, len(left))
+    width = SUBLANES * PANEL
+    for begin in range(0, len(left), PANEL):
+        base = SUBLANES * begin
+        own_left, own_right = left[begin : begin + PANEL], right[begin : begin + PANEL]
+        columns = [[column_of(v, base + c, half_start) for c in range(width)] for v in own_left]
+        rest = range(begin + PANEL, len(left))
         rest_columns = {
-            h: [column_of(left[h], base + c, half_start) for c in range(SUBLANES)] for h in rest
+            h: [column_of(left[h], base + c, half_start) for c in range(width)] for h in rest
         }
         inverses = []
-        collected = pivots = None
-        for a in range(0, SUBLANES, 2):
-            first = row_of(columns[a], a)
-            cross = row_of(columns[a + 1], a)
-            determinant = first * row_of(columns[a + 1], a + 1) - cross * cross
-            inverse_first = 1.0 / first
-            inverse_second = first * (1.0 / determinant)
-            second = determinant * inverse_first
-            for at, diagonal, inverse in (
-                (a, first, inverse_first),
-                (a + 1, second, inverse_second),
-            ):
-                factor = jnp.where(equal[at], 0.0, columns[at]) * inverse
-                for b in range(at + 1, SUBLANES):
-                    columns[b] = columns[b] - factor * row_of(columns[b], at)
-                current_left, current_right = row_of(pivot_left, at), row_of(pivot_right, at)
-                pivot_left = pivot_left - factor * current_left
-                pivot_right = pivot_right - factor * current_right
-                collected = current_right if at == 0 else jnp.where(after[at], current_right, collected)
-                pivots = diagonal if at == 0 else jnp.where(after[at], diagonal, pivots)
-                inverses.append(inverse)
-        finished.append(collected * lax.rsqrt(pivots))
-        if group + 1 < len(left):
-            solved_left = [row_of(pivot_left, c) * inverses[c] for c in range(SUBLANES)]
-            solved_right = [row_of(pivot_right, c) * inverses[c] for c in range(SUBLANES)]
+        for tile in range(PANEL):
+            collected = pivots = None
+            for row in range(0, SUBLANES, 2):
+                at = SUBLANES * tile + row
+                first = row_of(columns[tile][at], row)
+                cross = row_of(columns[tile][at + 1], row)
+                determinant = first * row_of(columns[tile][at + 1], row + 1) - cross * cross
+                inverse_first = 1.0 / first
+                inverse_second = first * (1.0 / determinant)
+                second = determinant * inverse_first
+                for r, diagonal, inverse in (
+                    (row, first, inverse_first),
+                    (row + 1, second, inverse_second),
+                ):
+                    at = SUBLANES * tile + r
+                    factors = [columns[t][at] * inverse for t in range(PANEL)]
+                    factors[tile] = jnp.where(equal[r], 0.0, factors[tile])
+                    for c in range(at + 1, width):
+                        entry = row_of(columns[tile][c], r)
+                        for t in range(PANEL):
+                            columns[t][c] = columns[t][c] - factors[t] * entry
+                    current_left, current_right = row_of(own_left[tile], r), row_of(own_right[tile], r)
+                    for t in range(PANEL):
+                        own_left[t] = own_left[t] - factors[t] * current_left
+                        own_right[t] = own_right[t] - factors[t] * current_right
+                    collected = current_right if r == 0 else jnp.where(after[r], current_right, collected)
+                    pivots = diagonal if r == 0 else jnp.where(after[r], diagonal, pivots)
+                    inverses.append(inverse)
+            finished.append(collected * lax.rsqrt(pivots))
+        if len(rest):
+            solved_left, solved_right = [], []
+            for c in range(width):
+                tile, r = divmod(c, SUBLANES)
+                solved_left.append(row_of(own_left[tile], r) * inverses[c])
+                solved_right.append(row_of(own_right[tile], r) * inverses[c])
             for h in rest:
                 left[h] = left[h] - sum_tree(
-                    [rest_columns[h][c] * solved_left[c] for c in range(SUBLANES)]
+                    [rest_columns[h][c] * solved_left[c] for c in range(width)]
                 )
                 right[h] = right[h] - sum_tree(
-                    [rest_columns[h][c] * solved_right[c] for c in range(SUBLANES)]
+                    [rest_columns[h][c] * solved_right[c] for c in range(width)]
                 )
     return jnp.concatenate(finished, 0)
 
@@ -421,11 +435,13 @@
             )
             columns = slice(which * piece_rows, (which + 1) * piece_rows)
             buffer_ref[at, columns] = both[:height] + both[height:]
+            copies.append(
+                pltpu.make_async_copy(
+                    buffer_ref.at[at, columns], out_ref.at[at, columns], sems.at[len(copies)]
+                )
+            )
+            copies[-1].start()
         held.clear()
-        copies.append(
-            pltpu.make_async_copy(buffer_ref.at[at], out_ref.at[at], sems.at[len(copies)])
-        )
-        copies[-1].start()
 
     inverse_factors(grams, take_rows)
     for copy in copies:

time: 46.2 us -> 44.2 us (0.957)
  Pallas kernels: 18.7 us -> 16.4 us
    pallas_call x1, Pallas kernels: 10.9 us -> 9.37 us  [slab_basis(): pl.pallas_call(functools.partial(slab_kernel, masks, count, ridge_share *...]
    pallas_call x1, Pallas kernels: 6 us -> 5.28 us  [couplings(): pl.pallas_call(functools.partial(coupling_kernel, tuple(parts), joined, 3...]
  transfers between devices with their start and end apart: 11 -> 11, of which waited for: 6 -> 6; matrix products, arithmetic and copies ran while one was open for 0% -> 0% of each run, Pallas kernels for 17% -> 16%
where the time goes in v4:
time: 44.2 us; the launch traced here: 44 us
  Pallas kernels  16.4 us (37%)
  starting transfers between devices  15.3 us (35%)
  waiting for transfers between devices  9.96 us (23%)
  local copies, waits for them, and re-layouts  2.26 us (5%)
    ppermute x11, starting transfers between devices, xor_permute(): return lax.ppermute(value, axis, pairs)  15.3 us
    ppermute x11, waiting for transfers between devices, xor_permute(): return lax.ppermute(value, axis, pairs)  9.96 us
    pallas_call x1, Pallas kernels, slab_basis(): pl.pallas_call(functools.partial(slab_kernel, masks, count, ridge_share *...  9.37 us
    pallas_call x1, Pallas kernels, couplings(): pl.pallas_call(functools.partial(coupling_kernel, tuple(parts), joined, 3...  5.28 us
    pallas_call x1, Pallas kernels, left_of_slab(): pl.pallas_call(left_kernel, in_specs=[smem(), hbm(), hbm()], out_specs=vm...  1.75 us
    unnamed x4, local copies, waits for them, and re-layouts  1.23 us
    dynamic_slice x2, local copies, waits for them, and re-layouts, piece_for(): lax.dynamic_slice_in_dim(values, (place ^ mask) * slab_rows, slab_rows, 1)  1.03 us
  transfers between devices with their start and end apart: 11, of which 6 were waited for; matrix products, arithmetic and copies ran while one was open for 0% of the time, Pallas kernels for 16%

profile of v4, /device:TPU:0, one launch (start us, length us, event | category | flops | bytes accessed | tf_op | source)
XLA Modules:
  0.0 44.0 jit_solution(4227183997592076027)
XLA Ops:
  0.0 1.0 %constant_dynamic-slice_fusion.3 = bf16[64,2048]{1,0:T(8,128)(2,1)S(1)} fusion(bf16[64,8192]{1,0:T(8,128)(2,1)} %param.5, s32[]{:T(128)S(6)} %select_n.12), kind=kLoop, calls=%fused_computation.7 | loop fusion | bytes 524292 | tf_op jit(solution)/shard_map/dynamic_slice | solution.py:559
  1.0 4.1 %collective-permute-start.2 = (bf16[64,2048]{1,0:T(8,128)(2,1)S(1)}, bf16[64,2048]{1,0:T(8,128)(2,1)S(1)}, u32[]{:S(2)}, u32[]{:S(2)}) collective-permute-start(bf16[64,2048]{1,0:T(8,128)(2,1)S(1)} %constant_dynamic-slice_fusion.3), channel_id=1, source_target_pairs={{0,2},{1,3},{2,0},{3,1},{4,6},{5,7},{6,4},{7,5},{8,10},{9,11},{10,... | collective-permute-start | bytes 786440 | tf_op jit(solution)/shard_map/ppermute | solution.py:24
  5.1 0.0 collective-permute-start
  5.1 1.3 %collective-permute-done.ranks_ref = s32[5]{0:T(128)S(1)} collective-permute-done((s32[5]{0:T(128)}, s32[5]{0:T(128)S(1)}, u32[]{:S(2)}, u32[]{:S(2)}) %collective-permute-start) | collective-permute-done | bytes 52 | tf_op jit(solution)/shard_map/ppermute | solution.py:24
  6.3 1.2 %copy-done = bf16[64,8192]{1,0:T(8,128)(2,1)S(1)} copy-done((bf16[64,8192]{1,0:T(8,128)(2,1)S(1)}, bf16[64,8192]{1,0:T(8,128)(2,1)}, u32[]{:S(2)}) %copy-start) | copy-done | bytes 1048600
  7.6 5.3 %couplings.1 = (f32[3,64,128]{2,1,0:T(8,128)S(1)}, bf16[2,64,128]{2,1,0:T(8,128)(2,1)S(1)}, bf16[4,64,128]{2,1,0:T(8,128)(2,1)S(1)}) custom-call(s32[5]{0:T(128)S(1)} %collective-permute-done.ranks_ref, bf16[64,8192]{1,0:T(8,128)(2,1)S(1)} %copy-done, bf16[5,128,8192]{2,1,0:T(8,128)(2,1)} %right_ref.1), custom_call_target="tpu_custom_call" | custom-call | flops 1 | bytes 1 | tf_op jit(solution)/shard_map/couplings/pallas_call | solution.py:135
  12.8 0.3 collective-permute-start.4
  13.1 0.1 constant_dynamic-slice_fusion
  13.2 1.4 %collective-permute-start.3 = (bf16[64,2048]{1,0:T(8,128)(2,1)S(1)}, bf16[64,2048]{1,0:T(8,128)(2,1)S(1)}, u32[]{:S(2)}, u32[]{:S(2)}) collective-permute-start(bf16[64,2048]{1,0:T(8,128)(2,1)S(1)} %get-tuple-element.25), channel_id=1, source_target_pairs={{0,3},{1,2},{2,1},{3,0},{4,7},{5,6},{6,5},{7,4},{8,11},{9,10},{10,... | collective-permute-start | bytes 786440 | tf_op jit(solution)/shard_map/ppermute | solution.py:24
  14.6 0.3 collective-permute-start.1
  14.9 0.0 collective-permute-done.4.near_ref
  14.9 1.6 %collective-permute-start.7 = (f32[64,128]{1,0:T(8,128)S(1)}, f32[64,128]{1,0:T(8,128)S(1)}, u32[]{:S(2)}, u32[]{:S(2)}) collective-permute-start(f32[64,128]{1,0:T(8,128)S(1)} %get-tuple-element.28), channel_id=1, source_target_pairs={{0,8},{4,12},{8,0},{12,4},{16,24},{20,28},{24,16},{28,20},{1,9},{5... | collective-permute-start | bytes 98312 | tf_op jit(solution)/shard_map/ppermute | solution.py:24
  16.5 1.5 %collective-permute-start.6 = (f32[64,128]{1,0:T(8,128)S(1)}, f32[64,128]{1,0:T(8,128)S(1)}, u32[]{:S(2)}, u32[]{:S(2)}) collective-permute-start(f32[64,128]{1,0:T(8,128)S(1)} %get-tuple-element.29), channel_id=1, source_target_pairs={{0,24},{4,28},{8,16},{12,20},{16,8},{20,12},{24,0},{28,4},{1,25},{... | collective-permute-start | bytes 98312 | tf_op jit(solution)/shard_map/ppermute | solution.py:24
  18.0 0.9 %collective-permute-done.7.refs_2_ = f32[64,128]{1,0:T(8,128)S(1)} collective-permute-done((f32[64,128]{1,0:T(8,128)S(1)}, f32[64,128]{1,0:T(8,128)S(1)}, u32[]{:S(2)}, u32[]{:S(2)}) %collective-permute-start.7) | collective-permute-done | bytes 32800 | tf_op jit(solution)/shard_map/ppermute | solution.py:24
  18.9 1.7 %collective-permute-start.5 = (f32[64,128]{1,0:T(8,128)S(1)}, f32[64,128]{1,0:T(8,128)S(1)}, u32[]{:S(2)}, u32[]{:S(2)}) collective-permute-start(f32[64,128]{1,0:T(8,128)S(1)} %get-tuple-element.29), channel_id=1, source_target_pairs={{0,16},{4,20},{8,24},{12,28},{16,0},{20,4},{24,8},{28,12},{1,17},{... | collective-permute-start | bytes 98312 | tf_op jit(solution)/shard_map/ppermute | solution.py:24
  20.6 0.7 %collective-permute-done.6.refs_1_ = f32[64,128]{1,0:T(8,128)S(1)} collective-permute-done((f32[64,128]{1,0:T(8,128)S(1)}, f32[64,128]{1,0:T(8,128)S(1)}, u32[]{:S(2)}, u32[]{:S(2)}) %collective-permute-start.6) | collective-permute-done | bytes 32800 | tf_op jit(solution)/shard_map/ppermute | solution.py:24
  21.3 1.5 %collective-permute-done.5.refs_0_ = f32[64,128]{1,0:T(8,128)S(1)} collective-permute-done((f32[64,128]{1,0:T(8,128)S(1)}, f32[64,128]{1,0:T(8,128)S(1)}, u32[]{:S(2)}, u32[]{:S(2)}) %collective-permute-start.5) | collective-permute-done | bytes 32800 | tf_op jit(solution)/shard_map/ppermute | solution.py:24
  22.9 1.8 %collective-permute-start.8 = (bf16[5,64,128]{2,1,0:T(8,128)(2,1)S(1)}, bf16[5,64,128]{2,1,0:T(8,128)(2,1)S(1)}, u32[]{:S(2)}, u32[]{:S(2)}) collective-permute-start(bf16[5,64,128]{2,1,0:T(8,128)(2,1)S(1)} %get-tuple-element.22), channel_id=1, source_target_pairs={{0,1},{1,0},{2,3},{3,2},{4,5},{5,4},{6,7},{7,6},{8,9},{9,8},{10,11... | collective-permute-start | bytes 245768 | tf_op jit(solution)/shard_map/ppermute | solution.py:24
  24.7 1.7 %collective-permute-start.9 = (bf16[5,64,128]{2,1,0:T(8,128)(2,1)S(1)}, bf16[5,64,128]{2,1,0:T(8,128)(2,1)S(1)}, u32[]{:S(2)}, u32[]{:S(2)}) collective-permute-start(bf16[5,64,128]{2,1,0:T(8,128)(2,1)S(1)} %get-tuple-element.23), channel_id=1, source_target_pairs={{0,2},{1,3},{2,0},{3,1},{4,6},{5,7},{6,4},{7,5},{8,10},{9,11},{10,... | collective-permute-start | bytes 245768 | tf_op jit(solution)/shard_map/ppermute | solution.py:24
  26.4 1.0 %collective-permute-start.10 = (bf16[5,64,128]{2,1,0:T(8,128)(2,1)S(1)}, bf16[5,64,128]{2,1,0:T(8,128)(2,1)S(1)}, u32[]{:S(2)}, u32[]{:S(2)}) collective-permute-start(bf16[5,64,128]{2,1,0:T(8,128)(2,1)S(1)} %get-tuple-element.24), channel_id=1, source_target_pairs={{0,3},{1,2},{2,1},{3,0},{4,7},{5,6},{6,5},{7,4},{8,11},{9,10},{10,... | collective-permute-start | bytes 245768 | tf_op jit(solution)/shard_map/ppermute | solution.py:24
  27.3 1.7 %left_of_slab.1.refs_8_ = bf16[5,128,2048]{2,1,0:T(8,128)(2,1)S(1)} custom-call(s32[1]{0:T(128)} %bitcast.where_ref, bf16[64,2048]{1,0:T(8,128)(2,1)S(1)} %collective-permute-done.2.early_ref.refs_2_, bf16[5,128,8192]{2,1,0:T(8,128)(2,1)} %left_ref.1), custom_call_target="tpu_custom_call" | custom-call | flops 1 | bytes 1 | tf_op jit(solution)/shard_map/left_of_slab/pallas_call | solution.py:163
  29.1 2.9 %collective-permute-done.8.refs_5_ = bf16[5,64,128]{2,1,0:T(8,128)(2,1)S(1)} collective-permute-done((bf16[5,64,128]{2,1,0:T(8,128)(2,1)S(1)}, bf16[5,64,128]{2,1,0:T(8,128)(2,1)S(1)}, u32[]{:S(2)}, u32[]{:S(2)}) %collective-permute-start.8) | collective-permute-done | bytes 81952 | tf_op jit(solution)/shard_map/ppermute | solution.py:24
  32.0 2.6 %collective-permute-done.10.refs_7_ = bf16[5,64,128]{2,1,0:T(8,128)(2,1)S(1)} collective-permute-done((bf16[5,64,128]{2,1,0:T(8,128)(2,1)S(1)}, bf16[5,64,128]{2,1,0:T(8,128)(2,1)S(1)}, u32[]{:S(2)}, u32[]{:S(2)}) %collective-permute-start.10) | collective-permute-done | bytes 81952 | tf_op jit(solution)/shard_map/ppermute | solution.py:24
  34.6 9.4 %slab_basis.1 = f32[256,2048]{1,0:T(8,128)} custom-call(s32[1]{0:T(128)} %bitcast.where_ref, bf16[64,2048]{1,0:T(8,128)(2,1)S(1)} %get-tuple-element.27.refs_0_, bf16[64,2048]{1,0:T(8,128)(2,1)S(1)} %collective-permute-done.1.refs_1_, bf16[64,2048]{1,0:T(8,128)(2,1)S(1)} %collective-permute-done.2.early_ref.refs_2_, ...), custom_call_target="tpu_custom_call" | custom-call | tf_op jit(solution)/shard_map/slab_basis/pallas_call | solution.py:498
  (9 shorter events, 0.1 us)
Async XLA Ops:
  1.0 25.4 %collective-permute-start.2 = (bf16[64,2048]{1,0:T(8,128)(2,1)S(1)}, bf16[64,2048]{1,0:T(8,128)(2,1)S(1)}, u32[]{:S(2)}, u32[]{:S(2)}) collective-permute-start(bf16[64,2048]{1,0:T(8,128)(2,1)S(1)} %constant_dynamic-slice_fusion.3), channel_id=1, source_target_pairs={{0,2},{1,3},{2,0},{3,1},{4,6},{5,7},{6,4},{7,5},{8,10},{9,11},{10,... | collective-permute-start | bytes 786440 | tf_op jit(solution)/shard_map/ppermute | solution.py:24
  5.1 1.3 %collective-permute-start = (s32[5]{0:T(128)}, s32[5]{0:T(128)S(1)}, u32[]{:S(2)}, u32[]{:S(2)}) collective-permute-start(s32[5]{0:T(128)} %param.9), channel_id=1, source_target_pairs={{0,4},{4,0},{8,12},{12,8},{16,20},{20,16},{24,28},{28,24},{1,5},{5... | collective-permute-start | bytes 68 | tf_op jit(solution)/shard_map/ppermute | solution.py:24
  6.3 1.2 %copy-start = (bf16[64,8192]{1,0:T(8,128)(2,1)S(1)}, bf16[64,8192]{1,0:T(8,128)(2,1)}, u32[]{:S(2)}) copy-start(bf16[64,8192]{1,0:T(8,128)(2,1)} %probes_ref.1) | copy-start | bytes 3145732
  7.6 5.6 %copy-start.1 = (bf16[64,8192]{1,0:T(8,128)(2,1)S(1)}, bf16[64,8192]{1,0:T(8,128)(2,1)}, u32[]{:S(2)}) copy-start(bf16[64,8192]{1,0:T(8,128)(2,1)} %param.5) | copy-start | bytes 3145732
  12.8 2.1 %collective-permute-start.4 = (f32[3,64,128]{2,1,0:T(8,128)S(1)}, f32[3,64,128]{2,1,0:T(8,128)S(1)}, u32[]{:S(2)}, u32[]{:S(2)}) collective-permute-start(f32[3,64,128]{2,1,0:T(8,128)S(1)} %get-tuple-element.18), channel_id=1, source_target_pairs={{0,4},{4,0},{8,12},{12,8},{16,20},{20,16},{24,28},{28,24},{1,5},{5... | collective-permute-start | bytes 294920 | tf_op jit(solution)/shard_map/ppermute | solution.py:24
  13.2 21.4 %collective-permute-start.3 = (bf16[64,2048]{1,0:T(8,128)(2,1)S(1)}, bf16[64,2048]{1,0:T(8,128)(2,1)S(1)}, u32[]{:S(2)}, u32[]{:S(2)}) collective-permute-start(bf16[64,2048]{1,0:T(8,128)(2,1)S(1)} %get-tuple-element.25), channel_id=1, source_target_pairs={{0,3},{1,2},{2,1},{3,0},{4,7},{5,6},{6,5},{7,4},{8,11},{9,10},{10,... | collective-permute-start | bytes 786440 | tf_op jit(solution)/shard_map/ppermute | solution.py:24
  14.6 20.0 %collective-permute-start.1 = (bf16[64,2048]{1,0:T(8,128)(2,1)S(1)}, bf16[64,2048]{1,0:T(8,128)(2,1)S(1)}, u32[]{:S(2)}, u32[]{:S(2)}) collective-permute-start(bf16[64,2048]{1,0:T(8,128)(2,1)S(1)} %get-tuple-element.26), channel_id=1, source_target_pairs={{0,1},{1,0},{2,3},{3,2},{4,5},{5,4},{6,7},{7,6},{8,9},{9,8},{10,11... | collective-permute-start | bytes 786440 | tf_op jit(solution)/shard_map/ppermute | solution.py:24
  14.9 4.0 %collective-permute-start.7 = (f32[64,128]{1,0:T(8,128)S(1)}, f32[64,128]{1,0:T(8,128)S(1)}, u32[]{:S(2)}, u32[]{:S(2)}) collective-permute-start(f32[64,128]{1,0:T(8,128)S(1)} %get-tuple-element.28), channel_id=1, source_target_pairs={{0,8},{4,12},{8,0},{12,4},{16,24},{20,28},{24,16},{28,20},{1,9},{5... | collective-permute-start | bytes 98312 | tf_op jit(solution)/shard_map/ppermute | solution.py:24
  16.5 4.8 %collective-permute-start.6 = (f32[64,128]{1,0:T(8,128)S(1)}, f32[64,128]{1,0:T(8,128)S(1)}, u32[]{:S(2)}, u32[]{:S(2)}) collective-permute-start(f32[64,128]{1,0:T(8,128)S(1)} %get-tuple-element.29), channel_id=1, source_target_pairs={{0,24},{4,28},{8,16},{12,20},{16,8},{20,12},{24,0},{28,4},{1,25},{... | collective-permute-start | bytes 98312 | tf_op jit(solution)/shard_map/ppermute | solution.py:24
  18.9 3.9 %collective-permute-start.5 = (f32[64,128]{1,0:T(8,128)S(1)}, f32[64,128]{1,0:T(8,128)S(1)}, u32[]{:S(2)}, u32[]{:S(2)}) collective-permute-start(f32[64,128]{1,0:T(8,128)S(1)} %get-tuple-element.29), channel_id=1, source_target_pairs={{0,16},{4,20},{8,24},{12,28},{16,0},{20,4},{24,8},{28,12},{1,17},{... | collective-permute-start | bytes 98312 | tf_op jit(solution)/shard_map/ppermute | solution.py:24
  22.9 9.1 %collective-permute-start.8 = (bf16[5,64,128]{2,1,0:T(8,128)(2,1)S(1)}, bf16[5,64,128]{2,1,0:T(8,128)(2,1)S(1)}, u32[]{:S(2)}, u32[]{:S(2)}) collective-permute-start(bf16[5,64,128]{2,1,0:T(8,128)(2,1)S(1)} %get-tuple-element.22), channel_id=1, source_target_pairs={{0,1},{1,0},{2,3},{3,2},{4,5},{5,4},{6,7},{7,6},{8,9},{9,8},{10,11... | collective-permute-start | bytes 245768 | tf_op jit(solution)/shard_map/ppermute | solution.py:24
  24.7 7.3 %collective-permute-start.9 = (bf16[5,64,128]{2,1,0:T(8,128)(2,1)S(1)}, bf16[5,64,128]{2,1,0:T(8,128)(2,1)S(1)}, u32[]{:S(2)}, u32[]{:S(2)}) collective-permute-start(bf16[5,64,128]{2,1,0:T(8,128)(2,1)S(1)} %get-tuple-element.23), channel_id=1, source_target_pairs={{0,2},{1,3},{2,0},{3,1},{4,6},{5,7},{6,4},{7,5},{8,10},{9,11},{10,... | collective-permute-start | bytes 245768 | tf_op jit(solution)/shard_map/ppermute | solution.py:24
  26.4 8.2 %collective-permute-start.10 = (bf16[5,64,128]{2,1,0:T(8,128)(2,1)S(1)}, bf16[5,64,128]{2,1,0:T(8,128)(2,1)S(1)}, u32[]{:S(2)}, u32[]{:S(2)}) collective-permute-start(bf16[5,64,128]{2,1,0:T(8,128)(2,1)S(1)} %get-tuple-element.24), channel_id=1, source_target_pairs={{0,3},{1,2},{2,1},{3,0},{4,7},{5,6},{6,5},{7,4},{8,11},{9,10},{10,... | collective-permute-start | bytes 245768 | tf_op jit(solution)/shard_map/ppermute | solution.py:24

commit v5 on v4

--- a/solution.py
+++ b/solution.py
@@ -232,24 +232,30 @@
 def eliminate(left, right):
     row_iota = lax.broadcasted_iota(jnp.int32, (SUBLANES, LANES), 0)
     half_start = lax.broadcasted_iota(jnp.int32, (SUBLANES, LANES), 1) // HALF * HALF
-    equal = [row_iota == r for r in range(SUBLANES)]
+    below = [row_iota > r for r in range(SUBLANES)]
     after = [row_iota >= r for r in range(SUBLANES)]
     left, right = list(left), list(right)
     finished = []
     width = SUBLANES * PANEL
     for begin in range(0, len(left), PANEL):
         base = SUBLANES * begin
-        own_left, own_right = left[begin : begin + PANEL], right[begin : begin + PANEL]
-        columns = [[column_of(v, base + c, half_start) for c in range(width)] for v in own_left]
+        own = range(begin, begin + PANEL)
         rest = range(begin + PANEL, len(left))
-        rest_columns = {
-            h: [column_of(left[h], base + c, half_start) for c in range(width)] for h in rest
+        columns = {
+            t: [column_of(left[t], base + c, half_start) for c in range(width)] for t in own
         }
-        inverses = []
-        for tile in range(PANEL):
+        for tile in own:
+            first_column = SUBLANES * (tile - begin)
+            rest_columns = {
+                h: [
+                    column_of(left[h], base + first_column + c, half_start)
+                    for c in range(SUBLANES)
+                ]
+                for h in rest
+            }
             collected = pivots = None
             for row in range(0, SUBLANES, 2):
-                at = SUBLANES * tile + row
+                at = first_column + row
                 first = row_of(columns[tile][at], row)
                 cross = row_of(columns[tile][at + 1], row)
                 determinant = first * row_of(columns[tile][at + 1], row + 1) - cross * cross
@@ -260,34 +266,31 @@
                     (row, first, inverse_first),
                     (row + 1, second, inverse_second),
                 ):
-                    at = SUBLANES * tile + r
-                    factors = [columns[t][at] * inverse for t in range(PANEL)]
-                    factors[tile] = jnp.where(equal[r], 0.0, factors[tile])
-                    for c in range(at + 1, width):
-                        entry = row_of(columns[tile][c], r)
-                        for t in range(PANEL):
-                            columns[t][c] = columns[t][c] - factors[t] * entry
-                    current_left, current_right = row_of(own_left[tile], r), row_of(own_right[tile], r)
-                    for t in range(PANEL):
-                        own_left[t] = own_left[t] - factors[t] * current_left
-                        own_right[t] = own_right[t] - factors[t] * current_right
-                    collected = current_right if r == 0 else jnp.where(after[r], current_right, collected)
-                    pivots = diagonal if r == 0 else jnp.where(after[r], diagonal, pivots)
-                    inverses.append(inverse)
+                    at = first_column + r
+                    current_left, current_right = row_of(left[tile], r), row_of(right[tile], r)
+                    entries = {c: row_of(columns[tile][c], r) for c in range(at + 1, width)}
+                    for t in range(tile, begin + PANEL):
+                        factor = columns[t][at] * inverse
+                        if t == tile:
+                            factor = jnp.where(below[r], factor, 0.0)
+                        for c in range(at + 1, width):
+                            columns[t][c] = columns[t][c] - factor * entries[c]
+                        left[t] = left[t] - factor * current_left
+                        right[t] = right[t] - factor * current_right
+                    for h in rest:
+                        factor = rest_columns[h][r] * inverse
+                        for c in range(r + 1, SUBLANES):
+                            rest_columns[h][c] = (
+                                rest_columns[h][c] - factor * entries[first_column + c]
+                            )
+                        left[h] = left[h] - factor * current_left
+                        right[h] = right[h] - factor * current_right
+                    if r == 0:
+                        collected, pivots = current_right, diagonal
+                    else:
+                        collected = jnp.where(after[r], current_right, collected)
+                        pivots = jnp.where(after[r], diagonal, pivots)
             finished.append(collected * lax.rsqrt(pivots))
-        if len(rest):
-            solved_left, solved_right = [], []
-            for c in range(width):
-                tile, r = divmod(c, SUBLANES)
-                solved_left.append(row_of(own_left[tile], r) * inverses[c])
-                solved_right.append(row_of(own_right[tile], r) * inverses[c])
-            for h in rest:
-                left[h] = left[h] - sum_tree(
-                    [rest_columns[h][c] * solved_left[c] for c in range(width)]
-                )
-                right[h] = right[h] - sum_tree(
-                    [rest_columns[h][c] * solved_right[c] for c in range(width)]
-                )
     return jnp.concatenate(finished, 0)
 
 

time: 44.2 us -> 44.4 us (level)
  no operation moved by 1% of the time
where the time goes in v5:
time: 44.4 us; the launch traced here: 44.2 us
  Pallas kernels  16.6 us (37%)
  starting transfers between devices  15.3 us (34%)
  waiting for transfers between devices  9.96 us (22%)
  local copies, waits for them, and re-layouts  2.26 us (5%)
    ppermute x11, starting transfers between devices, xor_permute(): return lax.ppermute(value, axis, pairs)  15.3 us
    ppermute x11, waiting for transfers between devices, xor_permute(): return lax.ppermute(value, axis, pairs)  9.96 us
    pallas_call x1, Pallas kernels, slab_basis(): pl.pallas_call(functools.partial(slab_kernel, masks, count, ridge_share *...  9.56 us
    pallas_call x1, Pallas kernels, couplings(): pl.pallas_call(functools.partial(coupling_kernel, tuple(parts), joined, 3...  5.29 us
    pallas_call x1, Pallas kernels, left_of_slab(): pl.pallas_call(left_kernel, in_specs=[smem(), hbm(), hbm()], out_specs=vm...  1.75 us
    unnamed x4, local copies, waits for them, and re-layouts  1.23 us
    dynamic_slice x2, local copies, waits for them, and re-layouts, piece_for(): lax.dynamic_slice_in_dim(values, (place ^ mask) * slab_rows, slab_rows, 1)  1.03 us
  transfers between devices with their start and end apart: 11, of which 6 were waited for; matrix products, arithmetic and copies ran while one was open for 0% of the time, Pallas kernels for 16%

profile of v5, /device:TPU:0, one launch (start us, length us, event | category | flops | bytes accessed | tf_op | source)
XLA Modules:
  0.0 44.2 jit_solution(16720973143629756744)
XLA Ops:
  0.0 1.0 %constant_dynamic-slice_fusion.3 = bf16[64,2048]{1,0:T(8,128)(2,1)S(1)} fusion(bf16[64,8192]{1,0:T(8,128)(2,1)} %param.5, s32[]{:T(128)S(6)} %select_n.12), kind=kLoop, calls=%fused_computation.7 | loop fusion | bytes 524292 | tf_op jit(solution)/shard_map/dynamic_slice | solution.py:562
  1.0 4.1 %collective-permute-start.2 = (bf16[64,2048]{1,0:T(8,128)(2,1)S(1)}, bf16[64,2048]{1,0:T(8,128)(2,1)S(1)}, u32[]{:S(2)}, u32[]{:S(2)}) collective-permute-start(bf16[64,2048]{1,0:T(8,128)(2,1)S(1)} %constant_dynamic-slice_fusion.3), channel_id=1, source_target_pairs={{0,2},{1,3},{2,0},{3,1},{4,6},{5,7},{6,4},{7,5},{8,10},{9,11},{10,... | collective-permute-start | bytes 786440 | tf_op jit(solution)/shard_map/ppermute | solution.py:24
  5.1 0.0 collective-permute-start
  5.1 1.3 %collective-permute-done.ranks_ref = s32[5]{0:T(128)S(1)} collective-permute-done((s32[5]{0:T(128)}, s32[5]{0:T(128)S(1)}, u32[]{:S(2)}, u32[]{:S(2)}) %collective-permute-start) | collective-permute-done | bytes 52 | tf_op jit(solution)/shard_map/ppermute | solution.py:24
  6.3 1.2 %copy-done = bf16[64,8192]{1,0:T(8,128)(2,1)S(1)} copy-done((bf16[64,8192]{1,0:T(8,128)(2,1)S(1)}, bf16[64,8192]{1,0:T(8,128)(2,1)}, u32[]{:S(2)}) %copy-start) | copy-done | bytes 1048600
  7.6 5.3 %couplings.1 = (f32[3,64,128]{2,1,0:T(8,128)S(1)}, bf16[2,64,128]{2,1,0:T(8,128)(2,1)S(1)}, bf16[4,64,128]{2,1,0:T(8,128)(2,1)S(1)}) custom-call(s32[5]{0:T(128)S(1)} %collective-permute-done.ranks_ref, bf16[64,8192]{1,0:T(8,128)(2,1)S(1)} %copy-done, bf16[5,128,8192]{2,1,0:T(8,128)(2,1)} %right_ref.1), custom_call_target="tpu_custom_call" | custom-call | flops 1 | bytes 1 | tf_op jit(solution)/shard_map/couplings/pallas_call | solution.py:135
  12.8 0.3 collective-permute-start.4
  13.1 0.1 constant_dynamic-slice_fusion
  13.2 1.4 %collective-permute-start.3 = (bf16[64,2048]{1,0:T(8,128)(2,1)S(1)}, bf16[64,2048]{1,0:T(8,128)(2,1)S(1)}, u32[]{:S(2)}, u32[]{:S(2)}) collective-permute-start(bf16[64,2048]{1,0:T(8,128)(2,1)S(1)} %get-tuple-element.25), channel_id=1, source_target_pairs={{0,3},{1,2},{2,1},{3,0},{4,7},{5,6},{6,5},{7,4},{8,11},{9,10},{10,... | collective-permute-start | bytes 786440 | tf_op jit(solution)/shard_map/ppermute | solution.py:24
  14.6 0.3 collective-permute-start.1
  14.9 1.6 %collective-permute-start.7 = (f32[64,128]{1,0:T(8,128)S(1)}, f32[64,128]{1,0:T(8,128)S(1)}, u32[]{:S(2)}, u32[]{:S(2)}) collective-permute-start(f32[64,128]{1,0:T(8,128)S(1)} %get-tuple-element.28), channel_id=1, source_target_pairs={{0,8},{4,12},{8,0},{12,4},{16,24},{20,28},{24,16},{28,20},{1,9},{5... | collective-permute-start | bytes 98312 | tf_op jit(solution)/shard_map/ppermute | solution.py:24
  16.5 1.5 %collective-permute-start.6 = (f32[64,128]{1,0:T(8,128)S(1)}, f32[64,128]{1,0:T(8,128)S(1)}, u32[]{:S(2)}, u32[]{:S(2)}) collective-permute-start(f32[64,128]{1,0:T(8,128)S(1)} %get-tuple-element.29), channel_id=1, source_target_pairs={{0,24},{4,28},{8,16},{12,20},{16,8},{20,12},{24,0},{28,4},{1,25},{... | collective-permute-start | bytes 98312 | tf_op jit(solution)/shard_map/ppermute | solution.py:24
  18.0 0.9 %collective-permute-done.7.refs_2_ = f32[64,128]{1,0:T(8,128)S(1)} collective-permute-done((f32[64,128]{1,0:T(8,128)S(1)}, f32[64,128]{1,0:T(8,128)S(1)}, u32[]{:S(2)}, u32[]{:S(2)}) %collective-permute-start.7) | collective-permute-done | bytes 32800 | tf_op jit(solution)/shard_map/ppermute | solution.py:24
  18.9 1.7 %collective-permute-start.5 = (f32[64,128]{1,0:T(8,128)S(1)}, f32[64,128]{1,0:T(8,128)S(1)}, u32[]{:S(2)}, u32[]{:S(2)}) collective-permute-start(f32[64,128]{1,0:T(8,128)S(1)} %get-tuple-element.29), channel_id=1, source_target_pairs={{0,16},{4,20},{8,24},{12,28},{16,0},{20,4},{24,8},{28,12},{1,17},{... | collective-permute-start | bytes 98312 | tf_op jit(solution)/shard_map/ppermute | solution.py:24
  20.6 0.7 %collective-permute-done.6.refs_1_ = f32[64,128]{1,0:T(8,128)S(1)} collective-permute-done((f32[64,128]{1,0:T(8,128)S(1)}, f32[64,128]{1,0:T(8,128)S(1)}, u32[]{:S(2)}, u32[]{:S(2)}) %collective-permute-start.6) | collective-permute-done | bytes 32800 | tf_op jit(solution)/shard_map/ppermute | solution.py:24
  21.3 1.5 %collective-permute-done.5.refs_0_ = f32[64,128]{1,0:T(8,128)S(1)} collective-permute-done((f32[64,128]{1,0:T(8,128)S(1)}, f32[64,128]{1,0:T(8,128)S(1)}, u32[]{:S(2)}, u32[]{:S(2)}) %collective-permute-start.5) | collective-permute-done | bytes 32800 | tf_op jit(solution)/shard_map/ppermute | solution.py:24
  22.9 1.8 %collective-permute-start.8 = (bf16[5,64,128]{2,1,0:T(8,128)(2,1)S(1)}, bf16[5,64,128]{2,1,0:T(8,128)(2,1)S(1)}, u32[]{:S(2)}, u32[]{:S(2)}) collective-permute-start(bf16[5,64,128]{2,1,0:T(8,128)(2,1)S(1)} %get-tuple-element.22), channel_id=1, source_target_pairs={{0,1},{1,0},{2,3},{3,2},{4,5},{5,4},{6,7},{7,6},{8,9},{9,8},{10,11... | collective-permute-start | bytes 245768 | tf_op jit(solution)/shard_map/ppermute | solution.py:24
  24.7 1.7 %collective-permute-start.9 = (bf16[5,64,128]{2,1,0:T(8,128)(2,1)S(1)}, bf16[5,64,128]{2,1,0:T(8,128)(2,1)S(1)}, u32[]{:S(2)}, u32[]{:S(2)}) collective-permute-start(bf16[5,64,128]{2,1,0:T(8,128)(2,1)S(1)} %get-tuple-element.23), channel_id=1, source_target_pairs={{0,2},{1,3},{2,0},{3,1},{4,6},{5,7},{6,4},{7,5},{8,10},{9,11},{10,... | collective-permute-start | bytes 245768 | tf_op jit(solution)/shard_map/ppermute | solution.py:24
  26.4 1.0 %collective-permute-start.10 = (bf16[5,64,128]{2,1,0:T(8,128)(2,1)S(1)}, bf16[5,64,128]{2,1,0:T(8,128)(2,1)S(1)}, u32[]{:S(2)}, u32[]{:S(2)}) collective-permute-start(bf16[5,64,128]{2,1,0:T(8,128)(2,1)S(1)} %get-tuple-element.24), channel_id=1, source_target_pairs={{0,3},{1,2},{2,1},{3,0},{4,7},{5,6},{6,5},{7,4},{8,11},{9,10},{10,... | collective-permute-start | bytes 245768 | tf_op jit(solution)/shard_map/ppermute | solution.py:24
  27.3 1.7 %left_of_slab.1.refs_8_ = bf16[5,128,2048]{2,1,0:T(8,128)(2,1)S(1)} custom-call(s32[1]{0:T(128)} %bitcast.where_ref, bf16[64,2048]{1,0:T(8,128)(2,1)S(1)} %collective-permute-done.2.early_ref.refs_2_, bf16[5,128,8192]{2,1,0:T(8,128)(2,1)} %left_ref.1), custom_call_target="tpu_custom_call" | custom-call | flops 1 | bytes 1 | tf_op jit(solution)/shard_map/left_of_slab/pallas_call | solution.py:163
  29.1 2.9 %collective-permute-done.8.refs_5_ = bf16[5,64,128]{2,1,0:T(8,128)(2,1)S(1)} collective-permute-done((bf16[5,64,128]{2,1,0:T(8,128)(2,1)S(1)}, bf16[5,64,128]{2,1,0:T(8,128)(2,1)S(1)}, u32[]{:S(2)}, u32[]{:S(2)}) %collective-permute-start.8) | collective-permute-done | bytes 81952 | tf_op jit(solution)/shard_map/ppermute | solution.py:24
  32.0 2.6 %collective-permute-done.10.refs_7_ = bf16[5,64,128]{2,1,0:T(8,128)(2,1)S(1)} collective-permute-done((bf16[5,64,128]{2,1,0:T(8,128)(2,1)S(1)}, bf16[5,64,128]{2,1,0:T(8,128)(2,1)S(1)}, u32[]{:S(2)}, u32[]{:S(2)}) %collective-permute-start.10) | collective-permute-done | bytes 81952 | tf_op jit(solution)/shard_map/ppermute | solution.py:24
  34.6 0.0 collective-permute-done.1.refs_1_
  34.6 9.6 %slab_basis.1 = f32[256,2048]{1,0:T(8,128)} custom-call(s32[1]{0:T(128)} %bitcast.where_ref, bf16[64,2048]{1,0:T(8,128)(2,1)S(1)} %get-tuple-element.27.refs_0_, bf16[64,2048]{1,0:T(8,128)(2,1)S(1)} %collective-permute-done.1.refs_1_, bf16[64,2048]{1,0:T(8,128)(2,1)S(1)} %collective-permute-done.2.early_ref.refs_2_, ...), custom_call_target="tpu_custom_call" | custom-call | tf_op jit(solution)/shard_map/slab_basis/pallas_call | solution.py:501
  (9 shorter events, 0.1 us)
Async XLA Ops:
  1.0 25.4 %collective-permute-start.2 = (bf16[64,2048]{1,0:T(8,128)(2,1)S(1)}, bf16[64,2048]{1,0:T(8,128)(2,1)S(1)}, u32[]{:S(2)}, u32[]{:S(2)}) collective-permute-start(bf16[64,2048]{1,0:T(8,128)(2,1)S(1)} %constant_dynamic-slice_fusion.3), channel_id=1, source_target_pairs={{0,2},{1,3},{2,0},{3,1},{4,6},{5,7},{6,4},{7,5},{8,10},{9,11},{10,... | collective-permute-start | bytes 786440 | tf_op jit(solution)/shard_map/ppermute | solution.py:24
  5.1 1.3 %collective-permute-start = (s32[5]{0:T(128)}, s32[5]{0:T(128)S(1)}, u32[]{:S(2)}, u32[]{:S(2)}) collective-permute-start(s32[5]{0:T(128)} %param.9), channel_id=1, source_target_pairs={{0,4},{4,0},{8,12},{12,8},{16,20},{20,16},{24,28},{28,24},{1,5},{5... | collective-permute-start | bytes 68 | tf_op jit(solution)/shard_map/ppermute | solution.py:24
  6.3 1.2 %copy-start = (bf16[64,8192]{1,0:T(8,128)(2,1)S(1)}, bf16[64,8192]{1,0:T(8,128)(2,1)}, u32[]{:S(2)}) copy-start(bf16[64,8192]{1,0:T(8,128)(2,1)} %probes_ref.1) | copy-start | bytes 3145732
  7.6 5.6 %copy-start.1 = (bf16[64,8192]{1,0:T(8,128)(2,1)S(1)}, bf16[64,8192]{1,0:T(8,128)(2,1)}, u32[]{:S(2)}) copy-start(bf16[64,8192]{1,0:T(8,128)(2,1)} %param.5) | copy-start | bytes 3145732
  12.8 2.1 %collective-permute-start.4 = (f32[3,64,128]{2,1,0:T(8,128)S(1)}, f32[3,64,128]{2,1,0:T(8,128)S(1)}, u32[]{:S(2)}, u32[]{:S(2)}) collective-permute-start(f32[3,64,128]{2,1,0:T(8,128)S(1)} %get-tuple-element.18), channel_id=1, source_target_pairs={{0,4},{4,0},{8,12},{12,8},{16,20},{20,16},{24,28},{28,24},{1,5},{5... | collective-permute-start | bytes 294920 | tf_op jit(solution)/shard_map/ppermute | solution.py:24
  13.2 21.4 %collective-permute-start.3 = (bf16[64,2048]{1,0:T(8,128)(2,1)S(1)}, bf16[64,2048]{1,0:T(8,128)(2,1)S(1)}, u32[]{:S(2)}, u32[]{:S(2)}) collective-permute-start(bf16[64,2048]{1,0:T(8,128)(2,1)S(1)} %get-tuple-element.25), channel_id=1, source_target_pairs={{0,3},{1,2},{2,1},{3,0},{4,7},{5,6},{6,5},{7,4},{8,11},{9,10},{10,... | collective-permute-start | bytes 786440 | tf_op jit(solution)/shard_map/ppermute | solution.py:24
  14.6 20.0 %collective-permute-start.1 = (bf16[64,2048]{1,0:T(8,128)(2,1)S(1)}, bf16[64,2048]{1,0:T(8,128)(2,1)S(1)}, u32[]{:S(2)}, u32[]{:S(2)}) collective-permute-start(bf16[64,2048]{1,0:T(8,128)(2,1)S(1)} %get-tuple-element.26), channel_id=1, source_target_pairs={{0,1},{1,0},{2,3},{3,2},{4,5},{5,4},{6,7},{7,6},{8,9},{9,8},{10,11... | collective-permute-start | bytes 786440 | tf_op jit(solution)/shard_map/ppermute | solution.py:24
  14.9 4.0 %collective-permute-start.7 = (f32[64,128]{1,0:T(8,128)S(1)}, f32[64,128]{1,0:T(8,128)S(1)}, u32[]{:S(2)}, u32[]{:S(2)}) collective-permute-start(f32[64,128]{1,0:T(8,128)S(1)} %get-tuple-element.28), channel_id=1, source_target_pairs={{0,8},{4,12},{8,0},{12,4},{16,24},{20,28},{24,16},{28,20},{1,9},{5... | collective-permute-start | bytes 98312 | tf_op jit(solution)/shard_map/ppermute | solution.py:24
  16.5 4.8 %collective-permute-start.6 = (f32[64,128]{1,0:T(8,128)S(1)}, f32[64,128]{1,0:T(8,128)S(1)}, u32[]{:S(2)}, u32[]{:S(2)}) collective-permute-start(f32[64,128]{1,0:T(8,128)S(1)} %get-tuple-element.29), channel_id=1, source_target_pairs={{0,24},{4,28},{8,16},{12,20},{16,8},{20,12},{24,0},{28,4},{1,25},{... | collective-permute-start | bytes 98312 | tf_op jit(solution)/shard_map/ppermute | solution.py:24
  18.9 3.9 %collective-permute-start.5 = (f32[64,128]{1,0:T(8,128)S(1)}, f32[64,128]{1,0:T(8,128)S(1)}, u32[]{:S(2)}, u32[]{:S(2)}) collective-permute-start(f32[64,128]{1,0:T(8,128)S(1)} %get-tuple-element.29), channel_id=1, source_target_pairs={{0,16},{4,20},{8,24},{12,28},{16,0},{20,4},{24,8},{28,12},{1,17},{... | collective-permute-start | bytes 98312 | tf_op jit(solution)/shard_map/ppermute | solution.py:24
  22.9 9.1 %collective-permute-start.8 = (bf16[5,64,128]{2,1,0:T(8,128)(2,1)S(1)}, bf16[5,64,128]{2,1,0:T(8,128)(2,1)S(1)}, u32[]{:S(2)}, u32[]{:S(2)}) collective-permute-start(bf16[5,64,128]{2,1,0:T(8,128)(2,1)S(1)} %get-tuple-element.22), channel_id=1, source_target_pairs={{0,1},{1,0},{2,3},{3,2},{4,5},{5,4},{6,7},{7,6},{8,9},{9,8},{10,11... | collective-permute-start | bytes 245768 | tf_op jit(solution)/shard_map/ppermute | solution.py:24
  24.7 7.3 %collective-permute-start.9 = (bf16[5,64,128]{2,1,0:T(8,128)(2,1)S(1)}, bf16[5,64,128]{2,1,0:T(8,128)(2,1)S(1)}, u32[]{:S(2)}, u32[]{:S(2)}) collective-permute-start(bf16[5,64,128]{2,1,0:T(8,128)(2,1)S(1)} %get-tuple-element.23), channel_id=1, source_target_pairs={{0,2},{1,3},{2,0},{3,1},{4,6},{5,7},{6,4},{7,5},{8,10},{9,11},{10,... | collective-permute-start | bytes 245768 | tf_op jit(solution)/shard_map/ppermute | solution.py:24
  26.4 8.2 %collective-permute-start.10 = (bf16[5,64,128]{2,1,0:T(8,128)(2,1)S(1)}, bf16[5,64,128]{2,1,0:T(8,128)(2,1)S(1)}, u32[]{:S(2)}, u32[]{:S(2)}) collective-permute-start(bf16[5,64,128]{2,1,0:T(8,128)(2,1)S(1)} %get-tuple-element.24), channel_id=1, source_target_pairs={{0,3},{1,2},{2,1},{3,0},{4,7},{5,6},{6,5},{7,4},{8,11},{9,10},{10,... | collective-permute-start | bytes 245768 | tf_op jit(solution)/shard_map/ppermute | solution.py:24

commit v6 on v5

--- a/solution.py
+++ b/solution.py
@@ -41,6 +41,17 @@
 
 
 RANK_STEP = 32
+
+
+def rank_layout(ranks_ref, levels, rank_width):
+    counts, starts = [], []
+    start = 0
+    for level in range(levels):
+        steps = (jnp.clip(ranks_ref[level], 1, rank_width) + RANK_STEP - 1) // RANK_STEP
+        counts.append(pl.multiple_of(steps * RANK_STEP, RANK_STEP))
+        starts.append(pl.multiple_of(start, RANK_STEP))
+        start = start + counts[-1]
+    return counts, starts, start
 
 
 def coupling_kernel(parts, joined, ahead, ranks_ref, probes_ref, right_ref, *refs):
@@ -50,13 +61,7 @@
     local_probes = probe_buffer.shape[0]
     chunks = probe_sems.shape[0]
     chunk = rows_dev // chunks
-    counts, starts = [], []
-    start = 0
-    for level in range(levels):
-        steps = (jnp.clip(ranks_ref[level], 1, rank_width) + RANK_STEP - 1) // RANK_STEP
-        counts.append(pl.multiple_of(steps * RANK_STEP, RANK_STEP))
-        starts.append(pl.multiple_of(start, RANK_STEP))
-        start = start + counts[-1]
+    counts, starts, start = rank_layout(ranks_ref, levels, rank_width)
 
     def columns_of(index):
         return pl.ds(pl.multiple_of(index * chunk, chunk), chunk)
@@ -150,31 +155,60 @@
     )(level_ranks, probes, right_factors)
 
 
-def left_kernel(where_ref, early_ref, left_ref, out_ref, sem):
-    slab_rows = out_ref.shape[2]
-    begin = pl.multiple_of(where_ref[0] * slab_rows, slab_rows)
-    copy = pltpu.make_async_copy(left_ref.at[:, :, pl.ds(begin, slab_rows)], out_ref, sem)
-    copy.start()
-    copy.wait()
-
-
-def left_of_slab(left_factors, early, where, slab_rows):
+def left_kernel(ranks_ref, where_ref, early_ref, left_ref, out_ref, sems):
+    levels, rank_width, _ = left_ref.shape
+    rows, slab_rows = out_ref.shape
+    counts, starts, total = rank_layout(ranks_ref, levels, rank_width)
+    columns = pl.ds(pl.multiple_of(where_ref[0] * slab_rows, slab_rows), slab_rows)
+    copies = [
+        pltpu.make_async_copy(
+            left_ref.at[level, pl.ds(0, counts[level]), columns],
+            out_ref.at[pl.ds(starts[level], counts[level]), :],
+            sems.at[level],
+        )
+        for level in range(levels)
+    ]
+    for copy in copies:
+        copy.start()
+    for begin in range(0, rows, RANK_STEP):
+        @pl.when(begin >= total)
+        def _():
+            out_ref[begin : begin + RANK_STEP, :] = jnp.zeros((RANK_STEP, slab_rows), out_ref.dtype)
+
+    for copy in copies:
+        copy.wait()
+
+
+def left_of_slab(left_factors, level_ranks, early, where, slab_rows):
     levels, rank_width, _ = left_factors.shape
     return pl.pallas_call(
         left_kernel,
-        in_specs=[smem(), hbm(), hbm()],
+        in_specs=[smem(), smem(), hbm(), hbm()],
         out_specs=vmem(),
-        out_shape=jax.ShapeDtypeStruct((levels, rank_width, slab_rows), left_factors.dtype),
-        scratch_shapes=[pltpu.SemaphoreType.DMA],
+        out_shape=jax.ShapeDtypeStruct((levels * rank_width, slab_rows), left_factors.dtype),
+        scratch_shapes=[pltpu.SemaphoreType.DMA((levels,))],
         compiler_params=pltpu.CompilerParams(vmem_limit_bytes=STREAM_VMEM),
         cost_estimate=CHEAP,
         name="left_of_slab",
-    )(where, early, left_factors)
-
-
-def pack_kernel(masks, sources, narrow_parts, where_ref, near_ref, *refs):
-    out_refs = refs[-len(masks) :]
-    term_refs = list(refs[: -len(masks)])
+    )(level_ranks, where, early, left_factors)
+
+
+def pack_kernel(masks, sources, narrow_parts, ranks_ref, where_ref, near_ref, *refs):
+    out_refs, group_ref = refs[-len(masks) - 1 : -1], refs[-1]
+    term_refs = list(refs[: -len(masks) - 1])
+    _, local_probes, rank_width = near_ref.shape
+    levels = len(sources) + len(narrow_parts)
+    _, starts, _ = rank_layout(ranks_ref, levels, rank_width)
+    lane = lax.broadcasted_iota(jnp.int32, (local_probes, rank_width), 1)
+    group_ref[...] = jnp.zeros_like(group_ref)
+
+    def add(level, value, which):
+        group, shift = starts[level] // rank_width, starts[level] % rank_width
+        value = pltpu.roll(value, shift, 1)
+        for i in which:
+            group_ref[i, group] += jnp.where(lane >= shift, value, 0.0)
+            group_ref[i, group + 1] += jnp.where(lane < shift, value, 0.0)
+
     level = 0
     for kind, value in sources:
         if kind == "slot":
@@ -182,28 +216,65 @@
         else:
             terms, term_refs = term_refs[:value], term_refs[value:]
             sibling = sum_tree([term[...] for term in terms])
-        sibling = sibling.astype(jnp.bfloat16)
-        for out_ref in out_refs:
-            out_ref[level] = sibling
+        add(level, sibling, range(len(masks)))
         level += 1
     for parts, values_ref in zip(narrow_parts, term_refs):
-        for mask, out_ref in zip(masks, out_refs):
-            out_ref[level] = values_ref[((where_ref[0] ^ mask) * parts // len(masks)) ^ 1]
+        for i, mask in enumerate(masks):
+            cluster = ((where_ref[0] ^ mask) * parts // len(masks)) ^ 1
+            add(level, values_ref[cluster].astype(jnp.float32), [i])
         level += 1
-
-
-def payloads_of(masks, sources, near, terms, narrow_parts, local, where):
+    whole = levels - 1
+    height = local_probes * RANK_STEP // rank_width
+    wide_lane = lax.broadcasted_iota(jnp.int32, (height, rank_width), 1)
+    for i, out_ref in enumerate(out_refs):
+        for group in range(whole):
+            out_ref[group * local_probes : (group + 1) * local_probes, :] = group_ref[
+                i, group
+            ].astype(jnp.bfloat16)
+        beside = jnp.zeros((height, rank_width), jnp.float32)
+        for piece in range(rank_width // RANK_STEP):
+            part = group_ref[i, whole, piece * height : (piece + 1) * height]
+            moved = pltpu.roll(part, piece * RANK_STEP, 1) if piece else part
+            beside = jnp.where(wide_lane // RANK_STEP == piece, moved, beside)
+        room = out_ref.shape[0] - whole * local_probes
+        if room > height:
+            beside = jnp.concatenate([beside, jnp.zeros((room - height, rank_width))], 0)
+        out_ref[whole * local_probes :, :] = beside.astype(jnp.bfloat16)
+
+
+def unpack(payload_ref, sibling_ref, rows, local_probes):
+    lanes = payload_ref.shape[1]
+    whole = payload_ref.shape[0] // local_probes
+    for group in range(whole):
+        sibling_ref[rows, group * lanes : (group + 1) * lanes] = payload_ref[
+            group * local_probes : (group + 1) * local_probes
+        ]
+    height = local_probes * RANK_STEP // lanes
+    beside = payload_ref[whole * local_probes :].astype(jnp.float32)[:height]
+    lane = lax.broadcasted_iota(jnp.int32, (height, lanes), 1)
+    pieces = []
+    for piece in range(lanes // RANK_STEP):
+        moved = pltpu.roll(beside, lanes - piece * RANK_STEP, 1) if piece else beside
+        pieces.append(jnp.where(lane < RANK_STEP, moved, 0.0))
+    sibling_ref[rows, whole * lanes :] = jnp.concatenate(pieces, 0).astype(jnp.bfloat16)
+
+
+def payloads_of(masks, sources, level_ranks, near, terms, narrow_parts, local, where):
     _, local_probes, rank_width = near.shape
-    shape = (len(sources) + len(local), local_probes, rank_width)
+    levels = len(sources) + len(local)
+    height = (levels - 1) * local_probes + max(16, local_probes * RANK_STEP // rank_width)
     return pl.pallas_call(
         functools.partial(pack_kernel, masks, tuple(sources), tuple(narrow_parts)),
-        in_specs=[smem()] + [vmem()] * (1 + len(terms) + len(local)),
+        in_specs=[smem(), smem()] + [vmem()] * (1 + len(terms) + len(local)),
         out_specs=[vmem()] * len(masks),
-        out_shape=[jax.ShapeDtypeStruct(shape, jnp.bfloat16)] * len(masks),
+        out_shape=[jax.ShapeDtypeStruct((height, rank_width), jnp.bfloat16)] * len(masks),
+        scratch_shapes=[
+            pltpu.VMEM((len(masks), levels + 1, local_probes, rank_width), jnp.float32)
+        ],
         compiler_params=pltpu.CompilerParams(vmem_limit_bytes=VMEM_LIMIT),
         cost_estimate=CHEAP,
         name="payloads",
-    )(where, near, *terms, *local)
+    )(level_ranks, where, near, *terms, *local)
 
 
 HALF = LANES // 2
@@ -376,24 +447,23 @@
         task()
 
 
-def fill_sample(masks, where_ref, piece_refs, payload_refs, left_ref, sample_ref, sibling_ref):
-    levels, local_probes, rank_width = payload_refs[0].shape
-    slab_rows = sample_ref.shape[1]
-    spans = []
-    for mask, payload_ref in zip(masks, payload_refs):
+def fill_sample(
+    masks, where_ref, piece_refs, payload_refs, left_ref, sample_ref, sibling_ref
+):
+    local_probes, slab_rows = piece_refs[0].shape
+    levels, lanes = left_ref.shape[0] // payload_refs[0].shape[1], payload_refs[0].shape[1]
+    for mask, payload_ref, piece_ref in zip(masks, payload_refs, piece_refs):
         start = pl.multiple_of((where_ref[0] ^ mask) * local_probes, local_probes)
-        spans.append(pl.ds(start, local_probes))
-        for level in range(levels):
-            sibling_ref[spans[-1], level * rank_width : (level + 1) * rank_width] = payload_ref[level]
-    for mask, piece_ref in zip(masks, piece_refs):
-        sample_ref[spans[mask], :] = piece_ref[...]
+        rows = pl.ds(start, local_probes)
+        unpack(payload_ref, sibling_ref, rows, local_probes)
+        sample_ref[rows, :] = piece_ref[...]
     chunk = slab_rows // chunks_of(slab_rows)
+
+    ranks = (levels - 1) * lanes + RANK_STEP
     for begin in range(0, slab_rows, chunk):
         columns = slice(begin, begin + chunk)
         update = jnp.dot(
-            sibling_ref[...],
-            left_ref[:, :, columns].reshape(levels * rank_width, chunk),
-            preferred_element_type=jnp.float32,
+            sibling_ref[:, :ranks], left_ref[:ranks, columns], preferred_element_type=jnp.float32
         )
         sample_ref[:, columns] = (sample_ref[:, columns].astype(jnp.float32) - update).astype(
             jnp.bfloat16
@@ -495,7 +565,7 @@
 
 
 def slab_basis(pieces, payloads, left_slab, masks, where, block_rows):
-    levels, rank_width, slab_rows = left_slab.shape
+    ranks, slab_rows = left_slab.shape
     all_probes = len(masks) * pieces[0].shape[0]
     count = slab_rows // block_rows
     return pl.pallas_call(
@@ -508,14 +578,14 @@
             pltpu.VMEM((all_probes, slab_rows), jnp.float32),
             pltpu.SemaphoreType.DMA((all_probes // HALF,)),
         ]
-        + [pltpu.VMEM((all_probes, levels * rank_width), jnp.bfloat16)],
+        + [pltpu.VMEM((all_probes, ranks), jnp.bfloat16)],
         compiler_params=pltpu.CompilerParams(vmem_limit_bytes=VMEM_LIMIT),
         name="slab_basis",
     )(where, *pieces, *payloads, left_slab)
 
 
 def shared_basis(pieces, payloads, left_slab, masks, where, block_rows):
-    levels, rank_width, slab_rows = left_slab.shape
+    ranks, slab_rows = left_slab.shape
     all_probes = len(masks) * pieces[0].shape[0]
     sample, gram = pl.pallas_call(
         functools.partial(sample_kernel, masks),
@@ -525,7 +595,7 @@
             jax.ShapeDtypeStruct((all_probes, slab_rows), jnp.bfloat16),
             jax.ShapeDtypeStruct((all_probes, all_probes), jnp.float32),
         ],
-        scratch_shapes=[pltpu.VMEM((all_probes, levels * rank_width), jnp.bfloat16)],
+        scratch_shapes=[pltpu.VMEM((all_probes, ranks), jnp.bfloat16)],
         compiler_params=pltpu.CompilerParams(vmem_limit_bytes=VMEM_LIMIT),
         name="sample_gram",
     )(where, *pieces, *payloads, left_slab)
@@ -564,12 +634,12 @@
     far = probe_count // 2
     far_piece = piece_for(responses, far)
     pieces = {far: xor_permute(far_piece, "probe", far)}
-    level_ranks, far_piece = lax.optimization_barrier((level_ranks, far_piece))
-    level_ranks = xor_permute(level_ranks, "rows", 1)
+    same_ranks, far_piece = lax.optimization_barrier((level_ranks, far_piece))
+    same_ranks = xor_permute(same_ranks, "rows", 1)
 
     parts = [max(1, 2 ** (l + 1) // rows_count) for l in range(levels_count)]
     wide = [l for l in range(levels_count) if 2 ** (l + 1) <= rows_count]
-    running, *local = couplings(probes, right_factors, level_ranks, parts, len(wide))
+    running, *local = couplings(probes, right_factors, same_ranks, parts, len(wide))
     later_responses, running = lax.optimization_barrier((responses, running))
     near = xor_permute(running, "rows", 1)
     for mask in sorted(range(1, probe_count), key=lambda mask: -mask.bit_length()):
@@ -587,13 +657,13 @@
             terms += [xor_permute(total, "rows", flip ^ low) for low in range(0, flip, 2)]
     narrow_parts = parts[len(wide) :]
 
-    payloads = payloads_of(masks, sources, near, terms, narrow_parts, local, where)
+    payloads = payloads_of(masks, sources, level_ranks, near, terms, narrow_parts, local, where)
     payloads = [payloads[0]] + [
         xor_permute(payloads[mask], "probe", mask) for mask in range(1, probe_count)
     ]
     ordered = [pieces[mask] for mask in masks]
     work = shared_basis if block_rows > slab_rows else slab_basis
-    left_slab = left_of_slab(left_factors, pieces[far], where, slab_rows)
+    left_slab = left_of_slab(left_factors, level_ranks, pieces[far], where, slab_rows)
     return work(ordered, payloads, left_slab, masks, where, block_rows)
 
 

time: 44.4 us -> 43.6 us (0.982)
  waiting for transfers between devices: 9.96 us -> 8.12 us
  Pallas kernels: 16.6 us -> 17.7 us
    ppermute x11, waiting for transfers between devices: 9.96 us -> 8.12 us  [xor_permute(): return lax.ppermute(value, axis, pairs)]
    pallas_call x1, Pallas kernels: 0.04 us -> 0.83 us  [payloads_of(): pl.pallas_call(functools.partial(pack_kernel, masks, tuple(sources), tupl...]
    unnamed x4 -> x6, local copies, waits for them, and re-layouts: 1.23 us -> 1.23 us
  transfers between devices with their start and end apart: 11 -> 11, of which waited for: 6 -> 6; matrix products, arithmetic and copies ran while one was open for 0% -> 0% of each run, Pallas kernels for 16% -> 19%
where the time goes in v6:
time: 43.6 us; the launch traced here: 43.5 us
  Pallas kernels  17.7 us (41%)
  starting transfers between devices  15.3 us (35%)
  waiting for transfers between devices  8.12 us (19%)
  local copies, waits for them, and re-layouts  2.28 us (5%)
    ppermute x11, starting transfers between devices, xor_permute(): return lax.ppermute(value, axis, pairs)  15.3 us
    pallas_call x1, Pallas kernels, slab_basis(): pl.pallas_call(functools.partial(slab_kernel, masks, count, ridge_share *...  9.58 us
    ppermute x11, waiting for transfers between devices, xor_permute(): return lax.ppermute(value, axis, pairs)  8.12 us
    pallas_call x1, Pallas kernels, couplings(): pl.pallas_call(functools.partial(coupling_kernel, tuple(parts), joined, 3...  5.32 us
    pallas_call x1, Pallas kernels, left_of_slab(): pl.pallas_call(left_kernel, in_specs=[smem(), smem(), hbm(), hbm()], out_...  2.01 us
    unnamed x6, local copies, waits for them, and re-layouts  1.23 us
    dynamic_slice x2, local copies, waits for them, and re-layouts, piece_for(): lax.dynamic_slice_in_dim(values, (place ^ mask) * slab_rows, slab_rows, 1)  1.05 us
  transfers between devices with their start and end apart: 11, of which 6 were waited for; matrix products, arithmetic and copies ran while one was open for 0% of the time, Pallas kernels for 19%

profile of v6, /device:TPU:0, one launch (start us, length us, event | category | flops | bytes accessed | tf_op | source)
XLA Modules:
  0.0 43.5 jit_solution(2683394066061317211)
XLA Ops:
  0.0 1.0 %constant_dynamic-slice_fusion.3 = bf16[64,2048]{1,0:T(8,128)(2,1)S(1)} fusion(bf16[64,8192]{1,0:T(8,128)(2,1)} %param.5, s32[]{:T(128)S(6)} %select_n.12), kind=kLoop, calls=%fused_computation.7 | loop fusion | bytes 524292 | tf_op jit(solution)/shard_map/dynamic_slice | solution.py:632
  1.0 4.1 %collective-permute-start.2 = (bf16[64,2048]{1,0:T(8,128)(2,1)S(1)}, bf16[64,2048]{1,0:T(8,128)(2,1)S(1)}, u32[]{:S(2)}, u32[]{:S(2)}) collective-permute-start(bf16[64,2048]{1,0:T(8,128)(2,1)S(1)} %constant_dynamic-slice_fusion.3), channel_id=1, source_target_pairs={{0,2},{1,3},{2,0},{3,1},{4,6},{5,7},{6,4},{7,5},{8,10},{9,11},{10,... | collective-permute-start | bytes 786440 | tf_op jit(solution)/shard_map/ppermute | solution.py:24
  5.1 1.3 %collective-permute-done.ranks_ref = s32[5]{0:T(128)S(1)} collective-permute-done((s32[5]{0:T(128)}, s32[5]{0:T(128)S(1)}, u32[]{:S(2)}, u32[]{:S(2)}) %collective-permute-start) | collective-permute-done | bytes 52 | tf_op jit(solution)/shard_map/ppermute | solution.py:24
  6.3 1.2 %copy-done = bf16[64,8192]{1,0:T(8,128)(2,1)S(1)} copy-done((bf16[64,8192]{1,0:T(8,128)(2,1)S(1)}, bf16[64,8192]{1,0:T(8,128)(2,1)}, u32[]{:S(2)}) %copy-start) | copy-done | bytes 1048600
  7.6 5.3 %couplings.1 = (f32[3,64,128]{2,1,0:T(8,128)S(1)}, bf16[2,64,128]{2,1,0:T(8,128)(2,1)S(1)}, bf16[4,64,128]{2,1,0:T(8,128)(2,1)S(1)}) custom-call(s32[5]{0:T(128)S(1)} %collective-permute-done.ranks_ref, bf16[64,8192]{1,0:T(8,128)(2,1)S(1)} %copy-done, bf16[5,128,8192]{2,1,0:T(8,128)(2,1)} %right_ref.1), custom_call_target="tpu_custom_call" | custom-call | flops 1 | bytes 1 | tf_op jit(solution)/shard_map/couplings/pallas_call | solution.py:140
  12.9 0.3 collective-permute-start.4
  13.2 0.1 constant_dynamic-slice_fusion
  13.3 1.4 %collective-permute-start.3 = (bf16[64,2048]{1,0:T(8,128)(2,1)S(1)}, bf16[64,2048]{1,0:T(8,128)(2,1)S(1)}, u32[]{:S(2)}, u32[]{:S(2)}) collective-permute-start(bf16[64,2048]{1,0:T(8,128)(2,1)S(1)} %get-tuple-element.25), channel_id=1, source_target_pairs={{0,3},{1,2},{2,1},{3,0},{4,7},{5,6},{6,5},{7,4},{8,11},{9,10},{10,... | collective-permute-start | bytes 786440 | tf_op jit(solution)/shard_map/ppermute | solution.py:24
  14.7 0.3 collective-permute-start.1
  15.0 1.6 %collective-permute-start.7 = (f32[64,128]{1,0:T(8,128)S(1)}, f32[64,128]{1,0:T(8,128)S(1)}, u32[]{:S(2)}, u32[]{:S(2)}) collective-permute-start(f32[64,128]{1,0:T(8,128)S(1)} %get-tuple-element.28), channel_id=1, source_target_pairs={{0,8},{4,12},{8,0},{12,4},{16,24},{20,28},{24,16},{28,20},{1,9},{5... | collective-permute-start | bytes 98312 | tf_op jit(solution)/shard_map/ppermute | solution.py:24
  16.5 1.5 %collective-permute-start.6 = (f32[64,128]{1,0:T(8,128)S(1)}, f32[64,128]{1,0:T(8,128)S(1)}, u32[]{:S(2)}, u32[]{:S(2)}) collective-permute-start(f32[64,128]{1,0:T(8,128)S(1)} %get-tuple-element.29), channel_id=1, source_target_pairs={{0,24},{4,28},{8,16},{12,20},{16,8},{20,12},{24,0},{28,4},{1,25},{... | collective-permute-start | bytes 98312 | tf_op jit(solution)/shard_map/ppermute | solution.py:24
  18.0 0.9 %collective-permute-done.7.refs_2_ = f32[64,128]{1,0:T(8,128)S(1)} collective-permute-done((f32[64,128]{1,0:T(8,128)S(1)}, f32[64,128]{1,0:T(8,128)S(1)}, u32[]{:S(2)}, u32[]{:S(2)}) %collective-permute-start.7) | collective-permute-done | bytes 32800 | tf_op jit(solution)/shard_map/ppermute | solution.py:24
  19.0 1.7 %collective-permute-start.5 = (f32[64,128]{1,0:T(8,128)S(1)}, f32[64,128]{1,0:T(8,128)S(1)}, u32[]{:S(2)}, u32[]{:S(2)}) collective-permute-start(f32[64,128]{1,0:T(8,128)S(1)} %get-tuple-element.29), channel_id=1, source_target_pairs={{0,16},{4,20},{8,24},{12,28},{16,0},{20,4},{24,8},{28,12},{1,17},{... | collective-permute-start | bytes 98312 | tf_op jit(solution)/shard_map/ppermute | solution.py:24
  20.6 0.7 %collective-permute-done.6.refs_1_ = f32[64,128]{1,0:T(8,128)S(1)} collective-permute-done((f32[64,128]{1,0:T(8,128)S(1)}, f32[64,128]{1,0:T(8,128)S(1)}, u32[]{:S(2)}, u32[]{:S(2)}) %collective-permute-start.6) | collective-permute-done | bytes 32800 | tf_op jit(solution)/shard_map/ppermute | solution.py:24
  21.4 1.5 %collective-permute-done.5.refs_0_ = f32[64,128]{1,0:T(8,128)S(1)} collective-permute-done((f32[64,128]{1,0:T(8,128)S(1)}, f32[64,128]{1,0:T(8,128)S(1)}, u32[]{:S(2)}, u32[]{:S(2)}) %collective-permute-start.5) | collective-permute-done | bytes 32800 | tf_op jit(solution)/shard_map/ppermute | solution.py:24
  22.9 0.8 %payloads.1 = (bf16[272,128]{1,0:T(8,128)(2,1)S(1)}, bf16[272,128]{1,0:T(8,128)(2,1)S(1)}, bf16[272,128]{1,0:T(8,128)(2,1)S(1)}, bf16[272,128]{1,0:T(8,128)(2,1)S(1)}) custom-call(s32[5]{0:T(128)S(1)} %copy-done.1, s32[1]{0:T(128)} %bitcast.where_ref, f32[3,64,128]{2,1,0:T(8,128)S(1)} %collective-permute-done.4.near_ref, ...), custom_call_target="tpu_custom_call" | custom-call | flops 1 | bytes 1 | tf_op jit(solution)/shard_map/payloads/pallas_call | solution.py:266
  23.7 1.8 %collective-permute-start.8 = (bf16[272,128]{1,0:T(8,128)(2,1)S(1)}, bf16[272,128]{1,0:T(8,128)(2,1)S(1)}, u32[]{:S(2)}, u32[]{:S(2)}) collective-permute-start(bf16[272,128]{1,0:T(8,128)(2,1)S(1)} %get-tuple-element.22), channel_id=1, source_target_pairs={{0,1},{1,0},{2,3},{3,2},{4,5},{5,4},{6,7},{7,6},{8,9},{9,8},{10,11... | collective-permute-start | bytes 208904 | tf_op jit(solution)/shard_map/ppermute | solution.py:24
  25.5 1.7 %collective-permute-start.9 = (bf16[272,128]{1,0:T(8,128)(2,1)S(1)}, bf16[272,128]{1,0:T(8,128)(2,1)S(1)}, u32[]{:S(2)}, u32[]{:S(2)}) collective-permute-start(bf16[272,128]{1,0:T(8,128)(2,1)S(1)} %get-tuple-element.23), channel_id=1, source_target_pairs={{0,2},{1,3},{2,0},{3,1},{4,6},{5,7},{6,4},{7,5},{8,10},{9,11},{10,... | collective-permute-start | bytes 208904 | tf_op jit(solution)/shard_map/ppermute | solution.py:24
  27.2 0.0 collective-permute-done.2.early_ref.refs_2_
  27.2 1.0 %collective-permute-start.10 = (bf16[272,128]{1,0:T(8,128)(2,1)S(1)}, bf16[272,128]{1,0:T(8,128)(2,1)S(1)}, u32[]{:S(2)}, u32[]{:S(2)}) collective-permute-start(bf16[272,128]{1,0:T(8,128)(2,1)S(1)} %get-tuple-element.24), channel_id=1, source_target_pairs={{0,3},{1,2},{2,1},{3,0},{4,7},{5,6},{6,5},{7,4},{8,11},{9,10},{10,... | collective-permute-start | bytes 208904 | tf_op jit(solution)/shard_map/ppermute | solution.py:24
  28.2 2.0 %left_of_slab.1.refs_8_ = bf16[640,2048]{1,0:T(8,128)(2,1)S(1)} custom-call(s32[5]{0:T(128)S(1)} %copy-done.1, s32[1]{0:T(128)} %bitcast.where_ref, bf16[64,2048]{1,0:T(8,128)(2,1)S(1)} %collective-permute-done.2.early_ref.refs_2_, bf16[5,128,8192]{2,1,0:T(8,128)(2,1)} %left_ref.1), custom_call_target="tpu_custom_call" | custom-call | flops 1 | bytes 1 | tf_op jit(solution)/shard_map/left_of_slab/pallas_call | solution.py:184
  30.2 1.3 %collective-permute-done.8.refs_5_ = bf16[272,128]{1,0:T(8,128)(2,1)S(1)} collective-permute-done((bf16[272,128]{1,0:T(8,128)(2,1)S(1)}, bf16[272,128]{1,0:T(8,128)(2,1)S(1)}, u32[]{:S(2)}, u32[]{:S(2)}) %collective-permute-start.8) | collective-permute-done | bytes 69664 | tf_op jit(solution)/shard_map/ppermute | solution.py:24
  31.5 2.4 %collective-permute-done.10.refs_7_ = bf16[272,128]{1,0:T(8,128)(2,1)S(1)} collective-permute-done((bf16[272,128]{1,0:T(8,128)(2,1)S(1)}, bf16[272,128]{1,0:T(8,128)(2,1)S(1)}, u32[]{:S(2)}, u32[]{:S(2)}) %collective-permute-start.10) | collective-permute-done | bytes 69664 | tf_op jit(solution)/shard_map/ppermute | solution.py:24
  33.9 9.6 %slab_basis.1 = f32[256,2048]{1,0:T(8,128)} custom-call(s32[1]{0:T(128)} %bitcast.where_ref, bf16[64,2048]{1,0:T(8,128)(2,1)S(1)} %get-tuple-element.27.refs_0_, bf16[64,2048]{1,0:T(8,128)(2,1)S(1)} %collective-permute-done.1.refs_1_, bf16[64,2048]{1,0:T(8,128)(2,1)S(1)} %collective-permute-done.2.early_ref.refs_2_, ...), custom_call_target="tpu_custom_call" | custom-call | tf_op jit(solution)/shard_map/slab_basis/pallas_call | solution.py:571
  (11 shorter events, 0.0 us)
Async XLA Ops:
  0.0 22.9 %copy-start.1 = (s32[5]{0:T(128)S(1)}, s32[5]{0:T(128)}, u32[]{:S(2)}) copy-start(s32[5]{0:T(128)} %ranks_ref.3) | copy-start | bytes 64
  1.0 26.2 %collective-permute-start.2 = (bf16[64,2048]{1,0:T(8,128)(2,1)S(1)}, bf16[64,2048]{1,0:T(8,128)(2,1)S(1)}, u32[]{:S(2)}, u32[]{:S(2)}) collective-permute-start(bf16[64,2048]{1,0:T(8,128)(2,1)S(1)} %constant_dynamic-slice_fusion.3), channel_id=1, source_target_pairs={{0,2},{1,3},{2,0},{3,1},{4,6},{5,7},{6,4},{7,5},{8,10},{9,11},{10,... | collective-permute-start | bytes 786440 | tf_op jit(solution)/shard_map/ppermute | solution.py:24
  5.1 1.3 %collective-permute-start = (s32[5]{0:T(128)}, s32[5]{0:T(128)S(1)}, u32[]{:S(2)}, u32[]{:S(2)}) collective-permute-start(s32[5]{0:T(128)} %ranks_ref.3), channel_id=1, source_target_pairs={{0,4},{4,0},{8,12},{12,8},{16,20},{20,16},{24,28},{28,24},{1,5},{5... | collective-permute-start | bytes 68 | tf_op jit(solution)/shard_map/ppermute | solution.py:24
  6.3 1.2 %copy-start = (bf16[64,8192]{1,0:T(8,128)(2,1)S(1)}, bf16[64,8192]{1,0:T(8,128)(2,1)}, u32[]{:S(2)}) copy-start(bf16[64,8192]{1,0:T(8,128)(2,1)} %probes_ref.1) | copy-start | bytes 3145732
  7.6 5.6 %copy-start.2 = (bf16[64,8192]{1,0:T(8,128)(2,1)S(1)}, bf16[64,8192]{1,0:T(8,128)(2,1)}, u32[]{:S(2)}) copy-start(bf16[64,8192]{1,0:T(8,128)(2,1)} %param.5) | copy-start | bytes 3145732
  12.9 2.1 %collective-permute-start.4 = (f32[3,64,128]{2,1,0:T(8,128)S(1)}, f32[3,64,128]{2,1,0:T(8,128)S(1)}, u32[]{:S(2)}, u32[]{:S(2)}) collective-permute-start(f32[3,64,128]{2,1,0:T(8,128)S(1)} %get-tuple-element.18), channel_id=1, source_target_pairs={{0,4},{4,0},{8,12},{12,8},{16,20},{20,16},{24,28},{28,24},{1,5},{5... | collective-permute-start | bytes 294920 | tf_op jit(solution)/shard_map/ppermute | solution.py:24
  13.3 20.6 %collective-permute-start.3 = (bf16[64,2048]{1,0:T(8,128)(2,1)S(1)}, bf16[64,2048]{1,0:T(8,128)(2,1)S(1)}, u32[]{:S(2)}, u32[]{:S(2)}) collective-permute-start(bf16[64,2048]{1,0:T(8,128)(2,1)S(1)} %get-tuple-element.25), channel_id=1, source_target_pairs={{0,3},{1,2},{2,1},{3,0},{4,7},{5,6},{6,5},{7,4},{8,11},{9,10},{10,... | collective-permute-start | bytes 786440 | tf_op jit(solution)/shard_map/ppermute | solution.py:24
  14.7 19.2 %collective-permute-start.1 = (bf16[64,2048]{1,0:T(8,128)(2,1)S(1)}, bf16[64,2048]{1,0:T(8,128)(2,1)S(1)}, u32[]{:S(2)}, u32[]{:S(2)}) collective-permute-start(bf16[64,2048]{1,0:T(8,128)(2,1)S(1)} %get-tuple-element.26), channel_id=1, source_target_pairs={{0,1},{1,0},{2,3},{3,2},{4,5},{5,4},{6,7},{7,6},{8,9},{9,8},{10,11... | collective-permute-start | bytes 786440 | tf_op jit(solution)/shard_map/ppermute | solution.py:24
  15.0 4.0 %collective-permute-start.7 = (f32[64,128]{1,0:T(8,128)S(1)}, f32[64,128]{1,0:T(8,128)S(1)}, u32[]{:S(2)}, u32[]{:S(2)}) collective-permute-start(f32[64,128]{1,0:T(8,128)S(1)} %get-tuple-element.28), channel_id=1, source_target_pairs={{0,8},{4,12},{8,0},{12,4},{16,24},{20,28},{24,16},{28,20},{1,9},{5... | collective-permute-start | bytes 98312 | tf_op jit(solution)/shard_map/ppermute | solution.py:24
  16.5 4.8 %collective-permute-start.6 = (f32[64,128]{1,0:T(8,128)S(1)}, f32[64,128]{1,0:T(8,128)S(1)}, u32[]{:S(2)}, u32[]{:S(2)}) collective-permute-start(f32[64,128]{1,0:T(8,128)S(1)} %get-tuple-element.29), channel_id=1, source_target_pairs={{0,24},{4,28},{8,16},{12,20},{16,8},{20,12},{24,0},{28,4},{1,25},{... | collective-permute-start | bytes 98312 | tf_op jit(solution)/shard_map/ppermute | solution.py:24
  19.0 3.9 %collective-permute-start.5 = (f32[64,128]{1,0:T(8,128)S(1)}, f32[64,128]{1,0:T(8,128)S(1)}, u32[]{:S(2)}, u32[]{:S(2)}) collective-permute-start(f32[64,128]{1,0:T(8,128)S(1)} %get-tuple-element.29), channel_id=1, source_target_pairs={{0,16},{4,20},{8,24},{12,28},{16,0},{20,4},{24,8},{28,12},{1,17},{... | collective-permute-start | bytes 98312 | tf_op jit(solution)/shard_map/ppermute | solution.py:24
  23.7 7.8 %collective-permute-start.8 = (bf16[272,128]{1,0:T(8,128)(2,1)S(1)}, bf16[272,128]{1,0:T(8,128)(2,1)S(1)}, u32[]{:S(2)}, u32[]{:S(2)}) collective-permute-start(bf16[272,128]{1,0:T(8,128)(2,1)S(1)} %get-tuple-element.22), channel_id=1, source_target_pairs={{0,1},{1,0},{2,3},{3,2},{4,5},{5,4},{6,7},{7,6},{8,9},{9,8},{10,11... | collective-permute-start | bytes 208904 | tf_op jit(solution)/shard_map/ppermute | solution.py:24
  25.5 6.0 %collective-permute-start.9 = (bf16[272,128]{1,0:T(8,128)(2,1)S(1)}, bf16[272,128]{1,0:T(8,128)(2,1)S(1)}, u32[]{:S(2)}, u32[]{:S(2)}) collective-permute-start(bf16[272,128]{1,0:T(8,128)(2,1)S(1)} %get-tuple-element.23), channel_id=1, source_target_pairs={{0,2},{1,3},{2,0},{3,1},{4,6},{5,7},{6,4},{7,5},{8,10},{9,11},{10,... | collective-permute-start | bytes 208904 | tf_op jit(solution)/shard_map/ppermute | solution.py:24
  27.2 6.7 %collective-permute-start.10 = (bf16[272,128]{1,0:T(8,128)(2,1)S(1)}, bf16[272,128]{1,0:T(8,128)(2,1)S(1)}, u32[]{:S(2)}, u32[]{:S(2)}) collective-permute-start(bf16[272,128]{1,0:T(8,128)(2,1)S(1)} %get-tuple-element.24), channel_id=1, source_target_pairs={{0,3},{1,2},{2,1},{3,0},{4,7},{5,6},{6,5},{7,4},{8,11},{9,10},{10,... | collective-permute-start | bytes 208904 | tf_op jit(solution)/shard_map/ppermute | solution.py:24

commit v7 on v6

--- a/solution.py
+++ b/solution.py
@@ -200,15 +200,14 @@
     levels = len(sources) + len(narrow_parts)
     _, starts, _ = rank_layout(ranks_ref, levels, rank_width)
     lane = lax.broadcasted_iota(jnp.int32, (local_probes, rank_width), 1)
-    group_ref[...] = jnp.zeros_like(group_ref)
-
-    def add(level, value, which):
+
+    def add(level, value, i):
         group, shift = starts[level] // rank_width, starts[level] % rank_width
         value = pltpu.roll(value, shift, 1)
-        for i in which:
-            group_ref[i, group] += jnp.where(lane >= shift, value, 0.0)
-            group_ref[i, group + 1] += jnp.where(lane < shift, value, 0.0)
-
+        group_ref[i, group] += jnp.where(lane >= shift, value, 0.0)
+        group_ref[i, group + 1] += jnp.where(lane < shift, value, 0.0)
+
+    group_ref[0] = jnp.zeros_like(group_ref[0])
     level = 0
     for kind, value in sources:
         if kind == "slot":
@@ -216,12 +215,14 @@
         else:
             terms, term_refs = term_refs[:value], term_refs[value:]
             sibling = sum_tree([term[...] for term in terms])
-        add(level, sibling, range(len(masks)))
+        add(level, sibling, 0)
         level += 1
+    for i in range(1, len(masks)):
+        group_ref[i] = group_ref[0]
     for parts, values_ref in zip(narrow_parts, term_refs):
         for i, mask in enumerate(masks):
             cluster = ((where_ref[0] ^ mask) * parts // len(masks)) ^ 1
-            add(level, values_ref[cluster].astype(jnp.float32), [i])
+            add(level, values_ref[cluster].astype(jnp.float32), i)
         level += 1
     whole = levels - 1
     height = local_probes * RANK_STEP // rank_width
@@ -298,6 +299,7 @@
 
 
 PANEL = 2
+NARROW = 2
 
 
 def eliminate(left, right):
@@ -307,23 +309,18 @@
     after = [row_iota >= r for r in range(SUBLANES)]
     left, right = list(left), list(right)
     finished = []
-    width = SUBLANES * PANEL
-    for begin in range(0, len(left), PANEL):
+    begins = list(range(NARROW)) + list(range(NARROW, len(left), PANEL)) + [len(left)]
+    for begin, end in zip(begins, begins[1:]):
         base = SUBLANES * begin
-        own = range(begin, begin + PANEL)
-        rest = range(begin + PANEL, len(left))
+        width = SUBLANES * (end - begin)
+        own, rest = range(begin, end), range(end, len(left))
         columns = {
             t: [column_of(left[t], base + c, half_start) for c in range(width)] for t in own
         }
+        spread = {h: width if h < end + PANEL else SUBLANES for h in rest}
+        rest_columns = {h: {} for h in rest}
         for tile in own:
             first_column = SUBLANES * (tile - begin)
-            rest_columns = {
-                h: [
-                    column_of(left[h], base + first_column + c, half_start)
-                    for c in range(SUBLANES)
-                ]
-                for h in rest
-            }
             collected = pivots = None
             for row in range(0, SUBLANES, 2):
                 at = first_column + row
@@ -340,7 +337,7 @@
                     at = first_column + r
                     current_left, current_right = row_of(left[tile], r), row_of(right[tile], r)
                     entries = {c: row_of(columns[tile][c], r) for c in range(at + 1, width)}
-                    for t in range(tile, begin + PANEL):
+                    for t in range(tile, end):
                         factor = columns[t][at] * inverse
                         if t == tile:
                             factor = jnp.where(below[r], factor, 0.0)
@@ -349,11 +346,12 @@
                         left[t] = left[t] - factor * current_left
                         right[t] = right[t] - factor * current_right
                     for h in rest:
-                        factor = rest_columns[h][r] * inverse
-                        for c in range(r + 1, SUBLANES):
-                            rest_columns[h][c] = (
-                                rest_columns[h][c] - factor * entries[first_column + c]
-                            )
+                        if at % spread[h] == 0:
+                            for c in range(at, at + spread[h]):
+                                rest_columns[h][c] = column_of(left[h], base + c, half_start)
+                        factor = rest_columns[h][at] * inverse
+                        for c in range(at + 1, (at // spread[h] + 1) * spread[h]):
+                            rest_columns[h][c] = rest_columns[h][c] - factor * entries[c]
                         left[h] = left[h] - factor * current_left
                         right[h] = right[h] - factor * current_right
                     if r == 0:

time: 43.6 us -> 43.3 us (level)
  no operation moved by 1% of the time
where the time goes in v7:
time: 43.3 us; the launch traced here: 43.1 us
  Pallas kernels  17.4 us (40%)
  starting transfers between devices  15.3 us (35%)
  waiting for transfers between devices  8.11 us (19%)
  local copies, waits for them, and re-layouts  2.28 us (5%)
    ppermute x11, starting transfers between devices, xor_permute(): return lax.ppermute(value, axis, pairs)  15.3 us
    pallas_call x1, Pallas kernels, slab_basis(): pl.pallas_call(functools.partial(slab_kernel, masks, count, ridge_share *...  9.24 us
    ppermute x11, waiting for transfers between devices, xor_permute(): return lax.ppermute(value, axis, pairs)  8.11 us
    pallas_call x1, Pallas kernels, couplings(): pl.pallas_call(functools.partial(coupling_kernel, tuple(parts), joined, 3...  5.31 us
    pallas_call x1, Pallas kernels, left_of_slab(): pl.pallas_call(left_kernel, in_specs=[smem(), smem(), hbm(), hbm()], out_...  2 us
    unnamed x6, local copies, waits for them, and re-layouts  1.23 us
    dynamic_slice x2, local copies, waits for them, and re-layouts, piece_for(): lax.dynamic_slice_in_dim(values, (place ^ mask) * slab_rows, slab_rows, 1)  1.05 us
  transfers between devices with their start and end apart: 11, of which 6 were waited for; matrix products, arithmetic and copies ran while one was open for 0% of the time, Pallas kernels for 19%

profile of v7, /device:TPU:0, one launch (start us, length us, event | category | flops | bytes accessed | tf_op | source)
XLA Modules:
  0.0 43.1 jit_solution(7506470779475715500)
XLA Ops:
  0.0 1.0 %constant_dynamic-slice_fusion.3 = bf16[64,2048]{1,0:T(8,128)(2,1)S(1)} fusion(bf16[64,8192]{1,0:T(8,128)(2,1)} %param.5, s32[]{:T(128)S(6)} %select_n.12), kind=kLoop, calls=%fused_computation.7 | loop fusion | bytes 524292 | tf_op jit(solution)/shard_map/dynamic_slice | solution.py:630
  1.0 4.1 %collective-permute-start.2 = (bf16[64,2048]{1,0:T(8,128)(2,1)S(1)}, bf16[64,2048]{1,0:T(8,128)(2,1)S(1)}, u32[]{:S(2)}, u32[]{:S(2)}) collective-permute-start(bf16[64,2048]{1,0:T(8,128)(2,1)S(1)} %constant_dynamic-slice_fusion.3), channel_id=1, source_target_pairs={{0,2},{1,3},{2,0},{3,1},{4,6},{5,7},{6,4},{7,5},{8,10},{9,11},{10,... | collective-permute-start | bytes 786440 | tf_op jit(solution)/shard_map/ppermute | solution.py:24
  5.1 0.0 collective-permute-start
  5.1 1.3 %collective-permute-done.ranks_ref = s32[5]{0:T(128)S(1)} collective-permute-done((s32[5]{0:T(128)}, s32[5]{0:T(128)S(1)}, u32[]{:S(2)}, u32[]{:S(2)}) %collective-permute-start) | collective-permute-done | bytes 52 | tf_op jit(solution)/shard_map/ppermute | solution.py:24
  6.3 1.2 %copy-done = bf16[64,8192]{1,0:T(8,128)(2,1)S(1)} copy-done((bf16[64,8192]{1,0:T(8,128)(2,1)S(1)}, bf16[64,8192]{1,0:T(8,128)(2,1)}, u32[]{:S(2)}) %copy-start) | copy-done | bytes 1048600
  7.6 5.3 %couplings.1 = (f32[3,64,128]{2,1,0:T(8,128)S(1)}, bf16[2,64,128]{2,1,0:T(8,128)(2,1)S(1)}, bf16[4,64,128]{2,1,0:T(8,128)(2,1)S(1)}) custom-call(s32[5]{0:T(128)S(1)} %collective-permute-done.ranks_ref, bf16[64,8192]{1,0:T(8,128)(2,1)S(1)} %copy-done, bf16[5,128,8192]{2,1,0:T(8,128)(2,1)} %right_ref.1), custom_call_target="tpu_custom_call" | custom-call | flops 1 | bytes 1 | tf_op jit(solution)/shard_map/couplings/pallas_call | solution.py:140
  12.9 0.3 collective-permute-start.4
  13.2 0.1 constant_dynamic-slice_fusion
  13.2 1.4 %collective-permute-start.3 = (bf16[64,2048]{1,0:T(8,128)(2,1)S(1)}, bf16[64,2048]{1,0:T(8,128)(2,1)S(1)}, u32[]{:S(2)}, u32[]{:S(2)}) collective-permute-start(bf16[64,2048]{1,0:T(8,128)(2,1)S(1)} %get-tuple-element.25), channel_id=1, source_target_pairs={{0,3},{1,2},{2,1},{3,0},{4,7},{5,6},{6,5},{7,4},{8,11},{9,10},{10,... | collective-permute-start | bytes 786440 | tf_op jit(solution)/shard_map/ppermute | solution.py:24
  14.7 0.3 collective-permute-start.1
  15.0 1.6 %collective-permute-start.7 = (f32[64,128]{1,0:T(8,128)S(1)}, f32[64,128]{1,0:T(8,128)S(1)}, u32[]{:S(2)}, u32[]{:S(2)}) collective-permute-start(f32[64,128]{1,0:T(8,128)S(1)} %get-tuple-element.28), channel_id=1, source_target_pairs={{0,8},{4,12},{8,0},{12,4},{16,24},{20,28},{24,16},{28,20},{1,9},{5... | collective-permute-start | bytes 98312 | tf_op jit(solution)/shard_map/ppermute | solution.py:24
  16.5 1.5 %collective-permute-start.6 = (f32[64,128]{1,0:T(8,128)S(1)}, f32[64,128]{1,0:T(8,128)S(1)}, u32[]{:S(2)}, u32[]{:S(2)}) collective-permute-start(f32[64,128]{1,0:T(8,128)S(1)} %get-tuple-element.29), channel_id=1, source_target_pairs={{0,24},{4,28},{8,16},{12,20},{16,8},{20,12},{24,0},{28,4},{1,25},{... | collective-permute-start | bytes 98312 | tf_op jit(solution)/shard_map/ppermute | solution.py:24
  18.0 0.9 %collective-permute-done.7.refs_2_ = f32[64,128]{1,0:T(8,128)S(1)} collective-permute-done((f32[64,128]{1,0:T(8,128)S(1)}, f32[64,128]{1,0:T(8,128)S(1)}, u32[]{:S(2)}, u32[]{:S(2)}) %collective-permute-start.7) | collective-permute-done | bytes 32800 | tf_op jit(solution)/shard_map/ppermute | solution.py:24
  19.0 1.7 %collective-permute-start.5 = (f32[64,128]{1,0:T(8,128)S(1)}, f32[64,128]{1,0:T(8,128)S(1)}, u32[]{:S(2)}, u32[]{:S(2)}) collective-permute-start(f32[64,128]{1,0:T(8,128)S(1)} %get-tuple-element.29), channel_id=1, source_target_pairs={{0,16},{4,20},{8,24},{12,28},{16,0},{20,4},{24,8},{28,12},{1,17},{... | collective-permute-start | bytes 98312 | tf_op jit(solution)/shard_map/ppermute | solution.py:24
  20.6 0.7 %collective-permute-done.6.refs_1_ = f32[64,128]{1,0:T(8,128)S(1)} collective-permute-done((f32[64,128]{1,0:T(8,128)S(1)}, f32[64,128]{1,0:T(8,128)S(1)}, u32[]{:S(2)}, u32[]{:S(2)}) %collective-permute-start.6) | collective-permute-done | bytes 32800 | tf_op jit(solution)/shard_map/ppermute | solution.py:24
  21.4 1.5 %collective-permute-done.5.refs_0_ = f32[64,128]{1,0:T(8,128)S(1)} collective-permute-done((f32[64,128]{1,0:T(8,128)S(1)}, f32[64,128]{1,0:T(8,128)S(1)}, u32[]{:S(2)}, u32[]{:S(2)}) %collective-permute-start.5) | collective-permute-done | bytes 32800 | tf_op jit(solution)/shard_map/ppermute | solution.py:24
  22.9 0.8 %payloads.1 = (bf16[272,128]{1,0:T(8,128)(2,1)S(1)}, bf16[272,128]{1,0:T(8,128)(2,1)S(1)}, bf16[272,128]{1,0:T(8,128)(2,1)S(1)}, bf16[272,128]{1,0:T(8,128)(2,1)S(1)}) custom-call(s32[5]{0:T(128)S(1)} %copy-done.1, s32[1]{0:T(128)} %bitcast.where_ref, f32[3,64,128]{2,1,0:T(8,128)S(1)} %collective-permute-done.4.near_ref, ...), custom_call_target="tpu_custom_call" | custom-call | flops 1 | bytes 1 | tf_op jit(solution)/shard_map/payloads/pallas_call | solution.py:267
  23.7 1.8 %collective-permute-start.8 = (bf16[272,128]{1,0:T(8,128)(2,1)S(1)}, bf16[272,128]{1,0:T(8,128)(2,1)S(1)}, u32[]{:S(2)}, u32[]{:S(2)}) collective-permute-start(bf16[272,128]{1,0:T(8,128)(2,1)S(1)} %get-tuple-element.22), channel_id=1, source_target_pairs={{0,1},{1,0},{2,3},{3,2},{4,5},{5,4},{6,7},{7,6},{8,9},{9,8},{10,11... | collective-permute-start | bytes 208904 | tf_op jit(solution)/shard_map/ppermute | solution.py:24
  25.5 1.7 %collective-permute-start.9 = (bf16[272,128]{1,0:T(8,128)(2,1)S(1)}, bf16[272,128]{1,0:T(8,128)(2,1)S(1)}, u32[]{:S(2)}, u32[]{:S(2)}) collective-permute-start(bf16[272,128]{1,0:T(8,128)(2,1)S(1)} %get-tuple-element.23), channel_id=1, source_target_pairs={{0,2},{1,3},{2,0},{3,1},{4,6},{5,7},{6,4},{7,5},{8,10},{9,11},{10,... | collective-permute-start | bytes 208904 | tf_op jit(solution)/shard_map/ppermute | solution.py:24
  27.2 1.0 %collective-permute-start.10 = (bf16[272,128]{1,0:T(8,128)(2,1)S(1)}, bf16[272,128]{1,0:T(8,128)(2,1)S(1)}, u32[]{:S(2)}, u32[]{:S(2)}) collective-permute-start(bf16[272,128]{1,0:T(8,128)(2,1)S(1)} %get-tuple-element.24), channel_id=1, source_target_pairs={{0,3},{1,2},{2,1},{3,0},{4,7},{5,6},{6,5},{7,4},{8,11},{9,10},{10,... | collective-permute-start | bytes 208904 | tf_op jit(solution)/shard_map/ppermute | solution.py:24
  28.2 2.0 %left_of_slab.1.refs_8_ = bf16[640,2048]{1,0:T(8,128)(2,1)S(1)} custom-call(s32[5]{0:T(128)S(1)} %copy-done.1, s32[1]{0:T(128)} %bitcast.where_ref, bf16[64,2048]{1,0:T(8,128)(2,1)S(1)} %collective-permute-done.2.early_ref.refs_2_, bf16[5,128,8192]{2,1,0:T(8,128)(2,1)} %left_ref.1), custom_call_target="tpu_custom_call" | custom-call | flops 1 | bytes 1 | tf_op jit(solution)/shard_map/left_of_slab/pallas_call | solution.py:184
  30.2 1.3 %collective-permute-done.8.refs_5_ = bf16[272,128]{1,0:T(8,128)(2,1)S(1)} collective-permute-done((bf16[272,128]{1,0:T(8,128)(2,1)S(1)}, bf16[272,128]{1,0:T(8,128)(2,1)S(1)}, u32[]{:S(2)}, u32[]{:S(2)}) %collective-permute-start.8) | collective-permute-done | bytes 69664 | tf_op jit(solution)/shard_map/ppermute | solution.py:24
  31.5 2.4 %collective-permute-done.10.refs_7_ = bf16[272,128]{1,0:T(8,128)(2,1)S(1)} collective-permute-done((bf16[272,128]{1,0:T(8,128)(2,1)S(1)}, bf16[272,128]{1,0:T(8,128)(2,1)S(1)}, u32[]{:S(2)}, u32[]{:S(2)}) %collective-permute-start.10) | collective-permute-done | bytes 69664 | tf_op jit(solution)/shard_map/ppermute | solution.py:24
  33.9 9.2 %slab_basis.1 = f32[256,2048]{1,0:T(8,128)} custom-call(s32[1]{0:T(128)} %bitcast.where_ref, bf16[64,2048]{1,0:T(8,128)(2,1)S(1)} %get-tuple-element.27.refs_0_, bf16[64,2048]{1,0:T(8,128)(2,1)S(1)} %collective-permute-done.1.refs_1_, bf16[64,2048]{1,0:T(8,128)(2,1)S(1)} %collective-permute-done.2.early_ref.refs_2_, ...), custom_call_target="tpu_custom_call" | custom-call | tf_op jit(solution)/shard_map/slab_basis/pallas_call | solution.py:569
  (11 shorter events, 0.0 us)
Async XLA Ops:
  0.0 22.9 %copy-start.1 = (s32[5]{0:T(128)S(1)}, s32[5]{0:T(128)}, u32[]{:S(2)}) copy-start(s32[5]{0:T(128)} %ranks_ref.3) | copy-start | bytes 64
  1.0 26.2 %collective-permute-start.2 = (bf16[64,2048]{1,0:T(8,128)(2,1)S(1)}, bf16[64,2048]{1,0:T(8,128)(2,1)S(1)}, u32[]{:S(2)}, u32[]{:S(2)}) collective-permute-start(bf16[64,2048]{1,0:T(8,128)(2,1)S(1)} %constant_dynamic-slice_fusion.3), channel_id=1, source_target_pairs={{0,2},{1,3},{2,0},{3,1},{4,6},{5,7},{6,4},{7,5},{8,10},{9,11},{10,... | collective-permute-start | bytes 786440 | tf_op jit(solution)/shard_map/ppermute | solution.py:24
  5.1 1.3 %collective-permute-start = (s32[5]{0:T(128)}, s32[5]{0:T(128)S(1)}, u32[]{:S(2)}, u32[]{:S(2)}) collective-permute-start(s32[5]{0:T(128)} %ranks_ref.3), channel_id=1, source_target_pairs={{0,4},{4,0},{8,12},{12,8},{16,20},{20,16},{24,28},{28,24},{1,5},{5... | collective-permute-start | bytes 68 | tf_op jit(solution)/shard_map/ppermute | solution.py:24
  6.3 1.2 %copy-start = (bf16[64,8192]{1,0:T(8,128)(2,1)S(1)}, bf16[64,8192]{1,0:T(8,128)(2,1)}, u32[]{:S(2)}) copy-start(bf16[64,8192]{1,0:T(8,128)(2,1)} %probes_ref.1) | copy-start | bytes 3145732
  7.6 5.6 %copy-start.2 = (bf16[64,8192]{1,0:T(8,128)(2,1)S(1)}, bf16[64,8192]{1,0:T(8,128)(2,1)}, u32[]{:S(2)}) copy-start(bf16[64,8192]{1,0:T(8,128)(2,1)} %param.5) | copy-start | bytes 3145732
  12.9 2.1 %collective-permute-start.4 = (f32[3,64,128]{2,1,0:T(8,128)S(1)}, f32[3,64,128]{2,1,0:T(8,128)S(1)}, u32[]{:S(2)}, u32[]{:S(2)}) collective-permute-start(f32[3,64,128]{2,1,0:T(8,128)S(1)} %get-tuple-element.18), channel_id=1, source_target_pairs={{0,4},{4,0},{8,12},{12,8},{16,20},{20,16},{24,28},{28,24},{1,5},{5... | collective-permute-start | bytes 294920 | tf_op jit(solution)/shard_map/ppermute | solution.py:24
  13.2 20.6 %collective-permute-start.3 = (bf16[64,2048]{1,0:T(8,128)(2,1)S(1)}, bf16[64,2048]{1,0:T(8,128)(2,1)S(1)}, u32[]{:S(2)}, u32[]{:S(2)}) collective-permute-start(bf16[64,2048]{1,0:T(8,128)(2,1)S(1)} %get-tuple-element.25), channel_id=1, source_target_pairs={{0,3},{1,2},{2,1},{3,0},{4,7},{5,6},{6,5},{7,4},{8,11},{9,10},{10,... | collective-permute-start | bytes 786440 | tf_op jit(solution)/shard_map/ppermute | solution.py:24
  14.7 19.2 %collective-permute-start.1 = (bf16[64,2048]{1,0:T(8,128)(2,1)S(1)}, bf16[64,2048]{1,0:T(8,128)(2,1)S(1)}, u32[]{:S(2)}, u32[]{:S(2)}) collective-permute-start(bf16[64,2048]{1,0:T(8,128)(2,1)S(1)} %get-tuple-element.26), channel_id=1, source_target_pairs={{0,1},{1,0},{2,3},{3,2},{4,5},{5,4},{6,7},{7,6},{8,9},{9,8},{10,11... | collective-permute-start | bytes 786440 | tf_op jit(solution)/shard_map/ppermute | solution.py:24
  15.0 4.0 %collective-permute-start.7 = (f32[64,128]{1,0:T(8,128)S(1)}, f32[64,128]{1,0:T(8,128)S(1)}, u32[]{:S(2)}, u32[]{:S(2)}) collective-permute-start(f32[64,128]{1,0:T(8,128)S(1)} %get-tuple-element.28), channel_id=1, source_target_pairs={{0,8},{4,12},{8,0},{12,4},{16,24},{20,28},{24,16},{28,20},{1,9},{5... | collective-permute-start | bytes 98312 | tf_op jit(solution)/shard_map/ppermute | solution.py:24
  16.5 4.8 %collective-permute-start.6 = (f32[64,128]{1,0:T(8,128)S(1)}, f32[64,128]{1,0:T(8,128)S(1)}, u32[]{:S(2)}, u32[]{:S(2)}) collective-permute-start(f32[64,128]{1,0:T(8,128)S(1)} %get-tuple-element.29), channel_id=1, source_target_pairs={{0,24},{4,28},{8,16},{12,20},{16,8},{20,12},{24,0},{28,4},{1,25},{... | collective-permute-start | bytes 98312 | tf_op jit(solution)/shard_map/ppermute | solution.py:24
  19.0 3.9 %collective-permute-start.5 = (f32[64,128]{1,0:T(8,128)S(1)}, f32[64,128]{1,0:T(8,128)S(1)}, u32[]{:S(2)}, u32[]{:S(2)}) collective-permute-start(f32[64,128]{1,0:T(8,128)S(1)} %get-tuple-element.29), channel_id=1, source_target_pairs={{0,16},{4,20},{8,24},{12,28},{16,0},{20,4},{24,8},{28,12},{1,17},{... | collective-permute-start | bytes 98312 | tf_op jit(solution)/shard_map/ppermute | solution.py:24
  23.7 7.8 %collective-permute-start.8 = (bf16[272,128]{1,0:T(8,128)(2,1)S(1)}, bf16[272,128]{1,0:T(8,128)(2,1)S(1)}, u32[]{:S(2)}, u32[]{:S(2)}) collective-permute-start(bf16[272,128]{1,0:T(8,128)(2,1)S(1)} %get-tuple-element.22), channel_id=1, source_target_pairs={{0,1},{1,0},{2,3},{3,2},{4,5},{5,4},{6,7},{7,6},{8,9},{9,8},{10,11... | collective-permute-start | bytes 208904 | tf_op jit(solution)/shard_map/ppermute | solution.py:24
  25.5 6.0 %collective-permute-start.9 = (bf16[272,128]{1,0:T(8,128)(2,1)S(1)}, bf16[272,128]{1,0:T(8,128)(2,1)S(1)}, u32[]{:S(2)}, u32[]{:S(2)}) collective-permute-start(bf16[272,128]{1,0:T(8,128)(2,1)S(1)} %get-tuple-element.23), channel_id=1, source_target_pairs={{0,2},{1,3},{2,0},{3,1},{4,6},{5,7},{6,4},{7,5},{8,10},{9,11},{10,... | collective-permute-start | bytes 208904 | tf_op jit(solution)/shard_map/ppermute | solution.py:24
  27.2 6.7 %collective-permute-start.10 = (bf16[272,128]{1,0:T(8,128)(2,1)S(1)}, bf16[272,128]{1,0:T(8,128)(2,1)S(1)}, u32[]{:S(2)}, u32[]{:S(2)}) collective-permute-start(bf16[272,128]{1,0:T(8,128)(2,1)S(1)} %get-tuple-element.24), channel_id=1, source_target_pairs={{0,3},{1,2},{2,1},{3,0},{4,7},{5,6},{6,5},{7,4},{8,11},{9,10},{10,... | collective-permute-start | bytes 208904 | tf_op jit(solution)/shard_map/ppermute | solution.py:24

commit v8 on v7

--- a/solution.py
+++ b/solution.py
@@ -500,12 +500,16 @@
         for which, sample in enumerate(samples):
             factor = jnp.concatenate([factors[which] for factors in held], 0)
             high = factor.astype(jnp.bfloat16)
-            low = (factor - high.astype(jnp.float32)).astype(jnp.bfloat16)
-            both = jnp.dot(
-                jnp.concatenate([high, low], 0), sample, preferred_element_type=jnp.float32
+            rest = factor - high.astype(jnp.float32)
+            middle = rest.astype(jnp.bfloat16)
+            low = (rest - middle.astype(jnp.float32)).astype(jnp.bfloat16)
+            terms = jnp.dot(
+                jnp.concatenate([high, middle, low], 0), sample, preferred_element_type=jnp.float32
             )
             columns = slice(which * piece_rows, (which + 1) * piece_rows)
-            buffer_ref[at, columns] = both[:height] + both[height:]
+            buffer_ref[at, columns] = terms[:height] + (
+                terms[height : 2 * height] + terms[2 * height :]
+            )
             copies.append(
                 pltpu.make_async_copy(
                     buffer_ref.at[at, columns], out_ref.at[at, columns], sems.at[len(copies)]

time: 43.3 us -> 43.8 us (1.012)
  transfers between devices with their start and end apart: 11 -> 11, of which waited for: 6 -> 6; matrix products, arithmetic and copies ran while one was open for 0% -> 0% of each run, Pallas kernels for 19% -> 20%
where the time goes in v8:
time: 43.8 us; the launch traced here: 43.3 us
  Pallas kernels  17.8 us (41%)
  starting transfers between devices  15.3 us (35%)
  waiting for transfers between devices  7.93 us (18%)
  local copies, waits for them, and re-layouts  2.28 us (5%)
    ppermute x11, starting transfers between devices, xor_permute(): return lax.ppermute(value, axis, pairs)  15.3 us
    pallas_call x1, Pallas kernels, slab_basis(): pl.pallas_call(functools.partial(slab_kernel, masks, count, ridge_share *...  9.32 us
    ppermute x11, waiting for transfers between devices, xor_permute(): return lax.ppermute(value, axis, pairs)  7.93 us
    pallas_call x1, Pallas kernels, couplings(): pl.pallas_call(functools.partial(coupling_kernel, tuple(parts), joined, 3...  5.45 us
    pallas_call x1, Pallas kernels, left_of_slab(): pl.pallas_call(left_kernel, in_specs=[smem(), smem(), hbm(), hbm()], out_...  2.15 us
    unnamed x6, local copies, waits for them, and re-layouts  1.23 us
    dynamic_slice x2, local copies, waits for them, and re-layouts, piece_for(): lax.dynamic_slice_in_dim(values, (place ^ mask) * slab_rows, slab_rows, 1)  1.05 us
  transfers between devices with their start and end apart: 11, of which 6 were waited for; matrix products, arithmetic and copies ran while one was open for 0% of the time, Pallas kernels for 20%

profile of v8, /device:TPU:0, one launch (start us, length us, event | category | flops | bytes accessed | tf_op | source)
XLA Modules:
  0.0 43.3 jit_solution(17924751386125334661)
XLA Ops:
  0.0 1.0 %constant_dynamic-slice_fusion.3 = bf16[64,2048]{1,0:T(8,128)(2,1)S(1)} fusion(bf16[64,8192]{1,0:T(8,128)(2,1)} %param.5, s32[]{:T(128)S(6)} %select_n.12), kind=kLoop, calls=%fused_computation.7 | loop fusion | bytes 524292 | tf_op jit(solution)/shard_map/dynamic_slice | solution.py:634
  1.0 4.1 %collective-permute-start.2 = (bf16[64,2048]{1,0:T(8,128)(2,1)S(1)}, bf16[64,2048]{1,0:T(8,128)(2,1)S(1)}, u32[]{:S(2)}, u32[]{:S(2)}) collective-permute-start(bf16[64,2048]{1,0:T(8,128)(2,1)S(1)} %constant_dynamic-slice_fusion.3), channel_id=1, source_target_pairs={{0,2},{1,3},{2,0},{3,1},{4,6},{5,7},{6,4},{7,5},{8,10},{9,11},{10,... | collective-permute-start | bytes 786440 | tf_op jit(solution)/shard_map/ppermute | solution.py:24
  5.1 0.0 collective-permute-start
  5.1 1.3 %collective-permute-done.ranks_ref = s32[5]{0:T(128)S(1)} collective-permute-done((s32[5]{0:T(128)}, s32[5]{0:T(128)S(1)}, u32[]{:S(2)}, u32[]{:S(2)}) %collective-permute-start) | collective-permute-done | bytes 52 | tf_op jit(solution)/shard_map/ppermute | solution.py:24
  6.3 1.2 %copy-done = bf16[64,8192]{1,0:T(8,128)(2,1)S(1)} copy-done((bf16[64,8192]{1,0:T(8,128)(2,1)S(1)}, bf16[64,8192]{1,0:T(8,128)(2,1)}, u32[]{:S(2)}) %copy-start) | copy-done | bytes 1048600
  7.6 5.5 %couplings.1 = (f32[3,64,128]{2,1,0:T(8,128)S(1)}, bf16[2,64,128]{2,1,0:T(8,128)(2,1)S(1)}, bf16[4,64,128]{2,1,0:T(8,128)(2,1)S(1)}) custom-call(s32[5]{0:T(128)S(1)} %collective-permute-done.ranks_ref, bf16[64,8192]{1,0:T(8,128)(2,1)S(1)} %copy-done, bf16[5,128,8192]{2,1,0:T(8,128)(2,1)} %right_ref.1), custom_call_target="tpu_custom_call" | custom-call | flops 1 | bytes 1 | tf_op jit(solution)/shard_map/couplings/pallas_call | solution.py:140
  13.0 0.3 collective-permute-start.4
  13.3 0.1 constant_dynamic-slice_fusion
  13.4 1.4 %collective-permute-start.3 = (bf16[64,2048]{1,0:T(8,128)(2,1)S(1)}, bf16[64,2048]{1,0:T(8,128)(2,1)S(1)}, u32[]{:S(2)}, u32[]{:S(2)}) collective-permute-start(bf16[64,2048]{1,0:T(8,128)(2,1)S(1)} %get-tuple-element.25), channel_id=1, source_target_pairs={{0,3},{1,2},{2,1},{3,0},{4,7},{5,6},{6,5},{7,4},{8,11},{9,10},{10,... | collective-permute-start | bytes 786440 | tf_op jit(solution)/shard_map/ppermute | solution.py:24
  14.8 0.3 collective-permute-start.1
  15.1 1.6 %collective-permute-start.7 = (f32[64,128]{1,0:T(8,128)S(1)}, f32[64,128]{1,0:T(8,128)S(1)}, u32[]{:S(2)}, u32[]{:S(2)}) collective-permute-start(f32[64,128]{1,0:T(8,128)S(1)} %get-tuple-element.28), channel_id=1, source_target_pairs={{0,8},{4,12},{8,0},{12,4},{16,24},{20,28},{24,16},{28,20},{1,9},{5... | collective-permute-start | bytes 98312 | tf_op jit(solution)/shard_map/ppermute | solution.py:24
  16.7 1.5 %collective-permute-start.6 = (f32[64,128]{1,0:T(8,128)S(1)}, f32[64,128]{1,0:T(8,128)S(1)}, u32[]{:S(2)}, u32[]{:S(2)}) collective-permute-start(f32[64,128]{1,0:T(8,128)S(1)} %get-tuple-element.29), channel_id=1, source_target_pairs={{0,24},{4,28},{8,16},{12,20},{16,8},{20,12},{24,0},{28,4},{1,25},{... | collective-permute-start | bytes 98312 | tf_op jit(solution)/shard_map/ppermute | solution.py:24
  18.2 0.9 %collective-permute-done.7.refs_2_ = f32[64,128]{1,0:T(8,128)S(1)} collective-permute-done((f32[64,128]{1,0:T(8,128)S(1)}, f32[64,128]{1,0:T(8,128)S(1)}, u32[]{:S(2)}, u32[]{:S(2)}) %collective-permute-start.7) | collective-permute-done | bytes 32800 | tf_op jit(solution)/shard_map/ppermute | solution.py:24
  19.1 1.7 %collective-permute-start.5 = (f32[64,128]{1,0:T(8,128)S(1)}, f32[64,128]{1,0:T(8,128)S(1)}, u32[]{:S(2)}, u32[]{:S(2)}) collective-permute-start(f32[64,128]{1,0:T(8,128)S(1)} %get-tuple-element.29), channel_id=1, source_target_pairs={{0,16},{4,20},{8,24},{12,28},{16,0},{20,4},{24,8},{28,12},{1,17},{... | collective-permute-start | bytes 98312 | tf_op jit(solution)/shard_map/ppermute | solution.py:24
  20.8 0.7 %collective-permute-done.6.refs_1_ = f32[64,128]{1,0:T(8,128)S(1)} collective-permute-done((f32[64,128]{1,0:T(8,128)S(1)}, f32[64,128]{1,0:T(8,128)S(1)}, u32[]{:S(2)}, u32[]{:S(2)}) %collective-permute-start.6) | collective-permute-done | bytes 32800 | tf_op jit(solution)/shard_map/ppermute | solution.py:24
  21.5 1.5 %collective-permute-done.5.refs_0_ = f32[64,128]{1,0:T(8,128)S(1)} collective-permute-done((f32[64,128]{1,0:T(8,128)S(1)}, f32[64,128]{1,0:T(8,128)S(1)}, u32[]{:S(2)}, u32[]{:S(2)}) %collective-permute-start.5) | collective-permute-done | bytes 32800 | tf_op jit(solution)/shard_map/ppermute | solution.py:24
  23.0 0.8 %payloads.1 = (bf16[272,128]{1,0:T(8,128)(2,1)S(1)}, bf16[272,128]{1,0:T(8,128)(2,1)S(1)}, bf16[272,128]{1,0:T(8,128)(2,1)S(1)}, bf16[272,128]{1,0:T(8,128)(2,1)S(1)}) custom-call(s32[5]{0:T(128)S(1)} %copy-done.1, s32[1]{0:T(128)} %bitcast.where_ref, f32[3,64,128]{2,1,0:T(8,128)S(1)} %collective-permute-done.4.near_ref, ...), custom_call_target="tpu_custom_call" | custom-call | flops 1 | bytes 1 | tf_op jit(solution)/shard_map/payloads/pallas_call | solution.py:267
  23.9 1.8 %collective-permute-start.8 = (bf16[272,128]{1,0:T(8,128)(2,1)S(1)}, bf16[272,128]{1,0:T(8,128)(2,1)S(1)}, u32[]{:S(2)}, u32[]{:S(2)}) collective-permute-start(bf16[272,128]{1,0:T(8,128)(2,1)S(1)} %get-tuple-element.22), channel_id=1, source_target_pairs={{0,1},{1,0},{2,3},{3,2},{4,5},{5,4},{6,7},{7,6},{8,9},{9,8},{10,11... | collective-permute-start | bytes 208904 | tf_op jit(solution)/shard_map/ppermute | solution.py:24
  25.7 1.7 %collective-permute-start.9 = (bf16[272,128]{1,0:T(8,128)(2,1)S(1)}, bf16[272,128]{1,0:T(8,128)(2,1)S(1)}, u32[]{:S(2)}, u32[]{:S(2)}) collective-permute-start(bf16[272,128]{1,0:T(8,128)(2,1)S(1)} %get-tuple-element.23), channel_id=1, source_target_pairs={{0,2},{1,3},{2,0},{3,1},{4,6},{5,7},{6,4},{7,5},{8,10},{9,11},{10,... | collective-permute-start | bytes 208904 | tf_op jit(solution)/shard_map/ppermute | solution.py:24
  27.4 1.0 %collective-permute-start.10 = (bf16[272,128]{1,0:T(8,128)(2,1)S(1)}, bf16[272,128]{1,0:T(8,128)(2,1)S(1)}, u32[]{:S(2)}, u32[]{:S(2)}) collective-permute-start(bf16[272,128]{1,0:T(8,128)(2,1)S(1)} %get-tuple-element.24), channel_id=1, source_target_pairs={{0,3},{1,2},{2,1},{3,0},{4,7},{5,6},{6,5},{7,4},{8,11},{9,10},{10,... | collective-permute-start | bytes 208904 | tf_op jit(solution)/shard_map/ppermute | solution.py:24
  28.3 2.1 %left_of_slab.1.refs_8_ = bf16[640,2048]{1,0:T(8,128)(2,1)S(1)} custom-call(s32[5]{0:T(128)S(1)} %copy-done.1, s32[1]{0:T(128)} %bitcast.where_ref, bf16[64,2048]{1,0:T(8,128)(2,1)S(1)} %collective-permute-done.2.early_ref.refs_2_, bf16[5,128,8192]{2,1,0:T(8,128)(2,1)} %left_ref.1), custom_call_target="tpu_custom_call" | custom-call | flops 1 | bytes 1 | tf_op jit(solution)/shard_map/left_of_slab/pallas_call | solution.py:184
  30.5 1.2 %collective-permute-done.8.refs_5_ = bf16[272,128]{1,0:T(8,128)(2,1)S(1)} collective-permute-done((bf16[272,128]{1,0:T(8,128)(2,1)S(1)}, bf16[272,128]{1,0:T(8,128)(2,1)S(1)}, u32[]{:S(2)}, u32[]{:S(2)}) %collective-permute-start.8) | collective-permute-done | bytes 69664 | tf_op jit(solution)/shard_map/ppermute | solution.py:24
  31.7 2.4 %collective-permute-done.10.refs_7_ = bf16[272,128]{1,0:T(8,128)(2,1)S(1)} collective-permute-done((bf16[272,128]{1,0:T(8,128)(2,1)S(1)}, bf16[272,128]{1,0:T(8,128)(2,1)S(1)}, u32[]{:S(2)}, u32[]{:S(2)}) %collective-permute-start.10) | collective-permute-done | bytes 69664 | tf_op jit(solution)/shard_map/ppermute | solution.py:24
  34.0 9.3 %slab_basis.1 = f32[256,2048]{1,0:T(8,128)} custom-call(s32[1]{0:T(128)} %bitcast.where_ref, bf16[64,2048]{1,0:T(8,128)(2,1)S(1)} %get-tuple-element.27.refs_0_, bf16[64,2048]{1,0:T(8,128)(2,1)S(1)} %collective-permute-done.1.refs_1_, bf16[64,2048]{1,0:T(8,128)(2,1)S(1)} %collective-permute-done.2.early_ref.refs_2_, ...), custom_call_target="tpu_custom_call" | custom-call | tf_op jit(solution)/shard_map/slab_basis/pallas_call | solution.py:573
  (11 shorter events, 0.0 us)
Async XLA Ops:
  0.0 23.0 %copy-start.1 = (s32[5]{0:T(128)S(1)}, s32[5]{0:T(128)}, u32[]{:S(2)}) copy-start(s32[5]{0:T(128)} %ranks_ref.3) | copy-start | bytes 64
  1.0 26.4 %collective-permute-start.2 = (bf16[64,2048]{1,0:T(8,128)(2,1)S(1)}, bf16[64,2048]{1,0:T(8,128)(2,1)S(1)}, u32[]{:S(2)}, u32[]{:S(2)}) collective-permute-start(bf16[64,2048]{1,0:T(8,128)(2,1)S(1)} %constant_dynamic-slice_fusion.3), channel_id=1, source_target_pairs={{0,2},{1,3},{2,0},{3,1},{4,6},{5,7},{6,4},{7,5},{8,10},{9,11},{10,... | collective-permute-start | bytes 786440 | tf_op jit(solution)/shard_map/ppermute | solution.py:24
  5.1 1.3 %collective-permute-start = (s32[5]{0:T(128)}, s32[5]{0:T(128)S(1)}, u32[]{:S(2)}, u32[]{:S(2)}) collective-permute-start(s32[5]{0:T(128)} %ranks_ref.3), channel_id=1, source_target_pairs={{0,4},{4,0},{8,12},{12,8},{16,20},{20,16},{24,28},{28,24},{1,5},{5... | collective-permute-start | bytes 68 | tf_op jit(solution)/shard_map/ppermute | solution.py:24
  6.3 1.2 %copy-start = (bf16[64,8192]{1,0:T(8,128)(2,1)S(1)}, bf16[64,8192]{1,0:T(8,128)(2,1)}, u32[]{:S(2)}) copy-start(bf16[64,8192]{1,0:T(8,128)(2,1)} %probes_ref.1) | copy-start | bytes 3145732
  7.6 5.8 %copy-start.2 = (bf16[64,8192]{1,0:T(8,128)(2,1)S(1)}, bf16[64,8192]{1,0:T(8,128)(2,1)}, u32[]{:S(2)}) copy-start(bf16[64,8192]{1,0:T(8,128)(2,1)} %param.5) | copy-start | bytes 3145732
  13.0 2.1 %collective-permute-start.4 = (f32[3,64,128]{2,1,0:T(8,128)S(1)}, f32[3,64,128]{2,1,0:T(8,128)S(1)}, u32[]{:S(2)}, u32[]{:S(2)}) collective-permute-start(f32[3,64,128]{2,1,0:T(8,128)S(1)} %get-tuple-element.18), channel_id=1, source_target_pairs={{0,4},{4,0},{8,12},{12,8},{16,20},{20,16},{24,28},{28,24},{1,5},{5... | collective-permute-start | bytes 294920 | tf_op jit(solution)/shard_map/ppermute | solution.py:24
  13.4 20.6 %collective-permute-start.3 = (bf16[64,2048]{1,0:T(8,128)(2,1)S(1)}, bf16[64,2048]{1,0:T(8,128)(2,1)S(1)}, u32[]{:S(2)}, u32[]{:S(2)}) collective-permute-start(bf16[64,2048]{1,0:T(8,128)(2,1)S(1)} %get-tuple-element.25), channel_id=1, source_target_pairs={{0,3},{1,2},{2,1},{3,0},{4,7},{5,6},{6,5},{7,4},{8,11},{9,10},{10,... | collective-permute-start | bytes 786440 | tf_op jit(solution)/shard_map/ppermute | solution.py:24
  14.8 19.2 %collective-permute-start.1 = (bf16[64,2048]{1,0:T(8,128)(2,1)S(1)}, bf16[64,2048]{1,0:T(8,128)(2,1)S(1)}, u32[]{:S(2)}, u32[]{:S(2)}) collective-permute-start(bf16[64,2048]{1,0:T(8,128)(2,1)S(1)} %get-tuple-element.26), channel_id=1, source_target_pairs={{0,1},{1,0},{2,3},{3,2},{4,5},{5,4},{6,7},{7,6},{8,9},{9,8},{10,11... | collective-permute-start | bytes 786440 | tf_op jit(solution)/shard_map/ppermute | solution.py:24
  15.1 4.0 %collective-permute-start.7 = (f32[64,128]{1,0:T(8,128)S(1)}, f32[64,128]{1,0:T(8,128)S(1)}, u32[]{:S(2)}, u32[]{:S(2)}) collective-permute-start(f32[64,128]{1,0:T(8,128)S(1)} %get-tuple-element.28), channel_id=1, source_target_pairs={{0,8},{4,12},{8,0},{12,4},{16,24},{20,28},{24,16},{28,20},{1,9},{5... | collective-permute-start | bytes 98312 | tf_op jit(solution)/shard_map/ppermute | solution.py:24
  16.7 4.8 %collective-permute-start.6 = (f32[64,128]{1,0:T(8,128)S(1)}, f32[64,128]{1,0:T(8,128)S(1)}, u32[]{:S(2)}, u32[]{:S(2)}) collective-permute-start(f32[64,128]{1,0:T(8,128)S(1)} %get-tuple-element.29), channel_id=1, source_target_pairs={{0,24},{4,28},{8,16},{12,20},{16,8},{20,12},{24,0},{28,4},{1,25},{... | collective-permute-start | bytes 98312 | tf_op jit(solution)/shard_map/ppermute | solution.py:24
  19.1 3.9 %collective-permute-start.5 = (f32[64,128]{1,0:T(8,128)S(1)}, f32[64,128]{1,0:T(8,128)S(1)}, u32[]{:S(2)}, u32[]{:S(2)}) collective-permute-start(f32[64,128]{1,0:T(8,128)S(1)} %get-tuple-element.29), channel_id=1, source_target_pairs={{0,16},{4,20},{8,24},{12,28},{16,0},{20,4},{24,8},{28,12},{1,17},{... | collective-permute-start | bytes 98312 | tf_op jit(solution)/shard_map/ppermute | solution.py:24
  23.9 7.8 %collective-permute-start.8 = (bf16[272,128]{1,0:T(8,128)(2,1)S(1)}, bf16[272,128]{1,0:T(8,128)(2,1)S(1)}, u32[]{:S(2)}, u32[]{:S(2)}) collective-permute-start(bf16[272,128]{1,0:T(8,128)(2,1)S(1)} %get-tuple-element.22), channel_id=1, source_target_pairs={{0,1},{1,0},{2,3},{3,2},{4,5},{5,4},{6,7},{7,6},{8,9},{9,8},{10,11... | collective-permute-start | bytes 208904 | tf_op jit(solution)/shard_map/ppermute | solution.py:24
  25.7 6.0 %collective-permute-start.9 = (bf16[272,128]{1,0:T(8,128)(2,1)S(1)}, bf16[272,128]{1,0:T(8,128)(2,1)S(1)}, u32[]{:S(2)}, u32[]{:S(2)}) collective-permute-start(bf16[272,128]{1,0:T(8,128)(2,1)S(1)} %get-tuple-element.23), channel_id=1, source_target_pairs={{0,2},{1,3},{2,0},{3,1},{4,6},{5,7},{6,4},{7,5},{8,10},{9,11},{10,... | collective-permute-start | bytes 208904 | tf_op jit(solution)/shard_map/ppermute | solution.py:24
  27.4 6.7 %collective-permute-start.10 = (bf16[272,128]{1,0:T(8,128)(2,1)S(1)}, bf16[272,128]{1,0:T(8,128)(2,1)S(1)}, u32[]{:S(2)}, u32[]{:S(2)}) collective-permute-start(bf16[272,128]{1,0:T(8,128)(2,1)S(1)} %get-tuple-element.24), channel_id=1, source_target_pairs={{0,3},{1,2},{2,1},{3,0},{4,7},{5,6},{6,5},{7,4},{8,11},{9,10},{10,... | collective-permute-start | bytes 208904 | tf_op jit(solution)/shard_map/ppermute | solution.py:24

commit v9 on v8

--- a/solution.py
+++ b/solution.py
@@ -37,7 +37,7 @@
 
 
 def chunks_of(slab_rows):
-    return max(1, slab_rows // 512)
+    return max(1, slab_rows // 1024)
 
 
 RANK_STEP = 32
@@ -503,19 +503,23 @@
             rest = factor - high.astype(jnp.float32)
             middle = rest.astype(jnp.bfloat16)
             low = (rest - middle.astype(jnp.float32)).astype(jnp.bfloat16)
-            terms = jnp.dot(
-                jnp.concatenate([high, middle, low], 0), sample, preferred_element_type=jnp.float32
-            )
-            columns = slice(which * piece_rows, (which + 1) * piece_rows)
-            buffer_ref[at, columns] = terms[:height] + (
-                terms[height : 2 * height] + terms[2 * height :]
-            )
-            copies.append(
-                pltpu.make_async_copy(
-                    buffer_ref.at[at, columns], out_ref.at[at, columns], sems.at[len(copies)]
+            factors_of = jnp.concatenate([high, middle, low], 0)
+            steps = 2 if k == count - 1 else 1
+            width = piece_rows // steps
+            for step in range(steps):
+                within = slice(step * width, (step + 1) * width)
+                terms = jnp.dot(factors_of, sample[:, within], preferred_element_type=jnp.float32)
+                begin = which * piece_rows + step * width
+                columns = slice(begin, begin + width)
+                buffer_ref[at, columns] = terms[:height] + (
+                    terms[height : 2 * height] + terms[2 * height :]
                 )
-            )
-            copies[-1].start()
+                copies.append(
+                    pltpu.make_async_copy(
+                        buffer_ref.at[at, columns], out_ref.at[at, columns], sems.at[len(copies)]
+                    )
+                )
+                copies[-1].start()
         held.clear()
 
     inverse_factors(grams, take_rows)
@@ -578,7 +582,7 @@
         scratch_shapes=[
             pltpu.VMEM((all_probes, slab_rows), jnp.bfloat16),
             pltpu.VMEM((all_probes, slab_rows), jnp.float32),
-            pltpu.SemaphoreType.DMA((all_probes // HALF,)),
+            pltpu.SemaphoreType.DMA((2 * all_probes // HALF,)),
         ]
         + [pltpu.VMEM((all_probes, ranks), jnp.bfloat16)],
         compiler_params=pltpu.CompilerParams(vmem_limit_bytes=VMEM_LIMIT),
@@ -612,7 +616,7 @@
         out_shape=jax.ShapeDtypeStruct((all_probes, slab_rows), jnp.float32),
         scratch_shapes=[
             pltpu.VMEM((all_probes, slab_rows), jnp.float32),
-            pltpu.SemaphoreType.DMA((all_probes // HALF,)),
+            pltpu.SemaphoreType.DMA((2 * all_probes // HALF,)),
         ],
         compiler_params=pltpu.CompilerParams(vmem_limit_bytes=VMEM_LIMIT),
         name="basis",

time: 43.8 us -> 43.2 us (0.986)
  Pallas kernels: 17.8 us -> 16.8 us
  waiting for transfers between devices: 7.93 us -> 8.39 us
    pallas_call x1, Pallas kernels: 5.45 us -> 4.69 us  [couplings(): pl.pallas_call(functools.partial(coupling_kernel, tuple(parts), joined, 3...]
    ppermute x11, waiting for transfers between devices: 7.93 us -> 8.39 us  [xor_permute(): return lax.ppermute(value, axis, pairs)]
  transfers between devices with their start and end apart: 11 -> 11, of which waited for: 6 -> 6; matrix products, arithmetic and copies ran while one was open for 0% -> 0% of each run, Pallas kernels for 20% -> 17%
where the time goes in v9:
time: 43.2 us; the launch traced here: 42.8 us
  Pallas kernels  16.8 us (39%)
  starting transfers between devices  15.3 us (35%)
  waiting for transfers between devices  8.39 us (19%)
  local copies, waits for them, and re-layouts  2.28 us (5%)
    ppermute x11, starting transfers between devices, xor_permute(): return lax.ppermute(value, axis, pairs)  15.3 us
    pallas_call x1, Pallas kernels, slab_basis(): pl.pallas_call(functools.partial(slab_kernel, masks, count, ridge_share *...  9.32 us
    ppermute x11, waiting for transfers between devices, xor_permute(): return lax.ppermute(value, axis, pairs)  8.39 us
    pallas_call x1, Pallas kernels, couplings(): pl.pallas_call(functools.partial(coupling_kernel, tuple(parts), joined, 3...  4.69 us
    pallas_call x1, Pallas kernels, left_of_slab(): pl.pallas_call(left_kernel, in_specs=[smem(), smem(), hbm(), hbm()], out_...  1.95 us
    unnamed x6, local copies, waits for them, and re-layouts  1.23 us
    dynamic_slice x2, local copies, waits for them, and re-layouts, piece_for(): lax.dynamic_slice_in_dim(values, (place ^ mask) * slab_rows, slab_rows, 1)  1.05 us
  transfers between devices with their start and end apart: 11, of which 6 were waited for; matrix products, arithmetic and copies ran while one was open for 0% of the time, Pallas kernels for 17%

profile of v9, /device:TPU:0, one launch (start us, length us, event | category | flops | bytes accessed | tf_op | source)
XLA Modules:
  0.0 42.8 jit_solution(7244489894833297701)
XLA Ops:
  0.0 1.0 %constant_dynamic-slice_fusion.3 = bf16[64,2048]{1,0:T(8,128)(2,1)S(1)} fusion(bf16[64,8192]{1,0:T(8,128)(2,1)} %param.5, s32[]{:T(128)S(6)} %select_n.12), kind=kLoop, calls=%fused_computation.7 | loop fusion | bytes 524292 | tf_op jit(solution)/shard_map/dynamic_slice | solution.py:638
  1.0 4.1 %collective-permute-start.2 = (bf16[64,2048]{1,0:T(8,128)(2,1)S(1)}, bf16[64,2048]{1,0:T(8,128)(2,1)S(1)}, u32[]{:S(2)}, u32[]{:S(2)}) collective-permute-start(bf16[64,2048]{1,0:T(8,128)(2,1)S(1)} %constant_dynamic-slice_fusion.3), channel_id=1, source_target_pairs={{0,2},{1,3},{2,0},{3,1},{4,6},{5,7},{6,4},{7,5},{8,10},{9,11},{10,... | collective-permute-start | bytes 786440 | tf_op jit(solution)/shard_map/ppermute | solution.py:24
  5.1 1.3 %collective-permute-done.ranks_ref = s32[5]{0:T(128)S(1)} collective-permute-done((s32[5]{0:T(128)}, s32[5]{0:T(128)S(1)}, u32[]{:S(2)}, u32[]{:S(2)}) %collective-permute-start) | collective-permute-done | bytes 52 | tf_op jit(solution)/shard_map/ppermute | solution.py:24
  6.3 1.2 %copy-done = bf16[64,8192]{1,0:T(8,128)(2,1)S(1)} copy-done((bf16[64,8192]{1,0:T(8,128)(2,1)S(1)}, bf16[64,8192]{1,0:T(8,128)(2,1)}, u32[]{:S(2)}) %copy-start) | copy-done | bytes 1048600
  7.6 4.7 %couplings.1 = (f32[3,64,128]{2,1,0:T(8,128)S(1)}, bf16[2,64,128]{2,1,0:T(8,128)(2,1)S(1)}, bf16[4,64,128]{2,1,0:T(8,128)(2,1)S(1)}) custom-call(s32[5]{0:T(128)S(1)} %collective-permute-done.ranks_ref, bf16[64,8192]{1,0:T(8,128)(2,1)S(1)} %copy-done, bf16[5,128,8192]{2,1,0:T(8,128)(2,1)} %right_ref.1), custom_call_target="tpu_custom_call" | custom-call | flops 1 | bytes 1 | tf_op jit(solution)/shard_map/couplings/pallas_call | solution.py:140
  12.3 0.3 collective-permute-start.4
  12.6 0.1 constant_dynamic-slice_fusion
  12.6 1.4 %collective-permute-start.3 = (bf16[64,2048]{1,0:T(8,128)(2,1)S(1)}, bf16[64,2048]{1,0:T(8,128)(2,1)S(1)}, u32[]{:S(2)}, u32[]{:S(2)}) collective-permute-start(bf16[64,2048]{1,0:T(8,128)(2,1)S(1)} %get-tuple-element.25), channel_id=1, source_target_pairs={{0,3},{1,2},{2,1},{3,0},{4,7},{5,6},{6,5},{7,4},{8,11},{9,10},{10,... | collective-permute-start | bytes 786440 | tf_op jit(solution)/shard_map/ppermute | solution.py:24
  14.0 0.3 collective-permute-start.1
  14.4 1.6 %collective-permute-start.7 = (f32[64,128]{1,0:T(8,128)S(1)}, f32[64,128]{1,0:T(8,128)S(1)}, u32[]{:S(2)}, u32[]{:S(2)}) collective-permute-start(f32[64,128]{1,0:T(8,128)S(1)} %get-tuple-element.28), channel_id=1, source_target_pairs={{0,8},{4,12},{8,0},{12,4},{16,24},{20,28},{24,16},{28,20},{1,9},{5... | collective-permute-start | bytes 98312 | tf_op jit(solution)/shard_map/ppermute | solution.py:24
  15.9 1.5 %collective-permute-start.6 = (f32[64,128]{1,0:T(8,128)S(1)}, f32[64,128]{1,0:T(8,128)S(1)}, u32[]{:S(2)}, u32[]{:S(2)}) collective-permute-start(f32[64,128]{1,0:T(8,128)S(1)} %get-tuple-element.29), channel_id=1, source_target_pairs={{0,24},{4,28},{8,16},{12,20},{16,8},{20,12},{24,0},{28,4},{1,25},{... | collective-permute-start | bytes 98312 | tf_op jit(solution)/shard_map/ppermute | solution.py:24
  17.4 0.9 %collective-permute-done.7.refs_2_ = f32[64,128]{1,0:T(8,128)S(1)} collective-permute-done((f32[64,128]{1,0:T(8,128)S(1)}, f32[64,128]{1,0:T(8,128)S(1)}, u32[]{:S(2)}, u32[]{:S(2)}) %collective-permute-start.7) | collective-permute-done | bytes 32800 | tf_op jit(solution)/shard_map/ppermute | solution.py:24
  18.4 1.7 %collective-permute-start.5 = (f32[64,128]{1,0:T(8,128)S(1)}, f32[64,128]{1,0:T(8,128)S(1)}, u32[]{:S(2)}, u32[]{:S(2)}) collective-permute-start(f32[64,128]{1,0:T(8,128)S(1)} %get-tuple-element.29), channel_id=1, source_target_pairs={{0,16},{4,20},{8,24},{12,28},{16,0},{20,4},{24,8},{28,12},{1,17},{... | collective-permute-start | bytes 98312 | tf_op jit(solution)/shard_map/ppermute | solution.py:24
  20.0 0.7 %collective-permute-done.6.refs_1_ = f32[64,128]{1,0:T(8,128)S(1)} collective-permute-done((f32[64,128]{1,0:T(8,128)S(1)}, f32[64,128]{1,0:T(8,128)S(1)}, u32[]{:S(2)}, u32[]{:S(2)}) %collective-permute-start.6) | collective-permute-done | bytes 32800 | tf_op jit(solution)/shard_map/ppermute | solution.py:24
  20.8 1.5 %collective-permute-done.5.refs_0_ = f32[64,128]{1,0:T(8,128)S(1)} collective-permute-done((f32[64,128]{1,0:T(8,128)S(1)}, f32[64,128]{1,0:T(8,128)S(1)}, u32[]{:S(2)}, u32[]{:S(2)}) %collective-permute-start.5) | collective-permute-done | bytes 32800 | tf_op jit(solution)/shard_map/ppermute | solution.py:24
  22.3 0.8 %payloads.1 = (bf16[272,128]{1,0:T(8,128)(2,1)S(1)}, bf16[272,128]{1,0:T(8,128)(2,1)S(1)}, bf16[272,128]{1,0:T(8,128)(2,1)S(1)}, bf16[272,128]{1,0:T(8,128)(2,1)S(1)}) custom-call(s32[5]{0:T(128)S(1)} %copy-done.1, s32[1]{0:T(128)} %bitcast.where_ref, f32[3,64,128]{2,1,0:T(8,128)S(1)} %collective-permute-done.4.near_ref, ...), custom_call_target="tpu_custom_call" | custom-call | flops 1 | bytes 1 | tf_op jit(solution)/shard_map/payloads/pallas_call | solution.py:267
  23.1 1.8 %collective-permute-start.8 = (bf16[272,128]{1,0:T(8,128)(2,1)S(1)}, bf16[272,128]{1,0:T(8,128)(2,1)S(1)}, u32[]{:S(2)}, u32[]{:S(2)}) collective-permute-start(bf16[272,128]{1,0:T(8,128)(2,1)S(1)} %get-tuple-element.22), channel_id=1, source_target_pairs={{0,1},{1,0},{2,3},{3,2},{4,5},{5,4},{6,7},{7,6},{8,9},{9,8},{10,11... | collective-permute-start | bytes 208904 | tf_op jit(solution)/shard_map/ppermute | solution.py:24
  24.9 1.7 %collective-permute-start.9 = (bf16[272,128]{1,0:T(8,128)(2,1)S(1)}, bf16[272,128]{1,0:T(8,128)(2,1)S(1)}, u32[]{:S(2)}, u32[]{:S(2)}) collective-permute-start(bf16[272,128]{1,0:T(8,128)(2,1)S(1)} %get-tuple-element.23), channel_id=1, source_target_pairs={{0,2},{1,3},{2,0},{3,1},{4,6},{5,7},{6,4},{7,5},{8,10},{9,11},{10,... | collective-permute-start | bytes 208904 | tf_op jit(solution)/shard_map/ppermute | solution.py:24
  26.6 0.0 collective-permute-done.2.early_ref.refs_2_
  26.6 1.0 %collective-permute-start.10 = (bf16[272,128]{1,0:T(8,128)(2,1)S(1)}, bf16[272,128]{1,0:T(8,128)(2,1)S(1)}, u32[]{:S(2)}, u32[]{:S(2)}) collective-permute-start(bf16[272,128]{1,0:T(8,128)(2,1)S(1)} %get-tuple-element.24), channel_id=1, source_target_pairs={{0,3},{1,2},{2,1},{3,0},{4,7},{5,6},{6,5},{7,4},{8,11},{9,10},{10,... | collective-permute-start | bytes 208904 | tf_op jit(solution)/shard_map/ppermute | solution.py:24
  27.6 1.9 %left_of_slab.1.refs_8_ = bf16[640,2048]{1,0:T(8,128)(2,1)S(1)} custom-call(s32[5]{0:T(128)S(1)} %copy-done.1, s32[1]{0:T(128)} %bitcast.where_ref, bf16[64,2048]{1,0:T(8,128)(2,1)S(1)} %collective-permute-done.2.early_ref.refs_2_, bf16[5,128,8192]{2,1,0:T(8,128)(2,1)} %left_ref.1), custom_call_target="tpu_custom_call" | custom-call | flops 1 | bytes 1 | tf_op jit(solution)/shard_map/left_of_slab/pallas_call | solution.py:184
  29.5 1.5 %collective-permute-done.8.refs_5_ = bf16[272,128]{1,0:T(8,128)(2,1)S(1)} collective-permute-done((bf16[272,128]{1,0:T(8,128)(2,1)S(1)}, bf16[272,128]{1,0:T(8,128)(2,1)S(1)}, u32[]{:S(2)}, u32[]{:S(2)}) %collective-permute-start.8) | collective-permute-done | bytes 69664 | tf_op jit(solution)/shard_map/ppermute | solution.py:24
  31.0 2.5 %collective-permute-done.9.refs_6_ = bf16[272,128]{1,0:T(8,128)(2,1)S(1)} collective-permute-done((bf16[272,128]{1,0:T(8,128)(2,1)S(1)}, bf16[272,128]{1,0:T(8,128)(2,1)S(1)}, u32[]{:S(2)}, u32[]{:S(2)}) %collective-permute-start.9) | collective-permute-done | bytes 69664 | tf_op jit(solution)/shard_map/ppermute | solution.py:24
  33.5 9.3 %slab_basis.1 = f32[256,2048]{1,0:T(8,128)} custom-call(s32[1]{0:T(128)} %bitcast.where_ref, bf16[64,2048]{1,0:T(8,128)(2,1)S(1)} %get-tuple-element.27.refs_0_, bf16[64,2048]{1,0:T(8,128)(2,1)S(1)} %collective-permute-done.1.refs_1_, bf16[64,2048]{1,0:T(8,128)(2,1)S(1)} %collective-permute-done.2.early_ref.refs_2_, ...), custom_call_target="tpu_custom_call" | custom-call | tf_op jit(solution)/shard_map/slab_basis/pallas_call | solution.py:577
  (11 shorter events, 0.0 us)
Async XLA Ops:
  0.0 22.3 %copy-start.1 = (s32[5]{0:T(128)S(1)}, s32[5]{0:T(128)}, u32[]{:S(2)}) copy-start(s32[5]{0:T(128)} %ranks_ref.3) | copy-start | bytes 64
  1.0 25.6 %collective-permute-start.2 = (bf16[64,2048]{1,0:T(8,128)(2,1)S(1)}, bf16[64,2048]{1,0:T(8,128)(2,1)S(1)}, u32[]{:S(2)}, u32[]{:S(2)}) collective-permute-start(bf16[64,2048]{1,0:T(8,128)(2,1)S(1)} %constant_dynamic-slice_fusion.3), channel_id=1, source_target_pairs={{0,2},{1,3},{2,0},{3,1},{4,6},{5,7},{6,4},{7,5},{8,10},{9,11},{10,... | collective-permute-start | bytes 786440 | tf_op jit(solution)/shard_map/ppermute | solution.py:24
  5.1 1.3 %collective-permute-start = (s32[5]{0:T(128)}, s32[5]{0:T(128)S(1)}, u32[]{:S(2)}, u32[]{:S(2)}) collective-permute-start(s32[5]{0:T(128)} %ranks_ref.3), channel_id=1, source_target_pairs={{0,4},{4,0},{8,12},{12,8},{16,20},{20,16},{24,28},{28,24},{1,5},{5... | collective-permute-start | bytes 68 | tf_op jit(solution)/shard_map/ppermute | solution.py:24
  6.3 1.2 %copy-start = (bf16[64,8192]{1,0:T(8,128)(2,1)S(1)}, bf16[64,8192]{1,0:T(8,128)(2,1)}, u32[]{:S(2)}) copy-start(bf16[64,8192]{1,0:T(8,128)(2,1)} %probes_ref.1) | copy-start | bytes 3145732
  7.6 5.0 %copy-start.2 = (bf16[64,8192]{1,0:T(8,128)(2,1)S(1)}, bf16[64,8192]{1,0:T(8,128)(2,1)}, u32[]{:S(2)}) copy-start(bf16[64,8192]{1,0:T(8,128)(2,1)} %param.5) | copy-start | bytes 3145732
  12.3 2.1 %collective-permute-start.4 = (f32[3,64,128]{2,1,0:T(8,128)S(1)}, f32[3,64,128]{2,1,0:T(8,128)S(1)}, u32[]{:S(2)}, u32[]{:S(2)}) collective-permute-start(f32[3,64,128]{2,1,0:T(8,128)S(1)} %get-tuple-element.18), channel_id=1, source_target_pairs={{0,4},{4,0},{8,12},{12,8},{16,20},{20,16},{24,28},{28,24},{1,5},{5... | collective-permute-start | bytes 294920 | tf_op jit(solution)/shard_map/ppermute | solution.py:24
  12.6 20.8 %collective-permute-start.3 = (bf16[64,2048]{1,0:T(8,128)(2,1)S(1)}, bf16[64,2048]{1,0:T(8,128)(2,1)S(1)}, u32[]{:S(2)}, u32[]{:S(2)}) collective-permute-start(bf16[64,2048]{1,0:T(8,128)(2,1)S(1)} %get-tuple-element.25), channel_id=1, source_target_pairs={{0,3},{1,2},{2,1},{3,0},{4,7},{5,6},{6,5},{7,4},{8,11},{9,10},{10,... | collective-permute-start | bytes 786440 | tf_op jit(solution)/shard_map/ppermute | solution.py:24
  14.0 19.4 %collective-permute-start.1 = (bf16[64,2048]{1,0:T(8,128)(2,1)S(1)}, bf16[64,2048]{1,0:T(8,128)(2,1)S(1)}, u32[]{:S(2)}, u32[]{:S(2)}) collective-permute-start(bf16[64,2048]{1,0:T(8,128)(2,1)S(1)} %get-tuple-element.26), channel_id=1, source_target_pairs={{0,1},{1,0},{2,3},{3,2},{4,5},{5,4},{6,7},{7,6},{8,9},{9,8},{10,11... | collective-permute-start | bytes 786440 | tf_op jit(solution)/shard_map/ppermute | solution.py:24
  14.4 4.0 %collective-permute-start.7 = (f32[64,128]{1,0:T(8,128)S(1)}, f32[64,128]{1,0:T(8,128)S(1)}, u32[]{:S(2)}, u32[]{:S(2)}) collective-permute-start(f32[64,128]{1,0:T(8,128)S(1)} %get-tuple-element.28), channel_id=1, source_target_pairs={{0,8},{4,12},{8,0},{12,4},{16,24},{20,28},{24,16},{28,20},{1,9},{5... | collective-permute-start | bytes 98312 | tf_op jit(solution)/shard_map/ppermute | solution.py:24
  15.9 4.8 %collective-permute-start.6 = (f32[64,128]{1,0:T(8,128)S(1)}, f32[64,128]{1,0:T(8,128)S(1)}, u32[]{:S(2)}, u32[]{:S(2)}) collective-permute-start(f32[64,128]{1,0:T(8,128)S(1)} %get-tuple-element.29), channel_id=1, source_target_pairs={{0,24},{4,28},{8,16},{12,20},{16,8},{20,12},{24,0},{28,4},{1,25},{... | collective-permute-start | bytes 98312 | tf_op jit(solution)/shard_map/ppermute | solution.py:24
  18.4 3.9 %collective-permute-start.5 = (f32[64,128]{1,0:T(8,128)S(1)}, f32[64,128]{1,0:T(8,128)S(1)}, u32[]{:S(2)}, u32[]{:S(2)}) collective-permute-start(f32[64,128]{1,0:T(8,128)S(1)} %get-tuple-element.29), channel_id=1, source_target_pairs={{0,16},{4,20},{8,24},{12,28},{16,0},{20,4},{24,8},{28,12},{1,17},{... | collective-permute-start | bytes 98312 | tf_op jit(solution)/shard_map/ppermute | solution.py:24
  23.1 7.9 %collective-permute-start.8 = (bf16[272,128]{1,0:T(8,128)(2,1)S(1)}, bf16[272,128]{1,0:T(8,128)(2,1)S(1)}, u32[]{:S(2)}, u32[]{:S(2)}) collective-permute-start(bf16[272,128]{1,0:T(8,128)(2,1)S(1)} %get-tuple-element.22), channel_id=1, source_target_pairs={{0,1},{1,0},{2,3},{3,2},{4,5},{5,4},{6,7},{7,6},{8,9},{9,8},{10,11... | collective-permute-start | bytes 208904 | tf_op jit(solution)/shard_map/ppermute | solution.py:24
  24.9 8.6 %collective-permute-start.9 = (bf16[272,128]{1,0:T(8,128)(2,1)S(1)}, bf16[272,128]{1,0:T(8,128)(2,1)S(1)}, u32[]{:S(2)}, u32[]{:S(2)}) collective-permute-start(bf16[272,128]{1,0:T(8,128)(2,1)S(1)} %get-tuple-element.23), channel_id=1, source_target_pairs={{0,2},{1,3},{2,0},{3,1},{4,6},{5,7},{6,4},{7,5},{8,10},{9,11},{10,... | collective-permute-start | bytes 208904 | tf_op jit(solution)/shard_map/ppermute | solution.py:24
  26.6 6.9 %collective-permute-start.10 = (bf16[272,128]{1,0:T(8,128)(2,1)S(1)}, bf16[272,128]{1,0:T(8,128)(2,1)S(1)}, u32[]{:S(2)}, u32[]{:S(2)}) collective-permute-start(bf16[272,128]{1,0:T(8,128)(2,1)S(1)} %get-tuple-element.24), channel_id=1, source_target_pairs={{0,3},{1,2},{2,1},{3,0},{4,7},{5,6},{6,5},{7,4},{8,11},{9,10},{10,... | collective-permute-start | bytes 208904 | tf_op jit(solution)/shard_map/ppermute | solution.py:24
